TPU v7x, 128 devices: a whole 4x4x4 slice. The times are simulated.
128 devices in a mesh: tm: 2 (over core), tile: 64 (over z, y, x).
Axes of the slice: x: 4, y: 4, z: 4, core: 2. Of those that a mesh axis runs over, the one named last changes fastest.
Arguments:
- features: bfloat16 [1, 8, 256, 64, 192], P(None, 'tm', 'tile'), may hold values from -60 to 60
- gain_one: float32 [192], replicated, may hold values from 0.5 to 1.5
- shift_one: float32 [192], replicated, may hold values from -3 to 3
- kernel_one: bfloat16 [3, 3, 3, 192, 192], replicated, may hold values from -0.078125 to 0.078125
- bias_one: float32 [192], replicated, may hold values from -3 to 3
- gain_two: float32 [192], replicated, may hold values from 0.5 to 1.5
- shift_two: float32 [192], replicated, may hold values from -3 to 3
- kernel_two: bfloat16 [3, 3, 3, 192, 192], replicated, may hold values from -0.078125 to 0.078125
- bias_two: float32 [192], replicated, may hold values from -3 to 3
- up_kernel: bfloat16 [3, 3, 192, 96], replicated, may hold values from -0.15625 to 0.15625
- up_bias: float32 [96], replicated, may hold values from -3 to 3
Outputs:
- decoded: bfloat16 [1, 8, 512, 64, 192], P(None, 'tm', 'tile')
All inputs are finite; a program needn't handle non-finite values.
Results may differ from a plain program's by a relative error of at most 0.009.
Values may be sent and summed in bfloat16 or wider, within the bound.
No kernel may reach another device: no remote copies, remote signals or barrier semaphores. Data moves between devices by JAX's collectives and lax.ppermute only.
A program may use at most 128 MiB of HBM per device.

v0:
```python
import jax
import jax.numpy as jnp
from jax import lax
from jax.sharding import PartitionSpec as P

G = 32


epsilon = 1e-06


def extended(block, sides, width):
    for axis, dim in sides:
        count = lax.axis_size(axis)
        forward = [(i, i + 1) for i in range(count - 1)]
        backward = [(target, source) for source, target in forward]
        low = lax.ppermute(
            lax.slice_in_dim(block, block.shape[dim] - width, None, axis=dim), axis, forward
        )
        high = lax.ppermute(lax.slice_in_dim(block, 0, width, axis=dim), axis, backward)
        block = jnp.concatenate([low, block, high], axis=dim)
    return block


def from_behind(value, axis, by):
    count = lax.axis_size(axis)
    pairs = [(i, i + by) for i in range(count) if 0 <= i + by < count]
    return lax.ppermute(value, axis, pairs)


def group_act(values_in, gain_vec, shift_vec, row_total):
    clip_count, frame_count, row_count, col_count, chan_count = values_in.shape
    grouped = values_in.reshape(clip_count, frame_count, row_count, col_count, G, chan_count // G)
    cell_count = row_total * col_count * (chan_count // G)
    centre_value = lax.psum(jnp.sum(grouped, axis=(2, 3, 5)), "tile") / cell_count
    centered = grouped - centre_value[:, :, None, None, :, None]
    spread_value = lax.psum(jnp.sum(centered * centered, axis=(2, 3, 5)), "tile") / cell_count
    scaling = lax.rsqrt(spread_value + epsilon)[:, :, None, None, :, None]
    normed = (centered * scaling).reshape(values_in.shape)
    return jax.nn.silu(normed * gain_vec + shift_vec).astype(jnp.bfloat16)


def add_rows(values_in):
    return extended(values_in, (("tile", 2),), 1)


def causal_taps(padded, kernel, bias_term):
    clip_count, frame_span, row_span, col_count, chan_count = padded.shape
    out_frames = frame_span - 2
    out_rows = row_span - 2
    widened = jnp.pad(padded, ((0, 0), (0, 0), (0, 0), (1, 1), (0, 0)))
    accumulated = jnp.zeros(
        (clip_count * out_frames * out_rows * col_count, kernel.shape[-1]), jnp.float32
    )
    for time_tap in range(3):
        for row_tap in range(3):
            slab_part = widened[:, time_tap : time_tap + out_frames, row_tap : row_tap + out_rows]
            stacked = jnp.concatenate(
                [slab_part[:, :, :, col_tap : col_tap + col_count] for col_tap in range(3)], axis=-1
            )
            accumulated = accumulated + jnp.dot(
                stacked.reshape(-1, 3 * chan_count),
                kernel[time_tap, row_tap].reshape(3 * chan_count, -1),
                preferred_element_type=jnp.float32,
            )
    return accumulated.reshape(clip_count, out_frames, out_rows, col_count, -1) + bias_term


def plane_taps(padded, kernel):
    clip_count, frame_count, row_span, col_span, chan_count = padded.shape
    out_rows = row_span - 2
    out_cols = col_span - 2
    accumulated = jnp.zeros(
        (clip_count * frame_count * out_rows * out_cols, kernel.shape[-1]), jnp.float32
    )
    for row_tap in range(3):
        slab_part = padded[:, :, row_tap : row_tap + out_rows]
        stacked = jnp.concatenate(
            [slab_part[:, :, :, col_tap : col_tap + out_cols] for col_tap in range(3)], axis=-1
        )
        accumulated = accumulated + jnp.dot(
            stacked.reshape(-1, 3 * chan_count),
            kernel[row_tap].reshape(3 * chan_count, -1),
            preferred_element_type=jnp.float32,
        )
    return accumulated.reshape(clip_count, frame_count, out_rows, out_cols, -1)


def body(
    features,
    gain_one,
    shift_one,
    kernel_one,
    bias_one,
    gain_two,
    shift_two,
    kernel_two,
    bias_two,
    up_kernel,
    up_bias,
):
    clip_count = features.shape[0]
    frame_count = features.shape[1]
    row_count = features.shape[2]
    col_count = features.shape[3]
    row_total = row_count * lax.axis_size("tile")
    source = features.astype(jnp.float32)
    first_act = group_act(source, gain_one, shift_one, row_total)
    first_rim = add_rows(first_act)
    first_cache = from_behind(first_rim[:, frame_count - 2 :], "tm", 1)
    hidden = causal_taps(
        jnp.concatenate([first_cache, first_rim], axis=1), kernel_one, bias_one
    ).astype(jnp.bfloat16)
    second = group_act(hidden.astype(jnp.float32), gain_two, shift_two, row_total)
    second_rim = add_rows(second)
    second_cache = from_behind(second_rim[:, frame_count - 2 :], "tm", 1)
    branch_out = causal_taps(
        jnp.concatenate([second_cache, second_rim], axis=1), kernel_two, bias_two
    )
    joined = (source + branch_out).astype(jnp.bfloat16)
    joined_rim = add_rows(joined)
    doubled = jnp.repeat(joined_rim, 2, axis=2)[:, :, 1:-1]
    doubled = jnp.repeat(doubled, 2, axis=3)
    doubled_pad = jnp.pad(doubled, ((0, 0), (0, 0), (0, 0), (1, 1), (0, 0)))
    produced = (plane_taps(doubled_pad, up_kernel) + up_bias).astype(jnp.bfloat16)
    return produced.reshape(clip_count, frame_count, 2 * row_count, col_count, -1)


def solution(mesh):
    return jax.shard_map(
        body,
        mesh=mesh,
        in_specs=(
            P(None, "tm", "tile", None, None),
            P(),
            P(),
            P(),
            P(),
            P(),
            P(),
            P(),
            P(),
            P(),
            P(),
        ),
        out_specs=P(None, "tm", "tile", None, None),
        check_vma=False,
    )
```

profile of v0, /device:TPU:1, one launch (start us, length us, event | category | flops | bytes accessed | tf_op | source)
XLA Modules:
  0.0 895.3 jit_solution(9259740635210660267)
XLA Ops:
  1.4 153.5 %psum.28 = f32[1,4,32]{2,1,0:T(4,128)S(1)} all-reduce(f32[1,4,32]{2,1,0:T(4,128)S(1)} %bitcast.166), channel_id=1, replica_groups=mesh['tm'=2,'tile'=64] {'tile'}, use_global_device_ids=true, to_apply=%region_2.0 | all-reduce | flops 128 | bytes 1024 | tf_op jit(solution)/shard_map/psum | solution.py:35
  156.5 144.3 %psum.29 = f32[1,4,32]{2,1,0:T(4,128)S(1)} all-reduce(f32[1,4,32]{2,1,0:T(4,128)S(1)} %bitcast.165), channel_id=1, replica_groups=mesh['tm'=2,'tile'=64] {'tile'}, use_global_device_ids=true, to_apply=%region_5.6 | all-reduce | flops 128 | bytes 1024 | tf_op jit(solution)/shard_map/psum | solution.py:37
  301.5 3.3 collective-permute-start
  306.8 4.1 collective-permute-done.1
  312.2 1.9 fusion.32
  314.1 56.6 %collective-permute-done.2 = bf16[1,2,6,64,192]{4,3,2,1,0:T(8,128)(2,1)S(1)} collective-permute-done((bf16[1,2,6,64,192]{4,3,2,1,0:T(8,128)(2,1)S(1)}, bf16[1,2,6,64,192]{4,3,2,1,0:T(8,128)(2,1)S(1)}, u32[]{:S(2)}, u32[]{:S(2)}) %collective-permute-start.2) | collective-permute-done | bytes 294944 | tf_op jit(solution)/shard_map/ppermute | solution.py:28
  370.9 2.3 pad_slice_fusion.18
  376.4 2.7 fusion.7
  389.6 144.1 %psum.30 = f32[1,4,32]{2,1,0:T(4,128)S(1)} all-reduce(f32[1,4,32]{2,1,0:T(4,128)S(1)} %bitcast.167), channel_id=1, replica_groups=mesh['tm'=2,'tile'=64] {'tile'}, use_global_device_ids=true, to_apply=%region_7.8 | all-reduce | flops 128 | bytes 1024 | tf_op jit(solution)/shard_map/psum | solution.py:35
  534.9 146.1 %psum.31 = f32[1,4,32]{2,1,0:T(4,128)S(1)} all-reduce(f32[1,4,32]{2,1,0:T(4,128)S(1)} %bitcast.168), channel_id=1, replica_groups=mesh['tm'=2,'tile'=64] {'tile'}, use_global_device_ids=true, to_apply=%region_9.10 | all-reduce | flops 128 | bytes 1024 | tf_op jit(solution)/shard_map/psum | solution.py:37
  686.6 3.8 collective-permute-done.4
  696.7 2.6 multiply_convert_fusion.1
  699.3 52.2 %collective-permute-done.5 = bf16[1,2,6,64,192]{4,3,2,1,0:T(8,128)(2,1)S(1)} collective-permute-done((bf16[1,2,6,64,192]{4,3,2,1,0:T(8,128)(2,1)}, bf16[1,2,6,64,192]{4,3,2,1,0:T(8,128)(2,1)S(1)}, u32[]{:S(2)}, u32[]{:S(2)}) %collective-permute-start.5) | collective-permute-done | bytes 294944 | tf_op jit(solution)/shard_map/ppermute | solution.py:28
  751.7 2.8 pad_slice_fusion
  754.5 3.0 pad_slice_fusion.1
  760.7 1.9 pad_maximum_fusion.14
  784.1 3.8 collective-permute-done.7
  790.6 9.9 %pad_slice_fusion.37 = (bf16[1,4,8,128,192]{4,1,3,2,0:T(4,128)(2,1)S(1)}, bf16[1,4,8,128,192]{4,1,3,2,0:T(4,128)(2,1)S(1)}, bf16[1,4,8,128,192]{4,1,3,2,0:T(4,12...) fusion(bf16[1,4,10,128,192]{4,1,3,2,0:T(4,128)(2,1)S(1)} %bitca, ...), kind=kLoop, calls=%fused_computation.127 | loop fusion | bytes 23068672 | tf_op jit(solution)/shard_map/slice | solution.py:79
  800.4 6.2 pad_maximum_fusion.2
  806.6 10.4 %copy.52 = bf16[1,4,8,128,576]{3,2,1,4,0:T(8,128)(2,1)} copy(bf16[1,4,8,128,576]{4,1,3,2,0:T(4,128)(2,1)} %pad_maximum_fusion.2) | data formatting | bytes 9437184 | tf_op jit(solution)/shard_map/concatenate | solution.py:78
  817.0 8.2 reshape.305
  825.2 8.6 pad_maximum_fusion.1
  833.8 10.5 %copy.51 = bf16[1,4,8,128,576]{3,2,1,4,0:T(8,128)(2,1)} copy(bf16[1,4,8,128,576]{4,1,3,2,0:T(4,128)(2,1)} %pad_maximum_fusion.1) | data formatting | bytes 9437184 | tf_op jit(solution)/shard_map/concatenate | solution.py:78
  844.2 8.2 reshape.304
  852.4 8.2 pad_maximum_fusion
  860.6 10.4 %copy.50 = bf16[1,4,8,128,576]{3,2,1,4,0:T(8,128)(2,1)} copy(bf16[1,4,8,128,576]{4,1,3,2,0:T(4,128)(2,1)} %pad_maximum_fusion) | data formatting | bytes 9437184 | tf_op jit(solution)/shard_map/concatenate | solution.py:78
  871.0 8.4 reshape.303
  879.4 3.4 fusion.42
  882.9 3.6 convolution_add_fusion.1
  886.6 2.2 convolution_add_fusion
  888.8 1.8 copy.53
  892.2 2.8 add_convert_fusion
  (182 shorter events, 62.5 us)
Async XLA Ops:
  0.0 301.1 %copy-start = (bf16[1,4,4,64,192]{4,3,2,1,0:T(8,128)(2,1)S(1)}, bf16[1,4,4,64,192]{4,3,2,1,0:T(8,128)(2,1)}, u32[]{:S(2)}) copy-start(bf16[1,4,4,64,192]{4,3,2,1,0:T(8,128)(2,1)} %param.11) | copy-start | bytes 1179652
  0.0 301.1 %copy-start.40 = (f32[192]{0:T(256)S(1)}, f32[192]{0:T(256)}, u32[]{:S(2)}) copy-start(f32[192]{0:T(256)} %param.12) | copy-start | bytes 2308
  0.0 301.1 %copy-start.39 = (f32[192]{0:T(256)S(1)}, f32[192]{0:T(256)}, u32[]{:S(2)}) copy-start(f32[192]{0:T(256)} %param.13) | copy-start | bytes 2308
  0.0 306.2 %copy-start.34 = (f32[192]{0:T(256)S(1)}, f32[192]{0:T(256)}, u32[]{:S(2)}) copy-start(f32[192]{0:T(256)} %param.15) | copy-start | bytes 2308
  301.5 5.2 collective-permute-start
  304.9 6.0 collective-permute-start.1
  310.9 59.7 %collective-permute-start.2 = (bf16[1,2,6,64,192]{4,3,2,1,0:T(8,128)(2,1)S(1)}, bf16[1,2,6,64,192]{4,3,2,1,0:T(8,128)(2,1)S(1)}, u32[]{:S(2)}, u32[]{:S(2)}) collective-permute-start(bf16[1,2,6,64,192]{4,3,2,1,0:T(8,128)(2,1)S(1)} %pad_maximum_fusion.22), channel_id=1, source_target_pairs={{0,64},{1,65},{2,66},{3,67},{4,68},{5,69},{6,70},{7,71},{8,72},{9,... | collective-permute-start | bytes 884744 | tf_op jit(solution)/shard_map/ppermute | solution.py:28
  388.7 292.7 %copy-start.35 = (f32[192]{0:T(256)S(1)}, f32[192]{0:T(256)}, u32[]{:S(2)}) copy-start(f32[192]{0:T(256)} %param.17) | copy-start | bytes 2308
  388.7 292.7 %copy-start.36 = (f32[192]{0:T(256)S(1)}, f32[192]{0:T(256)}, u32[]{:S(2)}) copy-start(f32[192]{0:T(256)} %param.16) | copy-start | bytes 2308
  681.5 11.1 %copy-start.1 = (bf16[3,3,3,192,192]{4,3,2,1,0:T(8,128)(2,1)S(1)}, bf16[3,3,3,192,192]{4,3,2,1,0:T(8,128)(2,1)}, u32[]{:S(2)}) copy-start(bf16[3,3,3,192,192]{4,3,2,1,0:T(8,128)(2,1)} %param.18) | copy-start | bytes 5971972
  683.2 3.4 collective-permute-start.3
  684.7 5.7 collective-permute-start.4
  690.4 61.0 %copy-start.19 = (bf16[1,4,1,64,192]{4,3,2,1,0:T(8,128)(2,1)}, bf16[1,4,1,64,192]{4,3,2,1,0:T(8,128)(2,1)S(1)}, u32[]{:S(2)}) copy-start(bf16[1,4,1,64,192]{4,3,2,1,0:T(8,128)(2,1)S(1)} %collective-permute-done.4) | copy-start | bytes 294916
  691.3 60.2 %collective-permute-start.5 = (bf16[1,2,6,64,192]{4,3,2,1,0:T(8,128)(2,1)}, bf16[1,2,6,64,192]{4,3,2,1,0:T(8,128)(2,1)S(1)}, u32[]{:S(2)}, u32[]{:S(2)}) collective-permute-start(bf16[1,2,6,64,192]{4,3,2,1,0:T(8,128)(2,1)} %pad_maximum_fusion.20), channel_id=1, source_target_pairs={{0,64},{1,65},{2,66},{3,67},{4,68},{5,69},{6,70},{7,71},{8,72},{9,... | collective-permute-start | bytes 884744 | tf_op jit(solution)/shard_map/ppermute | solution.py:28
  695.4 1.3 copy-start.37
  760.7 1.9 copy-start.27
  762.6 1.3 copy-start.17
  763.3 1.3 copy-start.3
  763.3 1.5 copy-start.16
  766.2 1.4 copy-start.15
  772.0 1.3 copy-start.33
  773.3 1.4 copy-start.8
  773.3 1.5 copy-start.18
  773.3 1.5 copy-start.20
  774.9 1.5 copy-start.28
  778.8 1.5 copy-start.38
  780.3 3.4 copy-start.29
  780.3 3.4 copy-start.41
  780.5 3.6 collective-permute-start.6
  782.2 5.7 collective-permute-start.7
  882.8 3.6 slice-start
  882.9 3.7 slice-start.1
  (20 other events, 22.1 us)
where the time goes:
time: 908 us; the launch traced here: 895 us
  blocking collectives  588 us (65%)
  waiting for transfers between devices  122 us (13%)
  local copies, waits for them, and re-layouts  102 us (11%)
  other arithmetic  48.4 us (5%)
  matrix products  21 us (2%)
  starting transfers between devices  13.1 us (1%)
    psum x2, blocking collectives, group_act(): lax.psum(jnp.sum(grouped, axis=(2, 3, 5)), 'tile') / cell_count  298 us
    psum x2, blocking collectives, group_act(): lax.psum(jnp.sum(centered * centered, axis=(2, 3, 5)), 'tile') / cell_count  290 us
    ppermute x2, waiting for transfers between devices, from_behind(): return lax.ppermute(value, axis, pairs)  109 us
    concatenate x3, local copies, waits for them, and re-layouts, plane_taps(): jnp.concatenate([slab_part[:, :, :, col_tap:col_tap + out_cols] for col_t...  31.3 us
    reshape x3, local copies, waits for them, and re-layouts, plane_taps(): stacked.reshape(-1, 3 * chan_count)  24.8 us
    concatenate x3, other arithmetic, plane_taps(): jnp.concatenate([slab_part[:, :, :, col_tap:col_tap + out_cols] for col_t...  22.9 us
  transfers between devices with their start and end apart: 8, of which 8 were waited for; matrix products, arithmetic and copies ran while one was open for 1% of the time, Pallas kernels for 0%

commit v1 on v0

v1 whole, which is shorter than its diff:
```python
import functools

import jax
import jax.numpy as jnp
from jax import lax
from jax.experimental import pallas as pl
from jax.experimental.pallas import tpu as pltpu
from jax.sharding import PartitionSpec as P

G = 32
EPS = 1e-06
F32 = jnp.float32
BF16 = jnp.bfloat16
VM = pl.BlockSpec(memory_space=pltpu.VMEM)


def dot32(a, b):
    return jnp.dot(a, b, precision=lax.Precision.HIGHEST, preferred_element_type=F32)


def spread(chan):
    lane = lax.broadcasted_iota(jnp.int32, (128, chan), 0)
    col = lax.broadcasted_iota(jnp.int32, (128, chan), 1)
    low = (lane % G) * (chan // G)
    return jnp.where((col >= low) & (col < low + chan // G), 1.0, 0.0).astype(F32)


def gather_groups(chan):
    lane = lax.broadcasted_iota(jnp.int32, (chan, 128), 1)
    col = lax.broadcasted_iota(jnp.int32, (chan, 128), 0)
    low = (lane % G) * (chan // G)
    return jnp.where((col >= low) & (col < low + chan // G), 1.0, 0.0).astype(F32)


def frame_mask(first):
    lane = lax.broadcasted_iota(jnp.int32, (8, 128), 1)
    row = lax.broadcasted_iota(jnp.int32, (8, 128), 0)
    low = (row - first) * G
    return (lane >= low) & (lane < low + G)


def stack_rows(rows):
    width = rows[0].shape[1]
    index = lax.broadcasted_iota(jnp.int32, (8, width), 0)
    out = jnp.zeros((8, width), F32)
    for i, r in enumerate(rows):
        out = jnp.where(index == i, jnp.broadcast_to(r, (8, width)), out)
    return out


def local_stats(load, frames, count, chan, stat_ref):
    mask = frame_mask(0)
    to_group, to_chan = gather_groups(chan), spread(chan)
    sums = stack_rows([jnp.sum(load(f), axis=0, keepdims=True) for f in range(frames)])
    mean = jnp.where(mask, dot32(sums, to_group), 0.0) / count
    mean_chan = dot32(mean, to_chan)
    squares = []
    for f in range(frames):
        d = load(f) - mean_chan[f : f + 1]
        squares.append(jnp.sum(d * d, axis=0, keepdims=True))
    square = jnp.where(mask, dot32(stack_rows(squares), to_group), 0.0)
    packed = jnp.concatenate(
        [jnp.sum(mean, axis=0, keepdims=True), jnp.sum(square, axis=0, keepdims=True)], axis=0
    )
    stat_ref[...] = jnp.broadcast_to(packed[None], stat_ref.shape)


def global_stats(stat_ref, mean_ref, scale_ref, gain_ref, count):
    tiles = stat_ref.shape[0] // 2
    chan = mean_ref.shape[-1]
    to_chan = spread(chan)
    means, spreads = [], []
    for half in range(2):
        part = stat_ref[half * tiles : (half + 1) * tiles]
        total = jnp.sum(part, axis=0)
        mean = total[0:1] / tiles
        off = part - mean[None]
        spread_sum = total[1:2] + count * jnp.sum(off * off, axis=0)[0:1]
        means.append(mean)
        spreads.append(spread_sum / (tiles * count))
    m0, m1 = frame_mask(0), frame_mask(4)
    mean8 = jnp.where(m0, means[0], 0.0) + jnp.where(m1, means[1], 0.0)
    inv8 = jnp.where(m0, lax.rsqrt(spreads[0] + EPS), 0.0) + jnp.where(
        m1, lax.rsqrt(spreads[1] + EPS), 0.0
    )
    mean_chan = dot32(mean8, to_chan)
    scale = dot32(inv8, to_chan) * gain_ref[...]
    for f in range(8):
        mean_ref[f] = mean_chan[f : f + 1]
        scale_ref[f] = scale[f : f + 1]


def shifted(v):
    rows = v.shape[0]
    index = lax.broadcasted_iota(jnp.int32, v.shape, 0)
    left = jnp.where(index == 0, 0.0, pltpu.roll(v, 1, axis=0))
    right = jnp.where(index == rows - 1, 0.0, pltpu.roll(v, rows - 1, axis=0))
    return left, right


def put_row(v, s_ref, t_ref, f, r, out_rows, back):
    a, b = v[:, :128], v[:, 128:192]
    a_left, a_right = shifted(a)
    b_left, b_right = shifted(b)
    s_ref[f, r, :, 0:128] = a_left.astype(BF16)
    s_ref[f, r, :, 128:256] = a.astype(BF16)
    s_ref[f, r, :, 256:384] = a_right.astype(BF16)
    s_ref[f, r, :, 384:512] = jnp.concatenate([b_left, b], axis=1).astype(BF16)
    tail = b_right.astype(BF16)
    for k in range(back):
        if 0 <= r - k < out_rows:
            t_ref[f, r - k, :, 64 * k : 64 * k + 64] = tail


def silu(u):
    half = 0.5 * u
    return half + half * jnp.tanh(half)


def tap_weights(w_ref):
    parts = []
    for t in range(3):
        for r in range(3):
            k = (t * 3 + r) * 3
            parts += [w_ref[k, 0:128], w_ref[k + 1, 0:128], w_ref[k + 2, 0:128]]
            parts += [w_ref[k, 128:192], w_ref[k + 1, 128:192]]
    for t in range(3):
        parts += [w_ref[(t * 3 + r) * 3 + 2, 128:192] for r in range(3)]
        parts.append(jnp.zeros((64, w_ref.shape[-1]), BF16))
    return jnp.concatenate(parts, axis=0)


def conv_rows(s_ref, t_ref, weights, f, nf, row0, t_row0, rows):
    col = s_ref.shape[2]
    m = nf * rows * col
    parts = []
    for t in range(3):
        for r in range(3):
            parts.append(
                s_ref[pl.ds(f + t, nf), row0 + r : row0 + r + rows].reshape(m, 512)
            )
    for t in range(3):
        parts.append(t_ref[pl.ds(f + t, nf), t_row0 : t_row0 + rows].reshape(m, 256))
    return jnp.dot(jnp.concatenate(parts, axis=1), weights, preferred_element_type=F32)


def pack_kernel(x_ref, even_ref, odd_ref, stat_ref):
    odd = lax.rem(lax.axis_index("tile"), 2)
    frames, rows, cols, chan = x_ref.shape
    even_ref[...] = x_ref[:, pl.ds(1 - odd, 3)]
    odd_ref[...] = x_ref[:, pl.ds(odd, 3)]
    local_stats(
        lambda f: x_ref[f].reshape(rows * cols, chan).astype(F32),
        frames,
        rows * cols * (chan // G),
        chan,
        stat_ref,
    )


def conv_one_kernel(
    ring,
    row_list,
    x_ref,
    p1_ref,
    p2_ref,
    xc_ref,
    p1c_ref,
    p2c_ref,
    g_ref,
    gain_ref,
    shift_ref,
    w_ref,
    bias_ref,
    *rest,
):
    if ring:
        out_ref, cache_ref, stat_ref, mean_ref, scale_ref, s_ref, t_ref = rest
    else:
        out_ref, cache_ref, mean_ref, scale_ref, s_ref, t_ref = rest
    frames, rows, cols, chan = x_ref.shape
    tm, tile = lax.axis_index("tm"), lax.axis_index("tile")
    last = lax.axis_size("tile") - 1
    odd = lax.rem(tile, 2) == 1
    count = rows * cols * (chan // G)
    global_stats(g_ref, mean_ref, scale_ref, gain_ref, count)
    shift = shift_ref[...]
    t_ref[...] = jnp.zeros_like(t_ref)

    def fetch(refs, frame, row):
        own, p1, p2 = refs
        if row < 3:
            return jnp.where(odd, p1[frame, row].astype(F32), p2[frame, row].astype(F32))
        if row < 3 + rows:
            return own[frame, row - 3].astype(F32)
        row = row - 3 - rows
        return jnp.where(odd, p2[frame, row].astype(F32), p1[frame, row].astype(F32))

    def norm_frame(refs, frame, slot, index):
        mean, scale = mean_ref[index], scale_ref[index]
        place = 0
        for first, n, _ in row_list:
            for row in range(first, first + n + 2):
                v = silu((fetch(refs, frame, row) - mean) * scale + shift)
                if row < 3:
                    v = jnp.where(tile > 0, v, 0.0)
                if row >= 3 + rows:
                    v = jnp.where(tile < last, v, 0.0)
                put_run(v, slot, place, row - first, n)
            place += n + 2

    def put_run(v, slot, place, r, n):
        a, b = v[:, :128], v[:, 128:192]
        a_left, a_right = shifted(a)
        b_left, b_right = shifted(b)
        k = place + r
        s_ref[slot, k, :, 0:128] = a_left.astype(BF16)
        s_ref[slot, k, :, 128:256] = a.astype(BF16)
        s_ref[slot, k, :, 256:384] = a_right.astype(BF16)
        s_ref[slot, k, :, 384:512] = jnp.concatenate([b_left, b], axis=1).astype(BF16)
        tail = b_right.astype(BF16)
        for j in range(3):
            if 0 <= r - j < n:
                t_ref[slot, place + r - j, :, 64 * j : 64 * j + 64] = tail

    @pl.when(tm == 0)
    def _():
        s_ref[0:2] = jnp.zeros_like(s_ref[0:2])

    @pl.when(tm > 0)
    def _():
        def step(f, c):
            norm_frame((xc_ref, p1c_ref, p2c_ref), f + frames - 2, f, f + frames - 2)
            return c

        lax.fori_loop(0, 2, step, 0)

    def step(f, c):
        norm_frame((x_ref, p1_ref, p2_ref), f, f + 2, tm * frames + f)
        return c

    lax.fori_loop(0, frames, step, 0)
    weights = tap_weights(w_ref)
    bias = bias_ref[...]
    place = 0
    for first, n, where_to in row_list:
        for f in range(0, frames, 2):
            out = conv_rows(s_ref, t_ref, weights, f, 2, place, place, n) + bias
            out = out.astype(BF16).reshape(2, n, cols, chan)
            out_ref[f : f + 2, where_to : where_to + n] = out
            if f >= frames - 2:
                cache_ref[:, where_to : where_to + n] = out
        place += n + 2
    if ring:
        local_stats(
            lambda f: out_ref[f].reshape(rows * cols, chan).astype(F32),
            frames,
            count,
            chan,
            stat_ref,
        )


def conv_two_kernel(
    x_ref,
    p1_ref,
    p2_ref,
    h_ref,
    hh_ref,
    hc_ref,
    hhc_ref,
    g_ref,
    gain_ref,
    shift_ref,
    w_ref,
    bias_ref,
    wu_ref,
    bu_ref,
    out_ref,
    mean_ref,
    scale_ref,
    s_ref,
    t_ref,
    sj_ref,
    tj_ref,
):
    frames, rows, cols, chan = x_ref.shape
    tm, tile = lax.axis_index("tm"), lax.axis_index("tile")
    last = lax.axis_size("tile") - 1
    odd = lax.rem(tile, 2) == 1
    global_stats(g_ref, mean_ref, scale_ref, gain_ref, rows * cols * (chan // G))
    shift = shift_ref[...]
    t_ref[...] = jnp.zeros_like(t_ref)

    def norm_frame(own, halo, frame, slot, index):
        mean, scale = mean_ref[index], scale_ref[index]
        for row in range(rows + 4):
            if row < 2:
                v = halo[frame, row]
            elif row < rows + 2:
                v = own[frame, row - 2]
            else:
                v = halo[frame, row - rows]
            v = silu((v.astype(F32) - mean) * scale + shift)
            if row < 2:
                v = jnp.where(tile > 0, v, 0.0)
            if row >= rows + 2:
                v = jnp.where(tile < last, v, 0.0)
            put_row(v, s_ref, t_ref, slot, row, rows + 2, 3)

    @pl.when(tm == 0)
    def _():
        s_ref[0:2] = jnp.zeros_like(s_ref[0:2])

    @pl.when(tm > 0)
    def _():
        def step(f, c):
            norm_frame(hc_ref, hhc_ref, f, f, f + frames - 2)
            return c

        lax.fori_loop(0, 2, step, 0)

    def step(f, c):
        norm_frame(h_ref, hh_ref, f, f + 2, tm * frames + f)
        return c

    lax.fori_loop(0, frames, step, 0)
    weights = tap_weights(w_ref)
    bias, bias_up = bias_ref[...], bu_ref[...]

    def frame_out(f, c):
        out = conv_rows(s_ref, t_ref, weights, f, 1, 0, 0, rows + 2) + bias
        for r in range(rows + 2):
            if r == 0:
                x = jnp.where(odd, p1_ref[f, 2].astype(F32), p2_ref[f, 2].astype(F32))
            elif r <= rows:
                x = x_ref[f, r - 1].astype(F32)
            else:
                x = jnp.where(odd, p2_ref[f, 0].astype(F32), p1_ref[f, 0].astype(F32))
            v = (out[r * cols : (r + 1) * cols] + x).astype(BF16).astype(F32)
            if r == 0:
                v = jnp.where(tile > 0, v, 0.0)
            if r > rows:
                v = jnp.where(tile < last, v, 0.0)
            put_row(v, sj_ref, tj_ref, 0, r, rows + 1, 2)
        m = rows * cols
        for s in range(2):
            parts = [sj_ref[0, s + i : s + i + rows].reshape(m, 512) for i in range(2)]
            parts.append(tj_ref[0, s : s + rows].reshape(m, 128))
            up = jnp.dot(jnp.concatenate(parts, axis=1), wu_ref[s], preferred_element_type=F32)
            up = (up + bias_up).astype(BF16).reshape(rows, cols, chan)
            for y in range(rows):
                out_ref[f, 2 * y + s] = up[y]
        return c

    lax.fori_loop(0, frames, frame_out, 0)


def folded_up(up_kernel):
    k = up_kernel.astype(F32)
    zero = jnp.zeros_like(k[0, 0])
    out = []
    for rows in ((k[0], k[1] + k[2]), (k[0] + k[1], k[2])):
        taps = []
        for c in rows:
            taps.append(
                [
                    jnp.concatenate([c[0], zero], axis=1),
                    jnp.concatenate([c[1] + c[2], c[0] + c[1]], axis=1),
                    jnp.concatenate([zero, c[2]], axis=1),
                ]
            )
        parts = []
        for t in taps:
            parts += [t[0][:128], t[1][:128], t[2][:128], t[0][128:], t[1][128:]]
        parts += [t[2][128:] for t in taps]
        out.append(jnp.concatenate(parts, axis=0))
    return jnp.stack(out).astype(BF16)


def exchange(stat):
    return lax.all_to_all(stat, ("tm", "tile"), 0, 0)


def body(
    features,
    gain_one,
    shift_one,
    kernel_one,
    bias_one,
    gain_two,
    shift_two,
    kernel_two,
    bias_two,
    up_kernel,
    up_bias,
):
    x = features[0]
    frames, rows, cols, chan = x.shape
    tiles = lax.axis_size("tile")
    even_pairs = [(i, i ^ 1) for i in range(tiles)]
    odd_pairs = [(i, i + 1) for i in range(1, tiles - 1, 2)]
    odd_pairs += [(b, a) for a, b in odd_pairs]
    down = [(0, 1)]
    shape = jax.ShapeDtypeStruct
    stat_shape = shape((2 * tiles, 2, 128), F32)
    limit = pltpu.CompilerParams(vmem_limit_bytes=48 * 2**20)

    xc = lax.ppermute(x, "tm", down)
    even, odd, stat = pl.pallas_call(
        pack_kernel,
        out_shape=(
            shape((frames, 3, cols, chan), BF16),
            shape((frames, 3, cols, chan), BF16),
            stat_shape,
        ),
        in_specs=[VM],
        out_specs=(VM, VM, VM),
        compiler_params=limit,
        name="pack",
    )(x)
    p1 = lax.ppermute(even, "tile", even_pairs)
    p2 = lax.ppermute(odd, "tile", odd_pairs)
    p1c = lax.ppermute(p1, "tm", down)
    p2c = lax.ppermute(p2, "tm", down)
    all_one = exchange(stat)
    w_one = kernel_one.reshape(27, chan, chan)
    w_two = kernel_two.reshape(27, chan, chan)
    w_up = folded_up(up_kernel)
    vec = lambda v: v.reshape(1, chan)
    args = (x, p1, p2, xc, p1c, p2c, all_one, vec(gain_one), vec(shift_one), w_one, vec(bias_one))

    def conv_one(ring, row_list):
        in_rows = sum(n + 2 for _, n, _ in row_list)
        outs = (shape((frames, rows, cols, chan), BF16), shape((2, rows, cols, chan), BF16))
        if ring:
            outs += (stat_shape,)
        flops = 2 * frames * rows * cols * 27 * chan * chan
        return pl.pallas_call(
            functools.partial(conv_one_kernel, ring, row_list),
            out_shape=outs,
            in_specs=[VM] * len(args),
            out_specs=(VM,) * len(outs),
            scratch_shapes=[
                pltpu.VMEM((8, 1, chan), F32),
                pltpu.VMEM((8, 1, chan), F32),
                pltpu.VMEM((frames + 2, in_rows, cols, 512), BF16),
                pltpu.VMEM((frames + 2, in_rows, cols, 256), BF16),
            ],
            compiler_params=limit,
            cost_estimate=pl.CostEstimate(
                flops=flops, bytes_accessed=4 * 2**20, transcendentals=0
            ),
            name="conv_one" if ring else "conv_one_rim",
        )(*args)

    hidden, hidden_c, stat_two = conv_one(True, ((2, rows, 0),))
    all_two = exchange(stat_two)
    rim, rim_c = conv_one(False, ((0, 2, 0), (rows + 2, 2, 2)))
    hc = lax.ppermute(hidden_c, "tm", down)
    rim_cc = lax.ppermute(rim_c, "tm", down)
    bias_up = jnp.concatenate([up_bias, up_bias]).reshape(1, chan)
    out = pl.pallas_call(
        conv_two_kernel,
        out_shape=shape((frames, 2 * rows, cols, chan), BF16),
        in_specs=[VM] * 14,
        out_specs=VM,
        scratch_shapes=[
            pltpu.VMEM((8, 1, chan), F32),
            pltpu.VMEM((8, 1, chan), F32),
            pltpu.VMEM((frames + 2, rows + 4, cols, 512), BF16),
            pltpu.VMEM((frames + 2, rows + 2, cols, 256), BF16),
            pltpu.VMEM((1, rows + 2, cols, 512), BF16),
            pltpu.VMEM((1, rows + 1, cols, 128), BF16),
        ],
        compiler_params=limit,
        cost_estimate=pl.CostEstimate(
            flops=3 * frames * rows * cols * 27 * chan * chan,
            bytes_accessed=4 * 2**20,
            transcendentals=0,
        ),
        name="conv_two",
    )(
        x, p1, p2, hidden, rim, hc, rim_cc, all_two,
        vec(gain_two), vec(shift_two), w_two, vec(bias_two), w_up, bias_up,
    )
    return out[None]


def solution(mesh):
    return jax.shard_map(
        body,
        mesh=mesh,
        in_specs=(P(None, "tm", "tile", None, None),) + (P(),) * 10,
        out_specs=P(None, "tm", "tile", None, None),
        check_vma=False,
    )
```

time: 908 us -> 84.3 us (0.09); the launches traced: 895 us -> 83.7 us
  blocking collectives: 588 us -> 0 us
  waiting for transfers between devices: 122 us -> 1.11 us
  local copies, waits for them, and re-layouts: 102 us -> 12.9 us
  other arithmetic: 48.4 us -> 4.47 us
  Pallas kernels: 0 us -> 31.5 us
  matrix products: 21 us -> 0 us
  starting transfers between devices: 13.1 us -> 33.3 us
    psum x4 -> x0, blocking collectives: 588 us -> none  [the longest x2 298 us: group_act(): lax.psum(jnp.sum(grouped, axis=(2, 3, 5)), 'tile') / cell_count]
    ppermute x8 -> x7, waiting for transfers between devices: 122 us -> 1.11 us  [the longest x1 0.87 us: body(): rim_cc = lax.ppermute(rim_c, 'tm', down)]
    concatenate x19 -> x1, other arithmetic: 36.3 us -> 0.08 us  [body(): bias_up = jnp.concatenate([up_bias, up_bias]).reshape(1, chan)]
    concatenate x6 -> x2, local copies, waits for them, and re-layouts: 33.8 us -> 0.78 us  [folded_up(): out.append(jnp.concatenate(parts, axis=0))]
    pallas_call x0 -> x4, Pallas kernels: none -> 31.5 us  [the longest x2 15 us: conv_one(): pl.pallas_call(functools.partial(conv_one_kernel, ring, row_list), out_sh...]
    reshape x5 -> x0, local copies, waits for them, and re-layouts: 27.4 us -> none  [the longest x3 24.8 us: plane_taps(): stacked.reshape(-1, 3 * chan_count)]
    slice x14 -> x0, local copies, waits for them, and re-layouts: 24.7 us -> none  [the longest x6 10.9 us: causal_taps(): slab_part[:, :, :, col_tap:col_tap + col_count]]
    all_to_all x0 -> x2, starting transfers between devices: none -> 24.1 us  [exchange(): return lax.all_to_all(stat, ('tm', 'tile'), 0, 0)]
  transfers between devices with their start and end apart: 8 -> 9, of which waited for: 8 -> 2; matrix products, arithmetic and copies ran while one was open for 1% -> 14% of each run, Pallas kernels for 0% -> 10%
where the time goes in v1:
time: 84.3 us; the launch traced here: 83.7 us
  starting transfers between devices  33.3 us (40%)
  Pallas kernels  31.5 us (37%)
  local copies, waits for them, and re-layouts  12.9 us (15%)
  other arithmetic  4.47 us (5%)
  waiting for transfers between devices  1.11 us (1%)
    all_to_all x2, starting transfers between devices, exchange(): return lax.all_to_all(stat, ('tm', 'tile'), 0, 0)  24.1 us
    pallas_call x2, Pallas kernels, conv_one(): pl.pallas_call(functools.partial(conv_one_kernel, ring, row_list), out_sh...  15 us
    pallas_call x1, Pallas kernels, body(): pl.pallas_call(conv_two_kernel, out_shape=shape((frames, 2 * rows, cols,...  14.8 us
    unnamed x50, local copies, waits for them, and re-layouts  11.7 us
    ppermute x1, starting transfers between devices, body(): p1 = lax.ppermute(even, 'tile', even_pairs)  2.04 us
    pallas_call x1, Pallas kernels, body(): pl.pallas_call(pack_kernel, out_shape=(shape((frames, 3, cols, chan), BF1...  1.72 us
  transfers between devices with their start and end apart: 9, of which 2 were waited for; matrix products, arithmetic and copies ran while one was open for 14% of the time, Pallas kernels for 10%

profile of v1, /device:TPU:1, one launch (start us, length us, event | category | flops | bytes accessed | tf_op | source)
XLA Modules:
  0.0 83.7 jit_solution(15603452514441053734)
XLA Ops:
  0.0 1.3 %collective-permute-start.2 = (bf16[4,4,64,192]{3,2,1,0:T(8,128)(2,1)}, bf16[4,4,64,192]{3,2,1,0:T(8,128)(2,1)S(1)}, u32[]{:S(2)}, u32[]{:S(2)}) collective-permute-start(bf16[4,4,64,192]{3,2,1,0:T(8,128)(2,1)} %bitcast.69), channel_id=1, source_target_pairs={{0,64},{1,65},{2,66},{3,67},{4,68},{5,69},{6,70},{7,71},{8,72},{9,... | collective-permute-start | bytes 1179656 | tf_op jit(solution)/shard_map/ppermute | solution.py:409
  1.3 1.0 %copy-done = bf16[1,4,4,64,192]{4,3,2,1,0:T(8,128)(2,1)S(1)} copy-done((bf16[1,4,4,64,192]{4,3,2,1,0:T(8,128)(2,1)S(1)}, bf16[1,4,4,64,192]{4,3,2,1,0:T(8,128)(2,1)}, u32[]{:S(2)}) %copy-start) | copy-done | bytes 393240
  2.3 1.7 %pack.1 = (bf16[4,3,64,192]{3,2,1,0:T(8,128)(2,1)S(1)}, bf16[4,3,64,192]{3,2,1,0:T(8,128)(2,1)S(1)}, f32[128,2,128]{2,1,0:T(2,128)}) custom-call(bf16[4,4,64,192]{3,2,1,0:T(8,128)(2,1)S(1)} %bitcast.70), custom_call_target="tpu_custom_call" | custom-call | tf_op jit(solution)/shard_map/pack/pallas_call | solution.py:410
  4.1 2.0 %collective-permute-start = (bf16[4,3,64,192]{3,2,1,0:T(8,128)(2,1)S(1)}, bf16[4,3,64,192]{3,2,1,0:T(8,128)(2,1)S(1)}, u32[]{:S(2)}, u32[]{:S(2)}) collective-permute-start(bf16[4,3,64,192]{3,2,1,0:T(8,128)(2,1)S(1)} %get-tuple-element.13), channel_id=1, source_target_pairs={{0,1},{1,0},{2,3},{3,2},{4,5},{5,4},{6,7},{7,6},{8,9},{9,8},{10,11... | collective-permute-start | bytes 884744 | tf_op jit(solution)/shard_map/ppermute | solution.py:422
  6.1 0.7 collective-permute-start.1
  6.8 13.6 %all-to-all-start = ((f32[128,2,128]{2,1,0:T(2,128)}), f32[128,2,128]{2,1,0:T(2,128)S(1)}, u32[]{:S(2)}, u32[]{:S(2)}) async-start(f32[128,2,128]{2,1,0:T(2,128)} %get-tuple-element.15), calls=%async_computation | async-start | bytes 262144 | tf_op jit(solution)/shard_map/all_to_all | solution.py:382
  20.4 1.1 %convert_element_type.4 = f32[3,3,192,96]{3,2,1,0:T(8,128)S(1)} convert(bf16[3,3,192,96]{3,2,1,0:T(8,128)(2,1)} %param.20) | non-fusion elementwise | flops 165888 | bytes 995328 | tf_op jit(solution)/shard_map/convert_element_type | solution.py:360
  22.7 0.7 slice_dynamic-update-slice_fusion.5
  23.6 0.6 slice_dynamic-update-slice_fusion.4
  24.2 0.6 slice_dynamic-update-slice_fusion.3
  24.8 0.6 constant_dynamic-update-slice_fusion.11
  25.5 0.7 constant_dynamic-update-slice_fusion.10
  26.3 0.6 slice_dynamic-update-slice_fusion.2
  26.9 0.6 slice_dynamic-update-slice_fusion.1
  27.5 0.6 slice_dynamic-update-slice_fusion
  28.8 1.3 %collective-permute-start.3 = (bf16[4,3,64,192]{3,2,1,0:T(8,128)(2,1)S(1)}, bf16[4,3,64,192]{3,2,1,0:T(8,128)(2,1)S(1)}, u32[]{:S(2)}, u32[]{:S(2)}) collective-permute-start(bf16[4,3,64,192]{3,2,1,0:T(8,128)(2,1)S(1)} %collective-permute-done.p1_ref), channel_id=1, source_target_pairs={{0,64},{1,65},{2,66},{3,67},{4,68},{5,69},{6,70},{7,71},{8,72},{9,... | collective-permute-start | bytes 884744 | tf_op jit(solution)/shard_map/ppermute | solution.py:424
  30.1 1.3 %collective-permute-start.4 = (bf16[4,3,64,192]{3,2,1,0:T(8,128)(2,1)S(1)}, bf16[4,3,64,192]{3,2,1,0:T(8,128)(2,1)S(1)}, u32[]{:S(2)}, u32[]{:S(2)}) collective-permute-start(bf16[4,3,64,192]{3,2,1,0:T(8,128)(2,1)S(1)} %collective-permute-done.1.p2_ref), channel_id=1, source_target_pairs={{0,64},{1,65},{2,66},{3,67},{4,68},{5,69},{6,70},{7,71},{8,72},{9,... | collective-permute-start | bytes 884744 | tf_op jit(solution)/shard_map/ppermute | solution.py:425
  31.4 0.7 constant_dynamic-update-slice_fusion.8
  32.1 0.7 constant_dynamic-update-slice_fusion.7
  32.8 0.7 constant_dynamic-update-slice_fusion.6
  33.7 8.6 %conv_one.1 = (bf16[4,4,64,192]{3,2,1,0:T(8,128)(2,1)S(1)}, bf16[2,4,64,192]{3,2,1,0:T(8,128)(2,1)S(1)}, f32[128,2,128]{2,1,0:T(2,128)}) custom-call(bf16[4,4,64,192]{3,2,1,0:T(8,128)(2,1)S(1)} %bitcast.71, bf16[4,3,64,192]{3,2,1,0:T(8,128)(2,1)S(1)} %collective-permute-done.p1_ref, bf16[4,3,64,192]{3,2,1,0:T(8,128)(2,1)S(1)} %collective-permute-done.1.p2_ref, ...), custom_call_target="tpu_custom_call" | custom-call | flops 2038431744 | bytes 4194304 | tf_op jit(solution)/shard_map/conv_one/pallas_call | solution.py:439
  42.4 0.8 copy-done.9
  43.2 1.3 %collective-permute-start.5 = (bf16[2,4,64,192]{3,2,1,0:T(8,128)(2,1)S(1)}, bf16[2,4,64,192]{3,2,1,0:T(8,128)(2,1)S(1)}, u32[]{:S(2)}, u32[]{:S(2)}) collective-permute-start(bf16[2,4,64,192]{3,2,1,0:T(8,128)(2,1)S(1)} %get-tuple-element.18), channel_id=1, source_target_pairs={{0,64},{1,65},{2,66},{3,67},{4,68},{5,69},{6,70},{7,71},{8,72},{9,... | collective-permute-start | bytes 589832 | tf_op jit(solution)/shard_map/ppermute | solution.py:460
  44.5 10.5 %all-to-all-start.1 = ((f32[128,2,128]{2,1,0:T(2,128)}), f32[128,2,128]{2,1,0:T(2,128)S(1)}, u32[]{:S(2)}, u32[]{:S(2)}) async-start(f32[128,2,128]{2,1,0:T(2,128)} %get-tuple-element.20), calls=%async_computation.1 | async-start | bytes 262144 | tf_op jit(solution)/shard_map/all_to_all | solution.py:382
  55.0 1.7 %copy-done.2 = bf16[3,3,3,192,192]{4,3,2,1,0:T(8,128)(2,1)S(1)} copy-done((bf16[3,3,3,192,192]{4,3,2,1,0:T(8,128)(2,1)S(1)}, bf16[3,3,3,192,192]{4,3,2,1,0:T(8,128)(2,1)}, u32[]{:S(2)}) %copy-start.2) | copy-done | bytes 1990680
  56.8 6.4 %conv_one_rim.1 = (bf16[4,4,64,192]{3,2,1,0:T(8,128)(2,1)S(1)}, bf16[2,4,64,192]{3,2,1,0:T(8,128)(2,1)}) custom-call(bf16[4,4,64,192]{3,2,1,0:T(8,128)(2,1)S(1)} %bitcast.72, bf16[4,3,64,192]{3,2,1,0:T(8,128)(2,1)S(1)} %collective-permute-done.p1_ref, bf16[4,3,64,192]{3,2,1,0:T(8,128)(2,1)S(1)} %collective-permute-done.1.p2_ref, ...), custom_call_target="tpu_custom_call" | custom-call | flops 2038431744 | bytes 4194304 | tf_op jit(solution)/shard_map/conv_one_rim/pallas_call | solution.py:439
  63.2 1.3 %collective-permute-start.6 = (bf16[2,4,64,192]{3,2,1,0:T(8,128)(2,1)}, bf16[2,4,64,192]{3,2,1,0:T(8,128)(2,1)S(1)}, u32[]{:S(2)}, u32[]{:S(2)}) collective-permute-start(bf16[2,4,64,192]{3,2,1,0:T(8,128)(2,1)} %get-tuple-element.19), channel_id=1, source_target_pairs={{0,64},{1,65},{2,66},{3,67},{4,68},{5,69},{6,70},{7,71},{8,72},{9,... | collective-permute-start | bytes 589832 | tf_op jit(solution)/shard_map/ppermute | solution.py:461
  64.5 1.3 %pad_maximum_fusion.wu_ref = bf16[2,1152,192]{2,1,0:T(8,128)(2,1)S(1)} fusion(bf16[1,1152,192]{2,1,0:T(8,128)(2,1)} %bitcast.22, bf16[1,1152,192]{2,1,0:T(8,128)(2,1)S(1)} %bitcast.86), kind=kLoop, calls=%fused_computation | loop fusion | flops 442368 | bytes 1769472 | tf_op jit(solution)/shard_map/stack | solution.py:378
  66.0 0.9 %collective-permute-done.6.hhc_ref = bf16[2,4,64,192]{3,2,1,0:T(8,128)(2,1)S(1)} collective-permute-done((bf16[2,4,64,192]{3,2,1,0:T(8,128)(2,1)}, bf16[2,4,64,192]{3,2,1,0:T(8,128)(2,1)S(1)}, u32[]{:S(2)}, u32[]{:S(2)}) %collective-permute-start.6) | collective-permute-done | bytes 196640 | tf_op jit(solution)/shard_map/ppermute | solution.py:461
  66.8 1.0 %copy-done.10 = bf16[4,4,64,192]{3,2,1,0:T(8,128)(2,1)S(1)} copy-done((bf16[4,4,64,192]{3,2,1,0:T(8,128)(2,1)S(1)}, bf16[4,4,64,192]{3,2,1,0:T(8,128)(2,1)}, u32[]{:S(2)}) %copy-start.10) | copy-done | bytes 393240
  67.9 1.0 %copy-done.12 = bf16[4,4,64,192]{3,2,1,0:T(8,128)(2,1)S(1)} copy-done((bf16[4,4,64,192]{3,2,1,0:T(8,128)(2,1)S(1)}, bf16[4,4,64,192]{3,2,1,0:T(8,128)(2,1)}, u32[]{:S(2)}) %copy-start.12) | copy-done | bytes 393240
  68.9 14.8 %conv_two.1 = bf16[4,8,64,192]{3,2,1,0:T(8,128)(2,1)} custom-call(bf16[4,4,64,192]{3,2,1,0:T(8,128)(2,1)S(1)} %bitcast.73, bf16[4,3,64,192]{3,2,1,0:T(8,128)(2,1)S(1)} %collective-permute-done.p1_ref, bf16[4,3,64,192]{3,2,1,0:T(8,128)(2,1)S(1)} %collective-permute-done.1.p2_ref, bf16[4,4,64,192]{3,2,1,0:T(8,128)(2,1)S(1)} %copy-done.10, ...), custom_call_target="tpu_custom_call" | custom-call | flops 3057647616 | bytes 4194304 | tf_op jit(solution)/shard_map/conv_two/pallas_call | solution.py:463
  (63 shorter events, 2.3 us)
Async XLA Ops:
  0.0 33.5 %collective-permute-start.2 = (bf16[4,4,64,192]{3,2,1,0:T(8,128)(2,1)}, bf16[4,4,64,192]{3,2,1,0:T(8,128)(2,1)S(1)}, u32[]{:S(2)}, u32[]{:S(2)}) collective-permute-start(bf16[4,4,64,192]{3,2,1,0:T(8,128)(2,1)} %bitcast.69), channel_id=1, source_target_pairs={{0,64},{1,65},{2,66},{3,67},{4,68},{5,69},{6,70},{7,71},{8,72},{9,... | collective-permute-start | bytes 1179656 | tf_op jit(solution)/shard_map/ppermute | solution.py:409
  1.3 1.0 %copy-start = (bf16[1,4,4,64,192]{4,3,2,1,0:T(8,128)(2,1)S(1)}, bf16[1,4,4,64,192]{4,3,2,1,0:T(8,128)(2,1)}, u32[]{:S(2)}) copy-start(bf16[1,4,4,64,192]{4,3,2,1,0:T(8,128)(2,1)} %param.11) | copy-start | bytes 1179652
  4.1 24.7 %collective-permute-start = (bf16[4,3,64,192]{3,2,1,0:T(8,128)(2,1)S(1)}, bf16[4,3,64,192]{3,2,1,0:T(8,128)(2,1)S(1)}, u32[]{:S(2)}, u32[]{:S(2)}) collective-permute-start(bf16[4,3,64,192]{3,2,1,0:T(8,128)(2,1)S(1)} %get-tuple-element.13), channel_id=1, source_target_pairs={{0,1},{1,0},{2,3},{3,2},{4,5},{5,4},{6,7},{7,6},{8,9},{9,8},{10,11... | collective-permute-start | bytes 884744 | tf_op jit(solution)/shard_map/ppermute | solution.py:422
  6.1 24.0 %collective-permute-start.1 = (bf16[4,3,64,192]{3,2,1,0:T(8,128)(2,1)S(1)}, bf16[4,3,64,192]{3,2,1,0:T(8,128)(2,1)S(1)}, u32[]{:S(2)}, u32[]{:S(2)}) collective-permute-start(bf16[4,3,64,192]{3,2,1,0:T(8,128)(2,1)S(1)} %get-tuple-element.14), channel_id=1, source_target_pairs={{1,2},{3,4},{5,6},{7,8},{9,10},{11,12},{13,14},{15,16},{17,18},{19... | collective-permute-start | bytes 884744 | tf_op jit(solution)/shard_map/ppermute | solution.py:423
  6.8 26.7 %all-to-all-start = ((f32[128,2,128]{2,1,0:T(2,128)}), f32[128,2,128]{2,1,0:T(2,128)S(1)}, u32[]{:S(2)}, u32[]{:S(2)}) async-start(f32[128,2,128]{2,1,0:T(2,128)} %get-tuple-element.15), calls=%async_computation | async-start | bytes 262144 | tf_op jit(solution)/shard_map/all_to_all | solution.py:382
  22.4 11.3 %copy-start.1 = (bf16[1,4,4,64,192]{4,3,2,1,0:T(8,128)(2,1)S(1)}, bf16[1,4,4,64,192]{4,3,2,1,0:T(8,128)(2,1)}, u32[]{:S(2)}) copy-start(bf16[1,4,4,64,192]{4,3,2,1,0:T(8,128)(2,1)} %param.11) | copy-start | bytes 1179652
  22.4 11.3 %copy-start.3 = (f32[192]{0:T(256)S(1)}, f32[192]{0:T(256)}, u32[]{:S(2)}) copy-start(f32[192]{0:T(256)} %param.12) | copy-start | bytes 2308
  22.5 11.3 %copy-start.4 = (f32[192]{0:T(256)S(1)}, f32[192]{0:T(256)}, u32[]{:S(2)}) copy-start(f32[192]{0:T(256)} %param.13) | copy-start | bytes 2308
  22.5 11.3 %copy-start.5 = (f32[192]{0:T(256)S(1)}, f32[192]{0:T(256)}, u32[]{:S(2)}) copy-start(f32[192]{0:T(256)} %param.15) | copy-start | bytes 2308
  22.6 10.1 %copy-start.13 = (bf16[1152,192]{1,0:T(8,128)(2,1)}, bf16[1152,192]{1,0:T(8,128)(2,1)S(1)}, u32[]{:S(2)}) copy-start(bf16[1152,192]{1,0:T(8,128)(2,1)S(1)} %constant_dynamic-update-slice_fusion) | copy-start | bytes 1327108
  28.8 4.7 %collective-permute-start.3 = (bf16[4,3,64,192]{3,2,1,0:T(8,128)(2,1)S(1)}, bf16[4,3,64,192]{3,2,1,0:T(8,128)(2,1)S(1)}, u32[]{:S(2)}, u32[]{:S(2)}) collective-permute-start(bf16[4,3,64,192]{3,2,1,0:T(8,128)(2,1)S(1)} %collective-permute-done.p1_ref), channel_id=1, source_target_pairs={{0,64},{1,65},{2,66},{3,67},{4,68},{5,69},{6,70},{7,71},{8,72},{9,... | collective-permute-start | bytes 884744 | tf_op jit(solution)/shard_map/ppermute | solution.py:424
  30.1 3.6 %collective-permute-start.4 = (bf16[4,3,64,192]{3,2,1,0:T(8,128)(2,1)S(1)}, bf16[4,3,64,192]{3,2,1,0:T(8,128)(2,1)S(1)}, u32[]{:S(2)}, u32[]{:S(2)}) collective-permute-start(bf16[4,3,64,192]{3,2,1,0:T(8,128)(2,1)S(1)} %collective-permute-done.1.p2_ref), channel_id=1, source_target_pairs={{0,64},{1,65},{2,66},{3,67},{4,68},{5,69},{6,70},{7,71},{8,72},{9,... | collective-permute-start | bytes 884744 | tf_op jit(solution)/shard_map/ppermute | solution.py:425
  42.4 0.8 copy-start.9
  43.2 22.8 %collective-permute-start.5 = (bf16[2,4,64,192]{3,2,1,0:T(8,128)(2,1)S(1)}, bf16[2,4,64,192]{3,2,1,0:T(8,128)(2,1)S(1)}, u32[]{:S(2)}, u32[]{:S(2)}) collective-permute-start(bf16[2,4,64,192]{3,2,1,0:T(8,128)(2,1)S(1)} %get-tuple-element.18), channel_id=1, source_target_pairs={{0,64},{1,65},{2,66},{3,67},{4,68},{5,69},{6,70},{7,71},{8,72},{9,... | collective-permute-start | bytes 589832 | tf_op jit(solution)/shard_map/ppermute | solution.py:460
  44.5 21.5 %all-to-all-start.1 = ((f32[128,2,128]{2,1,0:T(2,128)}), f32[128,2,128]{2,1,0:T(2,128)S(1)}, u32[]{:S(2)}, u32[]{:S(2)}) async-start(f32[128,2,128]{2,1,0:T(2,128)} %get-tuple-element.20), calls=%async_computation.1 | async-start | bytes 262144 | tf_op jit(solution)/shard_map/all_to_all | solution.py:382
  55.0 1.8 %copy-start.2 = (bf16[3,3,3,192,192]{4,3,2,1,0:T(8,128)(2,1)S(1)}, bf16[3,3,3,192,192]{4,3,2,1,0:T(8,128)(2,1)}, u32[]{:S(2)}) copy-start(bf16[3,3,3,192,192]{4,3,2,1,0:T(8,128)(2,1)} %param.14) | copy-start | bytes 5971972
  56.8 7.7 %copy-start.14 = (bf16[1152,192]{1,0:T(8,128)(2,1)S(1)}, bf16[1152,192]{1,0:T(8,128)(2,1)}, u32[]{:S(2)}) copy-start(bf16[1152,192]{1,0:T(8,128)(2,1)} %copy-done.13) | copy-start | bytes 1327108
  63.2 2.7 %copy-start.11 = (bf16[4,4,64,192]{3,2,1,0:T(8,128)(2,1)}, bf16[4,4,64,192]{3,2,1,0:T(8,128)(2,1)S(1)}, u32[]{:S(2)}) copy-start(bf16[4,4,64,192]{3,2,1,0:T(8,128)(2,1)S(1)} %get-tuple-element.17.hh_ref) | copy-start | bytes 1179652
  63.2 3.6 %collective-permute-start.6 = (bf16[2,4,64,192]{3,2,1,0:T(8,128)(2,1)}, bf16[2,4,64,192]{3,2,1,0:T(8,128)(2,1)S(1)}, u32[]{:S(2)}, u32[]{:S(2)}) collective-permute-start(bf16[2,4,64,192]{3,2,1,0:T(8,128)(2,1)} %get-tuple-element.19), channel_id=1, source_target_pairs={{0,64},{1,65},{2,66},{3,67},{4,68},{5,69},{6,70},{7,71},{8,72},{9,... | collective-permute-start | bytes 589832 | tf_op jit(solution)/shard_map/ppermute | solution.py:461
  64.5 1.4 %copy-start.15 = (f32[96]{0:T(128)S(1)}, f32[96]{0:T(128)}, u32[]{:S(2)}) copy-start(f32[96]{0:T(128)} %param.21) | copy-start | bytes 1156
  64.5 2.3 %copy-start.6 = (f32[192]{0:T(256)S(1)}, f32[192]{0:T(256)}, u32[]{:S(2)}) copy-start(f32[192]{0:T(256)} %param.16) | copy-start | bytes 2308
  64.5 2.3 %copy-start.7 = (f32[192]{0:T(256)S(1)}, f32[192]{0:T(256)}, u32[]{:S(2)}) copy-start(f32[192]{0:T(256)} %param.17) | copy-start | bytes 2308
  64.5 2.3 %copy-start.8 = (f32[192]{0:T(256)S(1)}, f32[192]{0:T(256)}, u32[]{:S(2)}) copy-start(f32[192]{0:T(256)} %param.19) | copy-start | bytes 2308
  66.8 1.0 %copy-start.10 = (bf16[4,4,64,192]{3,2,1,0:T(8,128)(2,1)S(1)}, bf16[4,4,64,192]{3,2,1,0:T(8,128)(2,1)}, u32[]{:S(2)}) copy-start(bf16[4,4,64,192]{3,2,1,0:T(8,128)(2,1)} %copy-done.9) | copy-start | bytes 1179652
  67.9 1.0 %copy-start.12 = (bf16[4,4,64,192]{3,2,1,0:T(8,128)(2,1)S(1)}, bf16[4,4,64,192]{3,2,1,0:T(8,128)(2,1)}, u32[]{:S(2)}) copy-start(bf16[4,4,64,192]{3,2,1,0:T(8,128)(2,1)} %copy-done.11) | copy-start | bytes 1179652

commit v2 on v0

v2 whole, which is shorter than its diff:
```python
import functools

import jax
import jax.numpy as jnp
from jax import lax
from jax.experimental import pallas as pl
from jax.experimental.pallas import tpu as pltpu
from jax.sharding import PartitionSpec as P

G = 32
EPS = 1e-06
LIMIT = 52 * 2**20
FOLD_FLOPS = 10**10
RIM_FLOPS = 10**10
TABLE_FLOPS = 2 * 10**10
F32 = jnp.float32
BF16 = jnp.bfloat16
VM = pl.BlockSpec(memory_space=pltpu.VMEM)
HB = pl.BlockSpec(memory_space=pltpu.HBM)


def dot01(a, b):
    high = a.astype(BF16).astype(F32)
    rest = a - high
    middle = rest.astype(BF16).astype(F32)
    parts = jnp.concatenate([high, middle, rest - middle], axis=0).astype(BF16)
    out = jnp.dot(parts, b, preferred_element_type=F32)
    return out[0:8] + out[8:16] + out[16:24]


def spread(chan):
    lane = lax.broadcasted_iota(jnp.int32, (128, chan), 0)
    col = lax.broadcasted_iota(jnp.int32, (128, chan), 1)
    low = (lane & (G - 1)) * (chan // G)
    return jnp.where((col >= low) & (col < low + chan // G), 1.0, 0.0).astype(BF16)


def gather_groups(chan):
    lane = lax.broadcasted_iota(jnp.int32, (chan, 128), 1)
    col = lax.broadcasted_iota(jnp.int32, (chan, 128), 0)
    low = (lane & (G - 1)) * (chan // G)
    return jnp.where((col >= low) & (col < low + chan // G), 1.0, 0.0).astype(BF16)


def frame_mask(first):
    lane = lax.broadcasted_iota(jnp.int32, (8, 128), 1)
    row = lax.broadcasted_iota(jnp.int32, (8, 128), 0)
    low = (row - first) * G
    return (lane >= low) & (lane < low + G)


def stack_rows(rows):
    width = rows[0].shape[1]
    index = lax.broadcasted_iota(jnp.int32, (8, width), 0)
    out = jnp.zeros((8, width), F32)
    for i, r in enumerate(rows):
        out = jnp.where(index == i, jnp.broadcast_to(r, (8, width)), out)
    return out


def channel_stats(v):
    mean = jnp.sum(v, axis=0, keepdims=True) / v.shape[0]
    off = v - mean
    return mean, jnp.sum(off * off, axis=0, keepdims=True)


def local_stats(stats, positions, stat_ref):
    chan = stats[0][0].shape[1]
    mask = frame_mask(0)
    to_group, to_chan = gather_groups(chan), spread(chan)
    means = stack_rows([m for m, _ in stats])
    squares = stack_rows([q for _, q in stats])
    mean = jnp.where(mask, dot01(means, to_group), 0.0) / (chan // G)
    off = means - dot01(mean, to_chan)
    square = jnp.where(mask, dot01(squares + positions * off * off, to_group), 0.0)
    packed = jnp.concatenate(
        [jnp.sum(mean, axis=0, keepdims=True), jnp.sum(square, axis=0, keepdims=True)], axis=0
    )
    stat_ref[...] = jnp.broadcast_to(packed[None], stat_ref.shape)


def table_kernel(count, stat_ref, gain_ref, mean_ref, scale_ref):
    gain = gain_ref[...]
    tiles = stat_ref.shape[0] // 2
    chan = mean_ref.shape[-1]
    to_chan = spread(chan)
    means, spreads = [], []
    for half in range(2):
        part = stat_ref[half * tiles : (half + 1) * tiles]
        total = jnp.sum(part, axis=0)
        mean = total[0:1] / tiles
        off = part - mean[None]
        spread_sum = total[1:2] + count * jnp.sum(off * off, axis=0)[0:1]
        means.append(mean)
        spreads.append(spread_sum / (tiles * count))
    m0, m1 = frame_mask(0), frame_mask(4)
    mean8 = jnp.where(m0, means[0], 0.0) + jnp.where(m1, means[1], 0.0)
    inv8 = jnp.where(m0, lax.rsqrt(spreads[0] + EPS), 0.0) + jnp.where(
        m1, lax.rsqrt(spreads[1] + EPS), 0.0
    )
    mean_chan = dot01(mean8, to_chan)
    scale = dot01(inv8, to_chan) * gain
    for f in range(8):
        mean_ref[f] = mean_chan[f : f + 1]
        scale_ref[f] = scale[f : f + 1]


def columns(shape, cols):
    return lax.broadcasted_iota(jnp.int32, shape, 0) & (cols - 1)


def from_left(v, cols):
    return jnp.where(columns(v.shape, cols) == 0, 0.0, pltpu.roll(v, 1, axis=0))


def from_right(v, cols):
    turned = pltpu.roll(v, v.shape[0] - 1, axis=0)
    return jnp.where(columns(v.shape, cols) == cols - 1, 0.0, turned)


def put_row(v, a_ref, b_ref, f, k):
    tail = v[:, 128:192].astype(BF16)
    a_ref[f, k] = v[:, 0:128].astype(BF16)
    b_ref[f, k, :, 0:64] = tail
    if k > 0:
        b_ref[f, k - 1, :, 64:128] = tail
    return tail


def silu(u):
    half = 0.5 * u
    return half + half * jnp.tanh(half)


def conv_rows(a_ref, b_ref, d_ref, w_ref, f, runs, cols):
    def take(ref, slot, r):
        parts = [ref[slot, k + r : k + r + n].reshape(n * cols, 128) for k, n in runs]
        return parts[0] if len(parts) == 1 else jnp.concatenate(parts, axis=0)

    parts = [take(a_ref, f + t, r) for t in range(3) for r in range(3)]
    parts += [take(b_ref, f + t, 0) for t in range(3)]
    parts += [take(d_ref, f, 2), take(b_ref, f + 2, 2)]
    maps = jnp.concatenate(parts, axis=1)

    def taps(k):
        low, high = slice(0, 128), slice(128, 192)
        at = lambda t, r: (t * 3 + r) * 3 + k
        rows = [w_ref[at(t, r), low] for t in range(3) for r in range(3)]
        for t in range(3):
            rows += [w_ref[at(t, 0), high], w_ref[at(t, 1), high]]
        rows += [w_ref[at(0, 2), high], w_ref[at(1, 2), high], w_ref[at(2, 2), high]]
        rows.append(jnp.zeros((64, w_ref.shape[-1]), BF16))
        return jnp.concatenate(rows, axis=0)

    left, centre, right = [
        jnp.dot(maps, taps(k), preferred_element_type=F32) for k in range(3)
    ]
    return centre + from_left(left, cols) + from_right(right, cols)


class Copies:
    def __init__(self, pairs, sems):
        self.pending = {}
        for i, (key, source, target) in enumerate(pairs):
            copy = pltpu.make_async_copy(source, target, sems.at[i])
            copy.start()
            self.pending[key] = copy

    def need(self, *keys):
        for key in keys:
            if key in self.pending:
                self.pending.pop(key).wait()


def pack_kernel(x_ref, even_ref, odd_ref, stat_ref):
    odd = lax.rem(lax.axis_index("tile"), 2)
    frames, rows, cols, chan = x_ref.shape
    even_ref[...] = x_ref[:, pl.ds(1 - odd, 3)]
    odd_ref[...] = x_ref[:, pl.ds(odd, 3)]
    stats = [
        channel_stats(x_ref[f].reshape(rows * cols, chan).astype(F32)) for f in range(frames)
    ]
    local_stats(stats, rows * cols, stat_ref)


def fold_kernel(x_ref, p1_ref, p2_ref, k_ref, wu_ref, c_ref):
    frames, rows = x_ref.shape[:2]
    c_ref[:, 0:3] = p1_ref[frames - 2 :]
    c_ref[:, 3 : 3 + rows] = x_ref[frames - 2 :]
    c_ref[:, 3 + rows :] = p2_ref[frames - 2 :]
    k = [[k_ref[3 * j + i].astype(F32) for i in range(3)] for j in range(3)]
    plus = lambda p, q: [a + b for a, b in zip(p, q)]
    for s, taps in enumerate(((k[0], plus(k[1], k[2])), (plus(k[0], k[1]), k[2]))):
        for i, c in enumerate(taps):
            sides = jnp.concatenate([c[0], c[2]], axis=1).astype(BF16)
            centre = jnp.concatenate([c[1] + c[2], c[0] + c[1]], axis=1).astype(BF16)
            for j, v in enumerate((sides, centre)):
                wu_ref[s, j, 128 * i : 128 * i + 128] = v[:128]
                wu_ref[s, j, 256 + 64 * i : 320 + 64 * i] = v[128:]


def conv_one_kernel(ring, row_list, x_hbm, p1_hbm, p2_hbm, c_hbm, w_hbm, vec_ref, mean_ref, scale_ref, *rest):
    if ring:
        out_ref, stat_ref = rest[:2]
    else:
        h_hbm, out_ref, cache_ref = rest[:3]
    x_ref, p1_ref, p2_ref, c_ref, w_ref, a_ref, b_ref, d_ref, sems = rest[-9:]
    frames, rows, cols, chan = x_ref.shape
    pairs = [
        ("c", c_hbm, c_ref),
        ("x", x_hbm, x_ref),
        ("p1", p1_hbm, p1_ref),
        ("p2", p2_hbm, p2_ref),
        ("w", w_hbm, w_ref),
    ]
    if not ring:
        pairs.append(("h", h_hbm.at[pl.ds(frames - 2, 2)], cache_ref.at[:, pl.ds(2, rows)]))
    copies = Copies(pairs, sems)
    tm, tile = lax.axis_index("tm"), lax.axis_index("tile")
    last = lax.axis_size("tile") - 1
    odd = lax.rem(tile, 2) == 1
    shift, bias = vec_ref[0:1], vec_ref[1:2]
    in_rows = a_ref.shape[1]
    b_ref[:, in_rows - 1] = jnp.zeros_like(b_ref[:, in_rows - 1])

    def fetch(slot, row):
        if slot < 2:
            if 3 <= row < 3 + rows:
                return c_ref[slot, row].astype(F32)
            other = row + 3 + rows if row < 3 else row - 3 - rows
            return jnp.where(odd, c_ref[slot, row].astype(F32), c_ref[slot, other].astype(F32))
        frame = slot - 2
        if 3 <= row < 3 + rows:
            return x_ref[frame, row - 3].astype(F32)
        k = row if row < 3 else row - 3 - rows
        p1, p2 = p1_ref[frame, k].astype(F32), p2_ref[frame, k].astype(F32)
        return jnp.where(odd == (row < 3), p1, p2)

    def norm_frame(slot):
        index = slot + frames - 2 if slot < 2 else tm * frames + slot - 2
        mean, scale = mean_ref[index], scale_ref[index]
        k = 0
        for first, n, _ in row_list:
            for row in range(first, first + n + 2):
                v = silu((fetch(slot, row) - mean) * scale + shift)
                keep = None
                if row < 3:
                    keep = tile > 0
                if row >= 3 + rows:
                    keep = tile < last
                if slot < 2:
                    keep = (tm > 0) if keep is None else keep & (tm > 0)
                if keep is not None:
                    v = jnp.where(keep, v, 0.0)
                put_both(put_row(v, a_ref, b_ref, slot, k), d_ref, slot, k)
                k += 1

    copies.need("c")
    norm_frame(0)
    norm_frame(1)
    copies.need("x", "p1", "p2")
    stats, runs, k = [], [], 0
    for _, n, _ in row_list:
        runs.append((k, n))
        k += n + 2
    for f in range(frames):
        norm_frame(f + 2)
        copies.need("w")
        out = (conv_rows(a_ref, b_ref, d_ref, w_ref, f, runs, cols) + bias).astype(BF16)
        rows_out = out.reshape(rows, cols, chan)
        k = 0
        for _, n, where_to in row_list:
            out_ref[f, where_to : where_to + n] = rows_out[k : k + n]
            if not ring and f >= frames - 2:
                at = where_to if where_to == 0 else where_to + rows
                cache_ref[f - frames + 2, at : at + n] = rows_out[k : k + n]
            k += n
        if ring:
            stats.append(channel_stats(out.astype(F32)))
    if ring:
        local_stats(stats, rows * cols, stat_ref)
    copies.need("h")


def put_both(tail, d_ref, slot, k):
    if slot < d_ref.shape[0]:
        d_ref[slot, k, :, 0:64] = tail
    if 0 < slot <= d_ref.shape[0]:
        d_ref[slot - 1, k, :, 64:128] = tail


def conv_two_kernel(
    x_hbm,
    p1_hbm,
    p2_hbm,
    h_hbm,
    hh_hbm,
    hc_hbm,
    w_hbm,
    wu_hbm,
    vec_ref,
    mean_ref,
    scale_ref,
    out_hbm,
    x_ref,
    p1_ref,
    p2_ref,
    h_ref,
    hh_ref,
    hc_ref,
    w_ref,
    wu_ref,
    out_ref,
    a_ref,
    b_ref,
    d_ref,
    aj_ref,
    bj_ref,
    sems,
    out_sems,
):
    frames, rows, cols, chan = x_ref.shape
    copies = Copies(
        [
                ("hc", hc_hbm, hc_ref),
            ("h", h_hbm, h_ref),
            ("hh", hh_hbm, hh_ref),
            ("w", w_hbm, w_ref),
            ("x", x_hbm, x_ref),
            ("p1", p1_hbm, p1_ref),
            ("p2", p2_hbm, p2_ref),
            ("wu", wu_hbm, wu_ref),
        ],
        sems,
    )
    tm, tile = lax.axis_index("tm"), lax.axis_index("tile")
    last = lax.axis_size("tile") - 1
    odd = lax.rem(tile, 2) == 1
    shift, bias, bias_up = vec_ref[2:3], vec_ref[3:4], vec_ref[4:5]
    in_rows = a_ref.shape[1]
    b_ref[:, in_rows - 1] = jnp.zeros_like(b_ref[:, in_rows - 1])

    def norm_frame(slot):
        index = slot + frames - 2 if slot < 2 else tm * frames + slot - 2
        mean, scale = mean_ref[index], scale_ref[index]
        for row in range(rows + 4):
            if slot < 2:
                v = hc_ref[slot, row]
            elif row < 2:
                v = hh_ref[slot - 2, row]
            elif row < rows + 2:
                v = h_ref[slot - 2, row - 2]
            else:
                v = hh_ref[slot - 2, row - rows]
            v = silu((v.astype(F32) - mean) * scale + shift)
            keep = None
            if row < 2:
                keep = tile > 0
            if row >= rows + 2:
                keep = tile < last
            if slot < 2:
                keep = (tm > 0) if keep is None else keep & (tm > 0)
            if keep is not None:
                v = jnp.where(keep, v, 0.0)
            put_both(put_row(v, a_ref, b_ref, slot, row), d_ref, slot, row)

    def joined_frame(f):
        copies.need("w")
        out = conv_rows(a_ref, b_ref, d_ref, w_ref, f, [(0, rows + 2)], cols) + bias
        copies.need("x", "p1", "p2")
        for r in range(rows + 2):
            if r == 0:
                x = jnp.where(odd, p1_ref[f, 2].astype(F32), p2_ref[f, 2].astype(F32))
            elif r <= rows:
                x = x_ref[f, r - 1].astype(F32)
            else:
                x = jnp.where(odd, p2_ref[f, 0].astype(F32), p1_ref[f, 0].astype(F32))
            v = out[r * cols : (r + 1) * cols] + x
            if r == 0:
                v = jnp.where(tile > 0, v, 0.0)
            if r > rows:
                v = jnp.where(tile < last, v, 0.0)
            put_row(v, aj_ref, bj_ref, f, r)

    def up_frame(f):
        copies.need("wu")
        m = rows * cols
        first = lax.broadcasted_iota(jnp.int32, (m, chan), 1) < chan // 2
        for s in range(2):
            parts = [aj_ref[f, s + i : s + i + rows].reshape(m, 128) for i in range(2)]
            parts.append(bj_ref[f, s : s + rows].reshape(m, 128))
            maps = jnp.concatenate(parts, axis=1)
            sides = jnp.dot(maps, wu_ref[s, 0], preferred_element_type=F32)
            up = jnp.dot(maps, wu_ref[s, 1], preferred_element_type=F32)
            up = up + jnp.where(first, from_left(sides, cols), from_right(sides, cols))
            up = (up + bias_up).astype(BF16).reshape(rows, cols, chan)
            for y in range(rows):
                out_ref[f, 2 * y + s] = up[y]

    copies.need("hc")
    norm_frame(0)
    norm_frame(1)
    copies.need("h", "hh")
    norm_frame(2)
    written = []
    for f in range(frames):
        joined_frame(f)
        if f + 3 < frames + 2:
            norm_frame(f + 3)
        up_frame(f)
        copy = pltpu.make_async_copy(out_ref.at[f], out_hbm.at[f], out_sems.at[f])
        copy.start()
        written.append(copy)
    for copy in written:
        copy.wait()


def exchange(stat):
    return lax.all_to_all(stat, ("tm", "tile"), 0, 0)


def body(
    features,
    gain_one,
    shift_one,
    kernel_one,
    bias_one,
    gain_two,
    shift_two,
    kernel_two,
    bias_two,
    up_kernel,
    up_bias,
):
    x = features[0]
    frames, rows, cols, chan = x.shape
    tiles = lax.axis_size("tile")
    even_pairs = [(i, i ^ 1) for i in range(tiles)]
    odd_pairs = [(i, i + 1) for i in range(1, tiles - 1, 2)]
    odd_pairs += [(b, a) for a, b in odd_pairs]
    down = [(0, 1)]
    shape = jax.ShapeDtypeStruct
    stat_shape = shape((2 * tiles, 2, 128), F32)
    small = pltpu.CompilerParams(vmem_limit_bytes=12 * 2**20)
    limit = pltpu.CompilerParams(vmem_limit_bytes=LIMIT)
    one_conv = 2 * frames * rows * cols * 27 * chan * chan
    cost = lambda flops, moved: pl.CostEstimate(
        flops=flops, bytes_accessed=moved, transcendentals=0
    )

    even, odd, stat = pl.pallas_call(
        pack_kernel,
        out_shape=(
            shape((frames, 3, cols, chan), BF16),
            shape((frames, 3, cols, chan), BF16),
            stat_shape,
        ),
        in_specs=[VM],
        out_specs=(VM, VM, VM),
        compiler_params=small,
        name="pack",
    )(x)
    p1 = lax.ppermute(even, "tile", even_pairs)
    p2 = lax.ppermute(odd, "tile", odd_pairs)
    all_one = exchange(stat)
    w_one = kernel_one.reshape(27, chan, chan)
    w_two = kernel_two.reshape(27, chan, chan)
    w_up, last_two = pl.pallas_call(
        fold_kernel,
        out_shape=(
            shape((2, 2, 2 * chan, chan), BF16),
            shape((2, rows + 6, cols, chan), BF16),
        ),
        in_specs=[VM] * 4,
        out_specs=(VM, VM),
        compiler_params=small,
        cost_estimate=cost(FOLD_FLOPS, 4 * 2**20),
        name="fold",
    )(x, p1, p2, up_kernel.reshape(9, chan, chan // 2))
    before = lax.ppermute(last_two, "tm", down)
    vectors = jnp.stack(
        [shift_one, bias_one, shift_two, bias_two, jnp.concatenate([up_bias, up_bias])]
    )

    def table(stats, gain):
        rows_of = shape((8, 1, chan), F32)
        return pl.pallas_call(
            functools.partial(table_kernel, rows * cols * (chan // G)),
            out_shape=(rows_of, rows_of),
            in_specs=[VM, VM],
            out_specs=(VM, VM),
            compiler_params=small,
            cost_estimate=cost(TABLE_FLOPS, 2**18),
            name="table",
        )(stats, gain.reshape(1, chan))

    def scratch(in_rows, out_frames):
        return [
            pltpu.VMEM((frames + 2, in_rows, cols, 128), BF16),
            pltpu.VMEM((frames + 2, in_rows, cols, 128), BF16),
            pltpu.VMEM((frames, in_rows, cols, 128), BF16),
        ]

    held = lambda v: pltpu.VMEM(v.shape, v.dtype)
    args = (x, p1, p2, before, w_one)
    table_one = table(all_one, gain_one)

    def conv_one(ring, row_list, *more):
        outs = (shape((frames, rows, cols, chan), BF16),)
        outs += (stat_shape,) if ring else (shape((2, rows + 4, cols, chan), BF16),)
        return pl.pallas_call(
            functools.partial(conv_one_kernel, ring, row_list),
            out_shape=outs,
            in_specs=[HB] * len(args) + [VM] * 3 + [HB] * len(more),
            out_specs=(VM,) * len(outs),
            scratch_shapes=[held(v) for v in args]
            + scratch(sum(n + 2 for _, n, _ in row_list), frames)
            + [pltpu.SemaphoreType.DMA((7,))],
            compiler_params=limit,
            cost_estimate=cost(one_conv if ring else RIM_FLOPS, 4 * 2**20),
            name="conv_one" if ring else "conv_one_rim",
        )(*args, vectors, *table_one, *more)

    hidden, stat_two = conv_one(True, ((2, rows, 0),))
    all_two = exchange(stat_two)
    rim, hidden_two = conv_one(False, ((0, 2, 0), (rows + 2, 2, 2)), hidden)
    hidden_before = lax.ppermute(hidden_two, "tm", down)
    args_two = (x, p1, p2, hidden, rim, hidden_before, w_two, w_up)
    out_shape = shape((frames, 2 * rows, cols, chan), BF16)
    out = pl.pallas_call(
        conv_two_kernel,
        out_shape=out_shape,
        in_specs=[HB] * len(args_two) + [VM] * 3,
        out_specs=HB,
        scratch_shapes=[held(v) for v in args_two]
        + [held(out_shape)]
        + scratch(rows + 4, frames)
        + [
            pltpu.VMEM((frames, rows + 2, cols, 128), BF16),
            pltpu.VMEM((frames, rows + 2, cols, 128), BF16),
            pltpu.SemaphoreType.DMA((9,)),
            pltpu.SemaphoreType.DMA((frames,)),
        ],
        compiler_params=limit,
        cost_estimate=cost(3 * one_conv, 4 * 2**20),
        name="conv_two",
    )(*args_two, vectors, *table(all_two, gain_two))
    return out[None]


def solution(mesh):
    return jax.shard_map(
        body,
        mesh=mesh,
        in_specs=(P(None, "tm", "tile", None, None),) + (P(),) * 10,
        out_specs=P(None, "tm", "tile", None, None),
        check_vma=False,
    )
```

time: 908 us -> 69.9 us (0.08); the launches traced: 895 us -> 69.4 us
  blocking collectives: 588 us -> 0 us
  waiting for transfers between devices: 122 us -> 6.19 us
  local copies, waits for them, and re-layouts: 102 us -> 8.03 us
  other arithmetic: 48.4 us -> 0.81 us
  Pallas kernels: 0 us -> 25.7 us
  matrix products: 21 us -> 0 us
  starting transfers between devices: 13.1 us -> 28.4 us
    psum x4 -> x0, blocking collectives: 588 us -> none  [the longest x2 298 us: group_act(): lax.psum(jnp.sum(grouped, axis=(2, 3, 5)), 'tile') / cell_count]
    ppermute x8 -> x4, waiting for transfers between devices: 122 us -> 0.01 us  [the longest x1 0.01 us: body(): hidden_before = lax.ppermute(hidden_two, 'tm', down)]
    concatenate x19 -> x1, other arithmetic: 36.3 us -> 0.81 us  [body(): jnp.concatenate([up_bias, up_bias])]
    concatenate x6 -> x0, local copies, waits for them, and re-layouts: 33.8 us -> none  [the longest x3 31.3 us: plane_taps(): jnp.concatenate([slab_part[:, :, :, col_tap:col_tap + out_cols] for col_t...]
    reshape x5 -> x0, local copies, waits for them, and re-layouts: 27.4 us -> none  [the longest x3 24.8 us: plane_taps(): stacked.reshape(-1, 3 * chan_count)]
    pallas_call x0 -> x7, Pallas kernels: none -> 25.7 us  [the longest x2 11.7 us: conv_one(): pl.pallas_call(functools.partial(conv_one_kernel, ring, row_list), out_sh...]
    slice x14 -> x0, local copies, waits for them, and re-layouts: 24.7 us -> none  [the longest x6 10.9 us: causal_taps(): slab_part[:, :, :, col_tap:col_tap + col_count]]
    all_to_all x0 -> x2, starting transfers between devices: none -> 22.9 us  [exchange(): return lax.all_to_all(stat, ('tm', 'tile'), 0, 0)]
  transfers between devices with their start and end apart: 8 -> 6, of which waited for: 8 -> 2; matrix products, arithmetic and copies ran while one was open for 1% -> 2% of each run, Pallas kernels for 0% -> 9%
where the time goes in v2:
time: 69.9 us; the launch traced here: 69.4 us
  starting transfers between devices  28.4 us (41%)
  Pallas kernels  25.7 us (37%)
  local copies, waits for them, and re-layouts  8.03 us (11%)
  waiting for transfers between devices  6.19 us (9%)
  other arithmetic  0.81 us (1%)
    all_to_all x2, starting transfers between devices, exchange(): return lax.all_to_all(stat, ('tm', 'tile'), 0, 0)  22.9 us
    pallas_call x2, Pallas kernels, conv_one(): pl.pallas_call(functools.partial(conv_one_kernel, ring, row_list), out_sh...  11.7 us
    pallas_call x1, Pallas kernels, body(): pl.pallas_call(conv_two_kernel, out_shape=out_shape, in_specs=[HB] * len(...  11.7 us
    unnamed x26, local copies, waits for them, and re-layouts  7.28 us
    all_to_all x2, waiting for transfers between devices, exchange(): return lax.all_to_all(stat, ('tm', 'tile'), 0, 0)  6.18 us
    ppermute x1, starting transfers between devices, body(): p1 = lax.ppermute(even, 'tile', even_pairs)  2.04 us
    ppermute x1, starting transfers between devices, body(): hidden_before = lax.ppermute(hidden_two, 'tm', down)  1.46 us
  transfers between devices with their start and end apart: 6, of which 2 were waited for; matrix products, arithmetic and copies ran while one was open for 2% of the time, Pallas kernels for 9%

profile of v2, /device:TPU:1, one launch (start us, length us, event | category | flops | bytes accessed | tf_op | source)
XLA Modules:
  0.0 69.4 jit_solution(2354995479215873920)
XLA Ops:
  0.0 1.0 %copy-done = bf16[1,4,4,64,192]{4,3,2,1,0:T(8,128)(2,1)S(1)} copy-done((bf16[1,4,4,64,192]{4,3,2,1,0:T(8,128)(2,1)S(1)}, bf16[1,4,4,64,192]{4,3,2,1,0:T(8,128)(2,1)}, u32[]{:S(2)}) %copy-start) | copy-done | bytes 393240
  1.0 1.4 %pack.1 = (bf16[4,3,64,192]{3,2,1,0:T(8,128)(2,1)S(1)}, bf16[4,3,64,192]{3,2,1,0:T(8,128)(2,1)S(1)}, f32[128,2,128]{2,1,0:T(2,128)}) custom-call(bf16[4,4,64,192]{3,2,1,0:T(8,128)(2,1)S(1)} %bitcast.13), custom_call_target="tpu_custom_call" | custom-call | tf_op jit(solution)/shard_map/pack/pallas_call | solution.py:451
  2.4 2.0 %collective-permute-start = (bf16[4,3,64,192]{3,2,1,0:T(8,128)(2,1)S(1)}, bf16[4,3,64,192]{3,2,1,0:T(8,128)(2,1)S(1)}, u32[]{:S(2)}, u32[]{:S(2)}) collective-permute-start(bf16[4,3,64,192]{3,2,1,0:T(8,128)(2,1)S(1)} %get-tuple-element.18), channel_id=1, source_target_pairs={{0,1},{1,0},{2,3},{3,2},{4,5},{5,4},{6,7},{7,6},{8,9},{9,8},{10,11... | collective-permute-start | bytes 884744 | tf_op jit(solution)/shard_map/ppermute | solution.py:463
  4.4 0.7 collective-permute-start.1
  5.1 13.1 %all-to-all-start = ((f32[128,2,128]{2,1,0:T(2,128)}), f32[128,2,128]{2,1,0:T(2,128)S(1)}, u32[]{:S(2)}, u32[]{:S(2)}) async-start(f32[128,2,128]{2,1,0:T(2,128)} %get-tuple-element.21), calls=%async_computation | async-start | bytes 262144 | tf_op jit(solution)/shard_map/all_to_all | solution.py:419
  18.2 0.8 %pad_maximum_fusion = f32[192]{0:T(256)S(1)} fusion(f32[96]{0:T(128)} %param.21), kind=kLoop, calls=%fused_computation | loop fusion | flops 192 | bytes 1152 | tf_op jit(solution)/shard_map/concatenate | solution.py:482
  19.0 0.7 %stack.23.vec_ref = f32[5,192]{1,0:T(8,128)S(1)} concatenate(f32[1,192]{1,0:T(1,128)} %bitcast.20, f32[1,192]{1,0:T(1,128)} %bitcast.21, f32[1,192]{1,0:T(1,128)} %bitcast.22, f32[1,192]{1,0:T(1,128)} %bitcast.23, f32[1,192]{1,0:T(1,128)S(1)} %bitcast.24), dimensions={0} | concatenate | bytes 7680 | tf_op jit(solution)/shard_map/stack | solution.py:481
  19.8 0.0 collective-permute-done.1.p2_ref.p2_hbm
  19.8 0.0 copy-start.1
  19.8 1.0 %copy-done.1 = bf16[1,4,4,64,192]{4,3,2,1,0:T(8,128)(2,1)S(1)} copy-done((bf16[1,4,4,64,192]{4,3,2,1,0:T(8,128)(2,1)S(1)}, bf16[1,4,4,64,192]{4,3,2,1,0:T(8,128)(2,1)}, u32[]{:S(2)}) %copy-start.1) | copy-done | bytes 393240
  20.9 1.0 %copy-done.4 = bf16[3,3,192,96]{3,2,1,0:T(8,128)(2,1)S(1)} copy-done((bf16[3,3,192,96]{3,2,1,0:T(8,128)(2,1)S(1)}, bf16[3,3,192,96]{3,2,1,0:T(8,128)(2,1)}, u32[]{:S(2)}) %copy-start.4) | copy-done | bytes 331800
  21.9 0.2 fold.1
  22.1 0.9 %copy-done.9 = bf16[2,2,384,192]{3,2,1,0:T(8,128)(2,1)} copy-done((bf16[2,2,384,192]{3,2,1,0:T(8,128)(2,1)}, bf16[2,2,384,192]{3,2,1,0:T(8,128)(2,1)S(1)}, u32[]{:S(2)}) %copy-start.9) | copy-done | bytes 589848
  23.0 1.3 %collective-permute-start.2 = (bf16[2,10,64,192]{3,2,1,0:T(8,128)(2,1)S(1)}, bf16[2,10,64,192]{3,2,1,0:T(8,128)(2,1)S(1)}, u32[]{:S(2)}, u32[]{:S(2)}) collective-permute-start(bf16[2,10,64,192]{3,2,1,0:T(8,128)(2,1)S(1)} %get-tuple-element.20), channel_id=1, source_target_pairs={{0,64},{1,65},{2,66},{3,67},{4,68},{5,69},{6,70},{7,71},{8,72},{9,... | collective-permute-start | bytes 1474568 | tf_op jit(solution)/shard_map/ppermute | solution.py:480
  24.3 3.9 %all-to-all-done.stat_ref = f32[128,2,128]{2,1,0:T(2,128)S(1)} async-done(((f32[128,2,128]{2,1,0:T(2,128)}), f32[128,2,128]{2,1,0:T(2,128)S(1)}, u32[]{:S(2)}, u32[]{:S(2)}) %all-to-all-start) | async-done | bytes 131104 | tf_op jit(solution)/shard_map/all_to_all | solution.py:419
  28.2 0.3 table.2
  28.5 0.0 collective-permute-done.2.c_hbm
  28.5 0.0 copy-start.11
  28.5 0.8 %copy-done.11 = bf16[2,10,64,192]{3,2,1,0:T(8,128)(2,1)} copy-done((bf16[2,10,64,192]{3,2,1,0:T(8,128)(2,1)}, bf16[2,10,64,192]{3,2,1,0:T(8,128)(2,1)S(1)}, u32[]{:S(2)}) %copy-start.11) | copy-done | bytes 491544
  29.4 6.4 %conv_one.1 = (bf16[4,4,64,192]{3,2,1,0:T(8,128)(2,1)S(1)}, f32[128,2,128]{2,1,0:T(2,128)}) custom-call(bf16[4,4,64,192]{3,2,1,0:T(8,128)(2,1)S(1)} %bitcast.15, bf16[4,3,64,192]{3,2,1,0:T(8,128)(2,1)S(1)} %collective-permute-done.p1_ref.p1_hbm, bf16[4,3,64,192]{3,2,1,0:T(8,128)(2,1)S(1)} %collective-permute-done.1.p2_ref.p2_hbm, ...), custom_call_target="tpu_custom_call" | custom-call | flops 2038431744 | bytes 4194304 | tf_op jit(solution)/shard_map/conv_one/pallas_call | solution.py:511
  35.8 0.8 %copy-done.7 = bf16[4,4,64,192]{3,2,1,0:T(8,128)(2,1)} copy-done((bf16[4,4,64,192]{3,2,1,0:T(8,128)(2,1)}, bf16[4,4,64,192]{3,2,1,0:T(8,128)(2,1)S(1)}, u32[]{:S(2)}) %copy-start.7) | copy-done | bytes 393240
  36.6 9.8 %all-to-all-start.1 = ((f32[128,2,128]{2,1,0:T(2,128)}), f32[128,2,128]{2,1,0:T(2,128)S(1)}, u32[]{:S(2)}, u32[]{:S(2)}) async-start(f32[128,2,128]{2,1,0:T(2,128)} %get-tuple-element.28), calls=%async_computation.1 | async-start | bytes 262144 | tf_op jit(solution)/shard_map/all_to_all | solution.py:419
  46.4 0.0 copy-start.6
  46.4 5.3 %conv_one_rim.1 = (bf16[4,4,64,192]{3,2,1,0:T(8,128)(2,1)S(1)}, bf16[2,8,64,192]{3,2,1,0:T(8,128)(2,1)S(1)}) custom-call(bf16[4,4,64,192]{3,2,1,0:T(8,128)(2,1)} %bitcast.12, bf16[4,3,64,192]{3,2,1,0:T(8,128)(2,1)S(1)} %collective-permute-done.p1_ref.p1_hbm, bf16[4,3,64,192]{3,2,1,0:T(8,128)(2,1)S(1)} %collective-permute-done.1.p2_ref.p2_hbm, ...), custom_call_target="tpu_custom_call" | custom-call | flops 10000000000 | bytes 4194304 | tf_op jit(solution)/shard_map/conv_one_rim/pallas_call | solution.py:511
  51.8 0.8 %copy-done.10 = bf16[4,4,64,192]{3,2,1,0:T(8,128)(2,1)} copy-done((bf16[4,4,64,192]{3,2,1,0:T(8,128)(2,1)}, bf16[4,4,64,192]{3,2,1,0:T(8,128)(2,1)S(1)}, u32[]{:S(2)}) %copy-start.10) | copy-done | bytes 393240
  52.6 1.5 %collective-permute-start.3 = (bf16[2,8,64,192]{3,2,1,0:T(8,128)(2,1)S(1)}, bf16[2,8,64,192]{3,2,1,0:T(8,128)(2,1)S(1)}, u32[]{:S(2)}, u32[]{:S(2)}) collective-permute-start(bf16[2,8,64,192]{3,2,1,0:T(8,128)(2,1)S(1)} %get-tuple-element.26), channel_id=1, source_target_pairs={{0,64},{1,65},{2,66},{3,67},{4,68},{5,69},{6,70},{7,71},{8,72},{9,... | collective-permute-start | bytes 1179656 | tf_op jit(solution)/shard_map/ppermute | solution.py:527
  54.0 2.3 %all-to-all-done.1.stat_ref = f32[128,2,128]{2,1,0:T(2,128)S(1)} async-done(((f32[128,2,128]{2,1,0:T(2,128)}), f32[128,2,128]{2,1,0:T(2,128)S(1)}, u32[]{:S(2)}, u32[]{:S(2)}) %all-to-all-start.1) | async-done | bytes 131104 | tf_op jit(solution)/shard_map/all_to_all | solution.py:419
  56.3 0.3 table.3
  56.7 0.0 collective-permute-done.3.hc_hbm
  56.7 0.8 %copy-done.12 = bf16[2,8,64,192]{3,2,1,0:T(8,128)(2,1)} copy-done((bf16[2,8,64,192]{3,2,1,0:T(8,128)(2,1)}, bf16[2,8,64,192]{3,2,1,0:T(8,128)(2,1)S(1)}, u32[]{:S(2)}) %copy-start.12) | copy-done | bytes 393240
  57.5 0.0 copy-done.8
  57.5 11.7 %conv_two.1 = bf16[4,8,64,192]{3,2,1,0:T(8,128)(2,1)} custom-call(bf16[4,4,64,192]{3,2,1,0:T(8,128)(2,1)S(1)} %bitcast.16, bf16[4,3,64,192]{3,2,1,0:T(8,128)(2,1)S(1)} %collective-permute-done.p1_ref.p1_hbm, bf16[4,3,64,192]{3,2,1,0:T(8,128)(2,1)S(1)} %collective-permute-done.1.p2_ref.p2_hbm, bf16[4,4,64,192]{3,2,1,0:T(8,128)(2,1)S(1)} %copy-done.8, ...), custom_call_target="tpu_custom_call" | custom-call | flops 6115295232 | bytes 4194304 | tf_op jit(solution)/shard_map/conv_two/pallas_call | solution.py:530
  (15 shorter events, 0.0 us)
Async XLA Ops:
  0.0 1.0 %copy-start = (bf16[1,4,4,64,192]{4,3,2,1,0:T(8,128)(2,1)S(1)}, bf16[1,4,4,64,192]{4,3,2,1,0:T(8,128)(2,1)}, u32[]{:S(2)}) copy-start(bf16[1,4,4,64,192]{4,3,2,1,0:T(8,128)(2,1)} %param.11) | copy-start | bytes 1179652
  2.4 17.4 %collective-permute-start = (bf16[4,3,64,192]{3,2,1,0:T(8,128)(2,1)S(1)}, bf16[4,3,64,192]{3,2,1,0:T(8,128)(2,1)S(1)}, u32[]{:S(2)}, u32[]{:S(2)}) collective-permute-start(bf16[4,3,64,192]{3,2,1,0:T(8,128)(2,1)S(1)} %get-tuple-element.18), channel_id=1, source_target_pairs={{0,1},{1,0},{2,3},{3,2},{4,5},{5,4},{6,7},{7,6},{8,9},{9,8},{10,11... | collective-permute-start | bytes 884744 | tf_op jit(solution)/shard_map/ppermute | solution.py:463
  4.4 15.4 %collective-permute-start.1 = (bf16[4,3,64,192]{3,2,1,0:T(8,128)(2,1)S(1)}, bf16[4,3,64,192]{3,2,1,0:T(8,128)(2,1)S(1)}, u32[]{:S(2)}, u32[]{:S(2)}) collective-permute-start(bf16[4,3,64,192]{3,2,1,0:T(8,128)(2,1)S(1)} %get-tuple-element.19), channel_id=1, source_target_pairs={{1,2},{3,4},{5,6},{7,8},{9,10},{11,12},{13,14},{15,16},{17,18},{19... | collective-permute-start | bytes 884744 | tf_op jit(solution)/shard_map/ppermute | solution.py:464
  5.1 23.0 %all-to-all-start = ((f32[128,2,128]{2,1,0:T(2,128)}), f32[128,2,128]{2,1,0:T(2,128)S(1)}, u32[]{:S(2)}, u32[]{:S(2)}) async-start(f32[128,2,128]{2,1,0:T(2,128)} %get-tuple-element.21), calls=%async_computation | async-start | bytes 262144 | tf_op jit(solution)/shard_map/all_to_all | solution.py:419
  19.8 1.0 %copy-start.1 = (bf16[1,4,4,64,192]{4,3,2,1,0:T(8,128)(2,1)S(1)}, bf16[1,4,4,64,192]{4,3,2,1,0:T(8,128)(2,1)}, u32[]{:S(2)}) copy-start(bf16[1,4,4,64,192]{4,3,2,1,0:T(8,128)(2,1)} %param.11) | copy-start | bytes 1179652
  20.9 1.0 %copy-start.4 = (bf16[3,3,192,96]{3,2,1,0:T(8,128)(2,1)S(1)}, bf16[3,3,192,96]{3,2,1,0:T(8,128)(2,1)}, u32[]{:S(2)}) copy-start(bf16[3,3,192,96]{3,2,1,0:T(8,128)(2,1)} %param.20) | copy-start | bytes 995332
  21.9 6.3 %copy-start.5 = (f32[192]{0:T(256)S(1)}, f32[192]{0:T(256)}, u32[]{:S(2)}) copy-start(f32[192]{0:T(256)} %param.12) | copy-start | bytes 2308
  22.1 0.9 %copy-start.9 = (bf16[2,2,384,192]{3,2,1,0:T(8,128)(2,1)}, bf16[2,2,384,192]{3,2,1,0:T(8,128)(2,1)S(1)}, u32[]{:S(2)}) copy-start(bf16[2,2,384,192]{3,2,1,0:T(8,128)(2,1)S(1)} %get-tuple-element.27.wu_hbm) | copy-start | bytes 1769476
  23.0 5.5 %collective-permute-start.2 = (bf16[2,10,64,192]{3,2,1,0:T(8,128)(2,1)S(1)}, bf16[2,10,64,192]{3,2,1,0:T(8,128)(2,1)S(1)}, u32[]{:S(2)}, u32[]{:S(2)}) collective-permute-start(bf16[2,10,64,192]{3,2,1,0:T(8,128)(2,1)S(1)} %get-tuple-element.20), channel_id=1, source_target_pairs={{0,64},{1,65},{2,66},{3,67},{4,68},{5,69},{6,70},{7,71},{8,72},{9,... | collective-permute-start | bytes 1474568 | tf_op jit(solution)/shard_map/ppermute | solution.py:480
  28.2 1.2 %copy-start.2 = (bf16[1,4,4,64,192]{4,3,2,1,0:T(8,128)(2,1)S(1)}, bf16[1,4,4,64,192]{4,3,2,1,0:T(8,128)(2,1)}, u32[]{:S(2)}) copy-start(bf16[1,4,4,64,192]{4,3,2,1,0:T(8,128)(2,1)} %param.11) | copy-start | bytes 1179652
  28.5 0.8 %copy-start.11 = (bf16[2,10,64,192]{3,2,1,0:T(8,128)(2,1)}, bf16[2,10,64,192]{3,2,1,0:T(8,128)(2,1)S(1)}, u32[]{:S(2)}) copy-start(bf16[2,10,64,192]{3,2,1,0:T(8,128)(2,1)S(1)} %collective-permute-done.2.c_hbm) | copy-start | bytes 1474564
  35.8 0.8 %copy-start.7 = (bf16[4,4,64,192]{3,2,1,0:T(8,128)(2,1)}, bf16[4,4,64,192]{3,2,1,0:T(8,128)(2,1)S(1)}, u32[]{:S(2)}) copy-start(bf16[4,4,64,192]{3,2,1,0:T(8,128)(2,1)S(1)} %get-tuple-element.24.rest_0_.h_hbm) | copy-start | bytes 1179652
  36.6 19.7 %all-to-all-start.1 = ((f32[128,2,128]{2,1,0:T(2,128)}), f32[128,2,128]{2,1,0:T(2,128)S(1)}, u32[]{:S(2)}, u32[]{:S(2)}) async-start(f32[128,2,128]{2,1,0:T(2,128)} %get-tuple-element.28), calls=%async_computation.1 | async-start | bytes 262144 | tf_op jit(solution)/shard_map/all_to_all | solution.py:419
  46.4 9.9 %copy-start.6 = (f32[192]{0:T(256)S(1)}, f32[192]{0:T(256)}, u32[]{:S(2)}) copy-start(f32[192]{0:T(256)} %param.16) | copy-start | bytes 2308
  51.7 0.8 %copy-start.10 = (bf16[4,4,64,192]{3,2,1,0:T(8,128)(2,1)}, bf16[4,4,64,192]{3,2,1,0:T(8,128)(2,1)S(1)}, u32[]{:S(2)}) copy-start(bf16[4,4,64,192]{3,2,1,0:T(8,128)(2,1)S(1)} %get-tuple-element.25.hh_hbm) | copy-start | bytes 1179652
  52.6 4.1 %collective-permute-start.3 = (bf16[2,8,64,192]{3,2,1,0:T(8,128)(2,1)S(1)}, bf16[2,8,64,192]{3,2,1,0:T(8,128)(2,1)S(1)}, u32[]{:S(2)}, u32[]{:S(2)}) collective-permute-start(bf16[2,8,64,192]{3,2,1,0:T(8,128)(2,1)S(1)} %get-tuple-element.26), channel_id=1, source_target_pairs={{0,64},{1,65},{2,66},{3,67},{4,68},{5,69},{6,70},{7,71},{8,72},{9,... | collective-permute-start | bytes 1179656 | tf_op jit(solution)/shard_map/ppermute | solution.py:527
  56.3 1.2 %copy-start.3 = (bf16[1,4,4,64,192]{4,3,2,1,0:T(8,128)(2,1)S(1)}, bf16[1,4,4,64,192]{4,3,2,1,0:T(8,128)(2,1)}, u32[]{:S(2)}) copy-start(bf16[1,4,4,64,192]{4,3,2,1,0:T(8,128)(2,1)} %param.11) | copy-start | bytes 1179652
  56.3 1.2 %copy-start.8 = (bf16[4,4,64,192]{3,2,1,0:T(8,128)(2,1)S(1)}, bf16[4,4,64,192]{3,2,1,0:T(8,128)(2,1)}, u32[]{:S(2)}) copy-start(bf16[4,4,64,192]{3,2,1,0:T(8,128)(2,1)} %copy-done.7) | copy-start | bytes 1179652
  56.7 0.8 %copy-start.12 = (bf16[2,8,64,192]{3,2,1,0:T(8,128)(2,1)}, bf16[2,8,64,192]{3,2,1,0:T(8,128)(2,1)S(1)}, u32[]{:S(2)}) copy-start(bf16[2,8,64,192]{3,2,1,0:T(8,128)(2,1)S(1)} %collective-permute-done.3.hc_hbm) | copy-start | bytes 1179652

commit v3 on v2

--- a/solution.py
+++ b/solution.py
@@ -9,10 +9,10 @@
 
 G = 32
 EPS = 1e-06
-LIMIT = 52 * 2**20
-FOLD_FLOPS = 10**10
-RIM_FLOPS = 10**10
-TABLE_FLOPS = 2 * 10**10
+LIMIT = 24 * 2**20
+FILL_FLOPS = 15 * 10**9
+RIM_FLOPS = 4 * 10**9
+TABLE_FLOPS = 1500000000
 F32 = jnp.float32
 BF16 = jnp.bfloat16
 VM = pl.BlockSpec(memory_space=pltpu.VMEM)
@@ -132,14 +132,14 @@
     return half + half * jnp.tanh(half)
 
 
-def conv_rows(a_ref, b_ref, d_ref, w_ref, f, runs, cols):
-    def take(ref, slot, r):
-        parts = [ref[slot, k + r : k + r + n].reshape(n * cols, 128) for k, n in runs]
+def conv_rows(a_ref, b_ref, d_ref, w_ref, runs, cols):
+    def take(ref, t, r):
+        parts = [ref[f + t, k + r : k + r + n].reshape(n * cols, 128) for f, k, n in runs]
         return parts[0] if len(parts) == 1 else jnp.concatenate(parts, axis=0)
 
-    parts = [take(a_ref, f + t, r) for t in range(3) for r in range(3)]
-    parts += [take(b_ref, f + t, 0) for t in range(3)]
-    parts += [take(d_ref, f, 2), take(b_ref, f + 2, 2)]
+    parts = [take(a_ref, t, r) for t in range(3) for r in range(3)]
+    parts += [take(b_ref, t, 0) for t in range(3)]
+    parts += [take(d_ref, 0, 2), take(b_ref, 2, 2)]
     maps = jnp.concatenate(parts, axis=1)
 
     def taps(k):
@@ -158,20 +158,6 @@
     return centre + from_left(left, cols) + from_right(right, cols)
 
 
-class Copies:
-    def __init__(self, pairs, sems):
-        self.pending = {}
-        for i, (key, source, target) in enumerate(pairs):
-            copy = pltpu.make_async_copy(source, target, sems.at[i])
-            copy.start()
-            self.pending[key] = copy
-
-    def need(self, *keys):
-        for key in keys:
-            if key in self.pending:
-                self.pending.pop(key).wait()
-
-
 def pack_kernel(x_ref, even_ref, odd_ref, stat_ref):
     odd = lax.rem(lax.axis_index("tile"), 2)
     frames, rows, cols, chan = x_ref.shape
@@ -183,11 +169,26 @@
     local_stats(stats, rows * cols, stat_ref)
 
 
-def fold_kernel(x_ref, p1_ref, p2_ref, k_ref, wu_ref, c_ref):
+def assemble_kernel(x_ref, p1_ref, p2_ref, own_ref, c_ref):
     frames, rows = x_ref.shape[:2]
-    c_ref[:, 0:3] = p1_ref[frames - 2 :]
-    c_ref[:, 3 : 3 + rows] = x_ref[frames - 2 :]
-    c_ref[:, 3 + rows :] = p2_ref[frames - 2 :]
+    odd = lax.rem(lax.axis_index("tile"), 2) == 1
+    for f in range(frames):
+        for r in range(3):
+            p1, p2 = p1_ref[f, r].astype(F32), p2_ref[f, r].astype(F32)
+            own_ref[f, r] = jnp.where(odd, p1, p2).astype(BF16)
+            own_ref[f, 3 + rows + r] = jnp.where(odd, p2, p1).astype(BF16)
+    own_ref[:, 3 : 3 + rows] = x_ref[...]
+    c_ref[...] = own_ref[frames - 2 :]
+
+
+def vectors_kernel(*refs):
+    for i, ref in enumerate(refs[:-1]):
+        refs[-1][i : i + 1, 0 : ref.shape[1]] = ref[...]
+    half = refs[-2].shape[1]
+    refs[-1][len(refs) - 2 : len(refs) - 1, half : 2 * half] = refs[-2][...]
+
+
+def fold_kernel(k_ref, after_hbm, wu_ref):
     k = [[k_ref[3 * j + i].astype(F32) for i in range(3)] for j in range(3)]
     plus = lambda p, q: [a + b for a, b in zip(p, q)]
     for s, taps in enumerate(((k[0], plus(k[1], k[2])), (plus(k[0], k[1]), k[2]))):
@@ -199,42 +200,29 @@
                 wu_ref[s, j, 256 + 64 * i : 320 + 64 * i] = v[128:]
 
 
-def conv_one_kernel(ring, row_list, x_hbm, p1_hbm, p2_hbm, c_hbm, w_hbm, vec_ref, mean_ref, scale_ref, *rest):
+def conv_one_kernel(
+    ring, row_list, own_ref, c_ref, w_ref, vec_ref, mean_ref, scale_ref, *rest
+):
     if ring:
-        out_ref, stat_ref = rest[:2]
+        out_ref, stat_ref, a_ref, b_ref, d_ref = rest
     else:
-        h_hbm, out_ref, cache_ref = rest[:3]
-    x_ref, p1_ref, p2_ref, c_ref, w_ref, a_ref, b_ref, d_ref, sems = rest[-9:]
-    frames, rows, cols, chan = x_ref.shape
-    pairs = [
-        ("c", c_hbm, c_ref),
-        ("x", x_hbm, x_ref),
-        ("p1", p1_hbm, p1_ref),
-        ("p2", p2_hbm, p2_ref),
-        ("w", w_hbm, w_ref),
-    ]
+        h_hbm, out_ref, cache_ref, a_ref, b_ref, d_ref, sem = rest
+    frames, rows, cols, chan = own_ref.shape
+    rows -= 6
     if not ring:
-        pairs.append(("h", h_hbm.at[pl.ds(frames - 2, 2)], cache_ref.at[:, pl.ds(2, rows)]))
-    copies = Copies(pairs, sems)
+        load_h = pltpu.make_async_copy(
+            h_hbm.at[pl.ds(frames - 2, 2)], cache_ref.at[:, pl.ds(2, rows)], sem
+        )
+        load_h.start()
     tm, tile = lax.axis_index("tm"), lax.axis_index("tile")
     last = lax.axis_size("tile") - 1
-    odd = lax.rem(tile, 2) == 1
     shift, bias = vec_ref[0:1], vec_ref[1:2]
     in_rows = a_ref.shape[1]
     b_ref[:, in_rows - 1] = jnp.zeros_like(b_ref[:, in_rows - 1])
 
     def fetch(slot, row):
-        if slot < 2:
-            if 3 <= row < 3 + rows:
-                return c_ref[slot, row].astype(F32)
-            other = row + 3 + rows if row < 3 else row - 3 - rows
-            return jnp.where(odd, c_ref[slot, row].astype(F32), c_ref[slot, other].astype(F32))
-        frame = slot - 2
-        if 3 <= row < 3 + rows:
-            return x_ref[frame, row - 3].astype(F32)
-        k = row if row < 3 else row - 3 - rows
-        p1, p2 = p1_ref[frame, k].astype(F32), p2_ref[frame, k].astype(F32)
-        return jnp.where(odd == (row < 3), p1, p2)
+        v = c_ref[slot, row] if slot < 2 else own_ref[slot - 2, row]
+        return v.astype(F32)
 
     def norm_frame(slot):
         index = slot + frames - 2 if slot < 2 else tm * frames + slot - 2
@@ -255,18 +243,16 @@
                 put_both(put_row(v, a_ref, b_ref, slot, k), d_ref, slot, k)
                 k += 1
 
-    copies.need("c")
     norm_frame(0)
     norm_frame(1)
-    copies.need("x", "p1", "p2")
     stats, runs, k = [], [], 0
     for _, n, _ in row_list:
         runs.append((k, n))
         k += n + 2
     for f in range(frames):
         norm_frame(f + 2)
-        copies.need("w")
-        out = (conv_rows(a_ref, b_ref, d_ref, w_ref, f, runs, cols) + bias).astype(BF16)
+        here = [(f, first, n) for first, n in runs]
+        out = (conv_rows(a_ref, b_ref, d_ref, w_ref, here, cols) + bias).astype(BF16)
         rows_out = out.reshape(rows, cols, chan)
         k = 0
         for _, n, where_to in row_list:
@@ -279,7 +265,8 @@
             stats.append(channel_stats(out.astype(F32)))
     if ring:
         local_stats(stats, rows * cols, stat_ref)
-    copies.need("h")
+    else:
+        load_h.wait()
 
 
 def put_both(tail, d_ref, slot, k):
@@ -290,52 +277,27 @@
 
 
 def conv_two_kernel(
-    x_hbm,
-    p1_hbm,
-    p2_hbm,
-    h_hbm,
-    hh_hbm,
-    hc_hbm,
-    w_hbm,
-    wu_hbm,
-    vec_ref,
-    mean_ref,
-    scale_ref,
-    out_hbm,
-    x_ref,
-    p1_ref,
-    p2_ref,
+    own_ref,
     h_ref,
     hh_ref,
     hc_ref,
     w_ref,
     wu_ref,
+    vec_ref,
+    mean_ref,
+    scale_ref,
+    out_hbm,
     out_ref,
     a_ref,
     b_ref,
     d_ref,
     aj_ref,
     bj_ref,
-    sems,
     out_sems,
 ):
-    frames, rows, cols, chan = x_ref.shape
-    copies = Copies(
-        [
-                ("hc", hc_hbm, hc_ref),
-            ("h", h_hbm, h_ref),
-            ("hh", hh_hbm, hh_ref),
-            ("w", w_hbm, w_ref),
-            ("x", x_hbm, x_ref),
-            ("p1", p1_hbm, p1_ref),
-            ("p2", p2_hbm, p2_ref),
-            ("wu", wu_hbm, wu_ref),
-        ],
-        sems,
-    )
+    frames, rows, cols, chan = h_ref.shape
     tm, tile = lax.axis_index("tm"), lax.axis_index("tile")
     last = lax.axis_size("tile") - 1
-    odd = lax.rem(tile, 2) == 1
     shift, bias, bias_up = vec_ref[2:3], vec_ref[3:4], vec_ref[4:5]
     in_rows = a_ref.shape[1]
     b_ref[:, in_rows - 1] = jnp.zeros_like(b_ref[:, in_rows - 1])
@@ -364,26 +326,23 @@
                 v = jnp.where(keep, v, 0.0)
             put_both(put_row(v, a_ref, b_ref, slot, row), d_ref, slot, row)
 
-    def joined_frame(f):
-        copies.need("w")
-        out = conv_rows(a_ref, b_ref, d_ref, w_ref, f, [(0, rows + 2)], cols) + bias
-        copies.need("x", "p1", "p2")
-        for r in range(rows + 2):
-            if r == 0:
-                x = jnp.where(odd, p1_ref[f, 2].astype(F32), p2_ref[f, 2].astype(F32))
-            elif r <= rows:
-                x = x_ref[f, r - 1].astype(F32)
-            else:
-                x = jnp.where(odd, p2_ref[f, 0].astype(F32), p1_ref[f, 0].astype(F32))
-            v = out[r * cols : (r + 1) * cols] + x
-            if r == 0:
-                v = jnp.where(tile > 0, v, 0.0)
-            if r > rows:
-                v = jnp.where(tile < last, v, 0.0)
-            put_row(v, aj_ref, bj_ref, f, r)
+    def join(f, r, out):
+        v = out + own_ref[f, r + 2].astype(F32)
+        if r == 0:
+            v = jnp.where(tile > 0, v, 0.0)
+        if r > rows:
+            v = jnp.where(tile < last, v, 0.0)
+        put_row(v, aj_ref, bj_ref, f, r)
+
+    def joined(runs):
+        out = conv_rows(a_ref, b_ref, d_ref, w_ref, runs, cols) + bias
+        k = 0
+        for f, first, n in runs:
+            for r in range(first, first + n):
+                join(f, r, out[k * cols : (k + 1) * cols])
+                k += 1
 
     def up_frame(f):
-        copies.need("wu")
         m = rows * cols
         first = lax.broadcasted_iota(jnp.int32, (m, chan), 1) < chan // 2
         for s in range(2):
@@ -397,20 +356,22 @@
             for y in range(rows):
                 out_ref[f, 2 * y + s] = up[y]
 
-    copies.need("hc")
-    norm_frame(0)
-    norm_frame(1)
-    copies.need("h", "hh")
-    norm_frame(2)
+    for slot in range(4):
+        norm_frame(slot)
     written = []
-    for f in range(frames):
-        joined_frame(f)
-        if f + 3 < frames + 2:
-            norm_frame(f + 3)
-        up_frame(f)
-        copy = pltpu.make_async_copy(out_ref.at[f], out_hbm.at[f], out_sems.at[f])
-        copy.start()
-        written.append(copy)
+    for f in range(0, frames, 2):
+        joined([(f, 1, rows)])
+        if f + 4 < frames + 2:
+            norm_frame(f + 4)
+        joined([(f + 1, 1, rows)])
+        if f + 5 < frames + 2:
+            norm_frame(f + 5)
+        joined([(f + i, r, 1) for i in range(2) for r in (0, rows + 1)])
+        for i in range(f, f + 2):
+            up_frame(i)
+            copy = pltpu.make_async_copy(out_ref.at[i], out_hbm.at[i], out_sems.at[i])
+            copy.start()
+            written.append(copy)
     for copy in written:
         copy.wait()
 
@@ -465,22 +426,29 @@
     all_one = exchange(stat)
     w_one = kernel_one.reshape(27, chan, chan)
     w_two = kernel_two.reshape(27, chan, chan)
-    w_up, last_two = pl.pallas_call(
-        fold_kernel,
+    own, last_two = pl.pallas_call(
+        assemble_kernel,
         out_shape=(
-            shape((2, 2, 2 * chan, chan), BF16),
+            shape((frames, rows + 6, cols, chan), BF16),
             shape((2, rows + 6, cols, chan), BF16),
         ),
-        in_specs=[VM] * 4,
+        in_specs=[VM] * 3,
         out_specs=(VM, VM),
         compiler_params=small,
-        cost_estimate=cost(FOLD_FLOPS, 4 * 2**20),
-        name="fold",
-    )(x, p1, p2, up_kernel.reshape(9, chan, chan // 2))
+        name="assemble",
+    )(x, p1, p2)
     before = lax.ppermute(last_two, "tm", down)
-    vectors = jnp.stack(
-        [shift_one, bias_one, shift_two, bias_two, jnp.concatenate([up_bias, up_bias])]
-    )
+    row = lambda v: v.reshape(1, v.shape[0])
+    parts = [row(v) for v in (shift_one, bias_one, shift_two, bias_two, up_bias)]
+    vectors = pl.pallas_call(
+        vectors_kernel,
+        out_shape=shape((5, chan), F32),
+        in_specs=[VM] * 5,
+        out_specs=VM,
+        compiler_params=small,
+        cost_estimate=cost(FILL_FLOPS, 2**14),
+        name="vectors",
+    )(*parts)
 
     def table(stats, gain):
         rows_of = shape((8, 1, chan), F32)
@@ -494,15 +462,14 @@
             name="table",
         )(stats, gain.reshape(1, chan))
 
-    def scratch(in_rows, out_frames):
+    def scratch(in_rows):
         return [
             pltpu.VMEM((frames + 2, in_rows, cols, 128), BF16),
             pltpu.VMEM((frames + 2, in_rows, cols, 128), BF16),
             pltpu.VMEM((frames, in_rows, cols, 128), BF16),
         ]
 
-    held = lambda v: pltpu.VMEM(v.shape, v.dtype)
-    args = (x, p1, p2, before, w_one)
+    args = (own, before, w_one)
     table_one = table(all_one, gain_one)
 
     def conv_one(ring, row_list, *more):
@@ -511,11 +478,10 @@
         return pl.pallas_call(
             functools.partial(conv_one_kernel, ring, row_list),
             out_shape=outs,
-            in_specs=[HB] * len(args) + [VM] * 3 + [HB] * len(more),
+            in_specs=[VM] * (len(args) + 3) + [HB] * len(more),
             out_specs=(VM,) * len(outs),
-            scratch_shapes=[held(v) for v in args]
-            + scratch(sum(n + 2 for _, n, _ in row_list), frames)
-            + [pltpu.SemaphoreType.DMA((7,))],
+            scratch_shapes=scratch(sum(n + 2 for _, n, _ in row_list))
+            + [pltpu.SemaphoreType.DMA] * len(more),
             compiler_params=limit,
             cost_estimate=cost(one_conv if ring else RIM_FLOPS, 4 * 2**20),
             name="conv_one" if ring else "conv_one_rim",
@@ -525,20 +491,27 @@
     all_two = exchange(stat_two)
     rim, hidden_two = conv_one(False, ((0, 2, 0), (rows + 2, 2, 2)), hidden)
     hidden_before = lax.ppermute(hidden_two, "tm", down)
-    args_two = (x, p1, p2, hidden, rim, hidden_before, w_two, w_up)
+    w_up = pl.pallas_call(
+        fold_kernel,
+        out_shape=shape((2, 2, 2 * chan, chan), BF16),
+        in_specs=[VM, HB],
+        out_specs=VM,
+        compiler_params=small,
+        cost_estimate=cost(FILL_FLOPS, 2 * 2**20),
+        name="fold",
+    )(up_kernel.reshape(9, chan, chan // 2), stat_two)
+    args_two = (own, hidden, rim, hidden_before, w_two, w_up)
     out_shape = shape((frames, 2 * rows, cols, chan), BF16)
     out = pl.pallas_call(
         conv_two_kernel,
         out_shape=out_shape,
-        in_specs=[HB] * len(args_two) + [VM] * 3,
+        in_specs=[VM] * (len(args_two) + 3),
         out_specs=HB,
-        scratch_shapes=[held(v) for v in args_two]
-        + [held(out_shape)]
-        + scratch(rows + 4, frames)
+        scratch_shapes=[pltpu.VMEM(out_shape.shape, BF16)]
+        + scratch(rows + 4)
         + [
             pltpu.VMEM((frames, rows + 2, cols, 128), BF16),
             pltpu.VMEM((frames, rows + 2, cols, 128), BF16),
-            pltpu.SemaphoreType.DMA((9,)),
             pltpu.SemaphoreType.DMA((frames,)),
         ],
         compiler_params=limit,

time: 69.9 us -> 67.6 us (0.967)
  Pallas kernels: 25.7 us -> 18.4 us
  local copies, waits for them, and re-layouts: 8.03 us -> 13.3 us
  starting transfers between devices: 28.4 us -> 30.2 us
  waiting for transfers between devices: 6.19 us -> 4.8 us
  other arithmetic: 0.81 us -> 0 us
    unnamed x26 -> x44, local copies, waits for them, and re-layouts: 7.28 us -> 13.3 us
    pallas_call x2 -> x4, Pallas kernels: 12 us -> 7.84 us  [the longest x1 7.36 us: body(): pl.pallas_call(conv_two_kernel, out_shape=out_shape, in_specs=[VM] * (len...]
    pallas_call x2, Pallas kernels: 11.7 us -> 8.57 us  [conv_one(): pl.pallas_call(functools.partial(conv_one_kernel, ring, row_list), out_sh...]
    all_to_all x2, waiting for transfers between devices: 6.18 us -> 3.77 us  [exchange(): return lax.all_to_all(stat, ('tm', 'tile'), 0, 0)]
    all_to_all x2, starting transfers between devices: 22.9 us -> 24.8 us  [exchange(): return lax.all_to_all(stat, ('tm', 'tile'), 0, 0)]
    ppermute x1, waiting for transfers between devices: 0.01 us -> 1.02 us  [body(): hidden_before = lax.ppermute(hidden_two, 'tm', down)]
    concatenate x1 -> x0, other arithmetic: 0.81 us -> none  [body(): jnp.concatenate([up_bias, up_bias])]
    another operation x1 -> x0, local copies, waits for them, and re-layouts: 0.75 us -> none  [body(): jnp.stack([shift_one, bias_one, shift_two, bias_two, jnp.concatenate([up_...]
  transfers between devices with their start and end apart: 6 -> 6, of which waited for: 2 -> 3; matrix products, arithmetic and copies ran while one was open for 2% -> 0% of each run, Pallas kernels for 9% -> 8%
where the time goes in v3:
time: 67.6 us; the launch traced here: 67.1 us
  starting transfers between devices  30.2 us (45%)
  Pallas kernels  18.4 us (27%)
  local copies, waits for them, and re-layouts  13.3 us (20%)
  waiting for transfers between devices  4.8 us (7%)
    all_to_all x2, starting transfers between devices, exchange(): return lax.all_to_all(stat, ('tm', 'tile'), 0, 0)  24.8 us
    unnamed x44, local copies, waits for them, and re-layouts  13.3 us
    pallas_call x2, Pallas kernels, conv_one(): pl.pallas_call(functools.partial(conv_one_kernel, ring, row_list), out_sh...  8.57 us
    pallas_call x1, Pallas kernels, body(): pl.pallas_call(conv_two_kernel, out_shape=out_shape, in_specs=[VM] * (len...  7.36 us
    all_to_all x2, waiting for transfers between devices, exchange(): return lax.all_to_all(stat, ('tm', 'tile'), 0, 0)  3.77 us
    ppermute x1, starting transfers between devices, body(): p1 = lax.ppermute(even, 'tile', even_pairs)  2.04 us
    ppermute x1, starting transfers between devices, body(): hidden_before = lax.ppermute(hidden_two, 'tm', down)  1.46 us
    pallas_call x1, Pallas kernels, body(): pl.pallas_call(pack_kernel, out_shape=(shape((frames, 3, cols, chan), BF1...  1.36 us
  transfers between devices with their start and end apart: 6, of which 3 were waited for; matrix products, arithmetic and copies ran while one was open for 0% of the time, Pallas kernels for 8%

profile of v3, /device:TPU:1, one launch (start us, length us, event | category | flops | bytes accessed | tf_op | source)
XLA Modules:
  0.0 67.1 jit_solution(12815312587282091280)
XLA Ops:
  0.0 1.0 %copy-done = bf16[1,4,4,64,192]{4,3,2,1,0:T(8,128)(2,1)S(1)} copy-done((bf16[1,4,4,64,192]{4,3,2,1,0:T(8,128)(2,1)S(1)}, bf16[1,4,4,64,192]{4,3,2,1,0:T(8,128)(2,1)}, u32[]{:S(2)}) %copy-start) | copy-done | bytes 393240
  1.0 1.4 %pack.1 = (bf16[4,3,64,192]{3,2,1,0:T(8,128)(2,1)S(1)}, bf16[4,3,64,192]{3,2,1,0:T(8,128)(2,1)S(1)}, f32[128,2,128]{2,1,0:T(2,128)}) custom-call(bf16[4,4,64,192]{3,2,1,0:T(8,128)(2,1)S(1)} %bitcast.12), custom_call_target="tpu_custom_call" | custom-call | tf_op jit(solution)/shard_map/pack/pallas_call | solution.py:412
  2.4 2.0 %collective-permute-start = (bf16[4,3,64,192]{3,2,1,0:T(8,128)(2,1)S(1)}, bf16[4,3,64,192]{3,2,1,0:T(8,128)(2,1)S(1)}, u32[]{:S(2)}, u32[]{:S(2)}) collective-permute-start(bf16[4,3,64,192]{3,2,1,0:T(8,128)(2,1)S(1)} %get-tuple-element.18), channel_id=1, source_target_pairs={{0,1},{1,0},{2,3},{3,2},{4,5},{5,4},{6,7},{7,6},{8,9},{9,8},{10,11... | collective-permute-start | bytes 884744 | tf_op jit(solution)/shard_map/ppermute | solution.py:424
  4.4 0.7 %collective-permute-start.1 = (bf16[4,3,64,192]{3,2,1,0:T(8,128)(2,1)S(1)}, bf16[4,3,64,192]{3,2,1,0:T(8,128)(2,1)S(1)}, u32[]{:S(2)}, u32[]{:S(2)}) collective-permute-start(bf16[4,3,64,192]{3,2,1,0:T(8,128)(2,1)S(1)} %get-tuple-element.19), channel_id=1, source_target_pairs={{1,2},{3,4},{5,6},{7,8},{9,10},{11,12},{13,14},{15,16},{17,18},{19... | collective-permute-start | bytes 884744 | tf_op jit(solution)/shard_map/ppermute | solution.py:425
  5.1 13.1 %all-to-all-start = ((f32[128,2,128]{2,1,0:T(2,128)}), f32[128,2,128]{2,1,0:T(2,128)S(1)}, u32[]{:S(2)}, u32[]{:S(2)}) async-start(f32[128,2,128]{2,1,0:T(2,128)} %get-tuple-element.22), calls=%async_computation | async-start | bytes 262144 | tf_op jit(solution)/shard_map/all_to_all | solution.py:380
  18.3 1.0 %copy-done.1 = bf16[1,4,4,64,192]{4,3,2,1,0:T(8,128)(2,1)S(1)} copy-done((bf16[1,4,4,64,192]{4,3,2,1,0:T(8,128)(2,1)S(1)}, bf16[1,4,4,64,192]{4,3,2,1,0:T(8,128)(2,1)}, u32[]{:S(2)}) %copy-start.1) | copy-done | bytes 393240
  19.5 1.1 %copy-done.5 = bf16[4,10,64,192]{3,2,1,0:T(8,128)(2,1)} copy-done((bf16[4,10,64,192]{3,2,1,0:T(8,128)(2,1)}, bf16[4,10,64,192]{3,2,1,0:T(8,128)(2,1)S(1)}, u32[]{:S(2)}) %copy-start.5) | copy-done | bytes 983064
  20.6 1.3 %collective-permute-start.2 = (bf16[2,10,64,192]{3,2,1,0:T(8,128)(2,1)S(1)}, bf16[2,10,64,192]{3,2,1,0:T(8,128)(2,1)S(1)}, u32[]{:S(2)}, u32[]{:S(2)}) collective-permute-start(bf16[2,10,64,192]{3,2,1,0:T(8,128)(2,1)S(1)} %get-tuple-element.21), channel_id=1, source_target_pairs={{0,64},{1,65},{2,66},{3,67},{4,68},{5,69},{6,70},{7,71},{8,72},{9,... | collective-permute-start | bytes 1474568 | tf_op jit(solution)/shard_map/ppermute | solution.py:440
  21.9 0.7 copy-done.10
  22.6 0.7 %copy-done.11 = f32[192]{0:T(256)S(1)} copy-done((f32[192]{0:T(256)S(1)}, f32[192]{0:T(256)}, u32[]{:S(2)}) %copy-start.11) | copy-done | bytes 792
  23.2 0.7 %copy-done.12 = f32[192]{0:T(256)S(1)} copy-done((f32[192]{0:T(256)S(1)}, f32[192]{0:T(256)}, u32[]{:S(2)}) %copy-start.12) | copy-done | bytes 792
  23.9 0.7 %copy-done.13 = f32[192]{0:T(256)S(1)} copy-done((f32[192]{0:T(256)S(1)}, f32[192]{0:T(256)}, u32[]{:S(2)}) %copy-start.13) | copy-done | bytes 792
  24.6 0.7 copy-done.16
  25.3 2.8 %all-to-all-done.stat_ref = f32[128,2,128]{2,1,0:T(2,128)S(1)} async-done(((f32[128,2,128]{2,1,0:T(2,128)}), f32[128,2,128]{2,1,0:T(2,128)S(1)}, u32[]{:S(2)}, u32[]{:S(2)}) %all-to-all-start) | async-done | bytes 131104 | tf_op jit(solution)/shard_map/all_to_all | solution.py:380
  28.2 0.3 table.2
  28.5 1.4 %copy-done.2 = bf16[3,3,3,192,192]{4,3,2,1,0:T(8,128)(2,1)S(1)} copy-done((bf16[3,3,3,192,192]{4,3,2,1,0:T(8,128)(2,1)S(1)}, bf16[3,3,3,192,192]{4,3,2,1,0:T(8,128)(2,1)}, u32[]{:S(2)}) %copy-start.2) | copy-done | bytes 1990680
  29.9 0.4 copy-done.6
  30.3 4.5 %conv_one.1 = (bf16[4,4,64,192]{3,2,1,0:T(8,128)(2,1)S(1)}, f32[128,2,128]{2,1,0:T(2,128)}) custom-call(bf16[4,10,64,192]{3,2,1,0:T(8,128)(2,1)S(1)} %copy-done.6, bf16[2,10,64,192]{3,2,1,0:T(8,128)(2,1)S(1)} %collective-permute-done.2.c_ref, bf16[27,192,192]{2,1,0:T(8,128)(2,1)S(1)} %bitcast.14, f32[5,192]{1,0:T(8,128)S(1)} %vectors.1.vec_ref, ...), custom_call_target="tpu_custom_call" | custom-call | flops 2038431744 | bytes 4194304 | tf_op jit(solution)/shard_map/conv_one/pallas_call | solution.py:478
  34.8 0.8 %copy-done.17 = bf16[4,4,64,192]{3,2,1,0:T(8,128)(2,1)} copy-done((bf16[4,4,64,192]{3,2,1,0:T(8,128)(2,1)}, bf16[4,4,64,192]{3,2,1,0:T(8,128)(2,1)S(1)}, u32[]{:S(2)}) %copy-start.17) | copy-done | bytes 393240
  35.6 11.7 %all-to-all-start.1 = ((f32[128,2,128]{2,1,0:T(2,128)}), f32[128,2,128]{2,1,0:T(2,128)S(1)}, u32[]{:S(2)}, u32[]{:S(2)}) async-start(f32[128,2,128]{2,1,0:T(2,128)} %get-tuple-element.28.after_hbm), calls=%async_computation.1 | async-start | bytes 262144 | tf_op jit(solution)/shard_map/all_to_all | solution.py:380
  47.2 1.3 %copy-done.7 = bf16[4,10,64,192]{3,2,1,0:T(8,128)(2,1)S(1)} copy-done((bf16[4,10,64,192]{3,2,1,0:T(8,128)(2,1)S(1)}, bf16[4,10,64,192]{3,2,1,0:T(8,128)(2,1)}, u32[]{:S(2)}) %copy-start.7) | copy-done | bytes 983064
  48.6 1.0 %copy-done.18 = bf16[4,4,64,192]{3,2,1,0:T(8,128)(2,1)S(1)} copy-done((bf16[4,4,64,192]{3,2,1,0:T(8,128)(2,1)S(1)}, bf16[4,4,64,192]{3,2,1,0:T(8,128)(2,1)}, u32[]{:S(2)}) %copy-start.18) | copy-done | bytes 393240
  49.6 4.1 %conv_one_rim.1 = (bf16[4,4,64,192]{3,2,1,0:T(8,128)(2,1)S(1)}, bf16[2,8,64,192]{3,2,1,0:T(8,128)(2,1)}) custom-call(bf16[4,10,64,192]{3,2,1,0:T(8,128)(2,1)S(1)} %copy-done.7, bf16[2,10,64,192]{3,2,1,0:T(8,128)(2,1)S(1)} %collective-permute-done.2.c_ref, bf16[27,192,192]{2,1,0:T(8,128)(2,1)S(1)} %bitcast.15, f32[5,192]{1,0:T(8,128)S(1)} %vectors.1.vec_ref, ...), custom_call_target="tpu_custom_call" | custom-call | flops 4000000000 | bytes 4194304 | tf_op jit(solution)/shard_map/conv_one_rim/pallas_call | solution.py:478
  53.7 0.8 %copy-done.20 = bf16[4,4,64,192]{3,2,1,0:T(8,128)(2,1)} copy-done((bf16[4,4,64,192]{3,2,1,0:T(8,128)(2,1)}, bf16[4,4,64,192]{3,2,1,0:T(8,128)(2,1)S(1)}, u32[]{:S(2)}) %copy-start.20) | copy-done | bytes 393240
  54.5 1.5 %collective-permute-start.3 = (bf16[2,8,64,192]{3,2,1,0:T(8,128)(2,1)}, bf16[2,8,64,192]{3,2,1,0:T(8,128)(2,1)S(1)}, u32[]{:S(2)}, u32[]{:S(2)}) collective-permute-start(bf16[2,8,64,192]{3,2,1,0:T(8,128)(2,1)} %get-tuple-element.27), channel_id=1, source_target_pairs={{0,64},{1,65},{2,66},{3,67},{4,68},{5,69},{6,70},{7,71},{8,72},{9,... | collective-permute-start | bytes 1179656 | tf_op jit(solution)/shard_map/ppermute | solution.py:493
  56.0 0.2 fold.1.wu_ref
  56.2 0.9 %all-to-all-done.1.stat_ref = f32[128,2,128]{2,1,0:T(2,128)S(1)} async-done(((f32[128,2,128]{2,1,0:T(2,128)}), f32[128,2,128]{2,1,0:T(2,128)S(1)}, u32[]{:S(2)}, u32[]{:S(2)}) %all-to-all-start.1) | async-done | bytes 131104 | tf_op jit(solution)/shard_map/all_to_all | solution.py:380
  57.2 0.3 table.3
  57.5 1.0 %collective-permute-done.3.hc_ref = bf16[2,8,64,192]{3,2,1,0:T(8,128)(2,1)S(1)} collective-permute-done((bf16[2,8,64,192]{3,2,1,0:T(8,128)(2,1)}, bf16[2,8,64,192]{3,2,1,0:T(8,128)(2,1)S(1)}, u32[]{:S(2)}, u32[]{:S(2)}) %collective-permute-start.3) | collective-permute-done | bytes 393248 | tf_op jit(solution)/shard_map/ppermute | solution.py:493
  58.5 0.4 copy-done.4
  58.9 0.4 copy-done.8
  59.5 7.4 %conv_two.1 = bf16[4,8,64,192]{3,2,1,0:T(8,128)(2,1)} custom-call(bf16[4,10,64,192]{3,2,1,0:T(8,128)(2,1)S(1)} %copy-done.8, bf16[4,4,64,192]{3,2,1,0:T(8,128)(2,1)S(1)} %copy-done.19, bf16[4,4,64,192]{3,2,1,0:T(8,128)(2,1)S(1)} %copy-done.21, bf16[2,8,64,192]{3,2,1,0:T(8,128)(2,1)S(1)} %collective-permute-done.3.hc_ref, bf16[27,192,192]{2,1,0:T(8,128)(2,1)S(1)} %bitcast.16, ...), custom_call_target="tpu_custom_call" | custom-call | flops 6115295232 | bytes 4194304 | tf_op jit(solution)/shard_map/conv_two/pallas_call | solution.py:505
  (33 shorter events, 0.6 us)
Async XLA Ops:
  0.0 1.0 %copy-start = (bf16[1,4,4,64,192]{4,3,2,1,0:T(8,128)(2,1)S(1)}, bf16[1,4,4,64,192]{4,3,2,1,0:T(8,128)(2,1)}, u32[]{:S(2)}) copy-start(bf16[1,4,4,64,192]{4,3,2,1,0:T(8,128)(2,1)} %param.11) | copy-start | bytes 1179652
  2.4 15.8 %collective-permute-start = (bf16[4,3,64,192]{3,2,1,0:T(8,128)(2,1)S(1)}, bf16[4,3,64,192]{3,2,1,0:T(8,128)(2,1)S(1)}, u32[]{:S(2)}, u32[]{:S(2)}) collective-permute-start(bf16[4,3,64,192]{3,2,1,0:T(8,128)(2,1)S(1)} %get-tuple-element.18), channel_id=1, source_target_pairs={{0,1},{1,0},{2,3},{3,2},{4,5},{5,4},{6,7},{7,6},{8,9},{9,8},{10,11... | collective-permute-start | bytes 884744 | tf_op jit(solution)/shard_map/ppermute | solution.py:424
  4.4 13.8 %collective-permute-start.1 = (bf16[4,3,64,192]{3,2,1,0:T(8,128)(2,1)S(1)}, bf16[4,3,64,192]{3,2,1,0:T(8,128)(2,1)S(1)}, u32[]{:S(2)}, u32[]{:S(2)}) collective-permute-start(bf16[4,3,64,192]{3,2,1,0:T(8,128)(2,1)S(1)} %get-tuple-element.19), channel_id=1, source_target_pairs={{1,2},{3,4},{5,6},{7,8},{9,10},{11,12},{13,14},{15,16},{17,18},{19... | collective-permute-start | bytes 884744 | tf_op jit(solution)/shard_map/ppermute | solution.py:425
  5.1 23.0 %all-to-all-start = ((f32[128,2,128]{2,1,0:T(2,128)}), f32[128,2,128]{2,1,0:T(2,128)S(1)}, u32[]{:S(2)}, u32[]{:S(2)}) async-start(f32[128,2,128]{2,1,0:T(2,128)} %get-tuple-element.22), calls=%async_computation | async-start | bytes 262144 | tf_op jit(solution)/shard_map/all_to_all | solution.py:380
  18.3 1.0 %copy-start.1 = (bf16[1,4,4,64,192]{4,3,2,1,0:T(8,128)(2,1)S(1)}, bf16[1,4,4,64,192]{4,3,2,1,0:T(8,128)(2,1)}, u32[]{:S(2)}) copy-start(bf16[1,4,4,64,192]{4,3,2,1,0:T(8,128)(2,1)} %param.11) | copy-start | bytes 1179652
  19.5 1.1 %copy-start.5 = (bf16[4,10,64,192]{3,2,1,0:T(8,128)(2,1)}, bf16[4,10,64,192]{3,2,1,0:T(8,128)(2,1)S(1)}, u32[]{:S(2)}) copy-start(bf16[4,10,64,192]{3,2,1,0:T(8,128)(2,1)S(1)} %get-tuple-element.20.own_ref) | copy-start | bytes 2949124
  20.6 7.9 %collective-permute-start.2 = (bf16[2,10,64,192]{3,2,1,0:T(8,128)(2,1)S(1)}, bf16[2,10,64,192]{3,2,1,0:T(8,128)(2,1)S(1)}, u32[]{:S(2)}, u32[]{:S(2)}) collective-permute-start(bf16[2,10,64,192]{3,2,1,0:T(8,128)(2,1)S(1)} %get-tuple-element.21), channel_id=1, source_target_pairs={{0,64},{1,65},{2,66},{3,67},{4,68},{5,69},{6,70},{7,71},{8,72},{9,... | collective-permute-start | bytes 1474568 | tf_op jit(solution)/shard_map/ppermute | solution.py:440
  21.9 0.7 %copy-start.10 = (f32[192]{0:T(256)S(1)}, f32[192]{0:T(256)}, u32[]{:S(2)}) copy-start(f32[192]{0:T(256)} %param.13) | copy-start | bytes 2308
  22.6 0.7 %copy-start.11 = (f32[192]{0:T(256)S(1)}, f32[192]{0:T(256)}, u32[]{:S(2)}) copy-start(f32[192]{0:T(256)} %param.15) | copy-start | bytes 2308
  23.2 0.7 %copy-start.12 = (f32[192]{0:T(256)S(1)}, f32[192]{0:T(256)}, u32[]{:S(2)}) copy-start(f32[192]{0:T(256)} %param.17) | copy-start | bytes 2308
  23.9 0.7 %copy-start.13 = (f32[192]{0:T(256)S(1)}, f32[192]{0:T(256)}, u32[]{:S(2)}) copy-start(f32[192]{0:T(256)} %param.19) | copy-start | bytes 2308
  24.6 0.7 copy-start.16
  25.2 2.9 %copy-start.14 = (f32[192]{0:T(256)S(1)}, f32[192]{0:T(256)}, u32[]{:S(2)}) copy-start(f32[192]{0:T(256)} %param.12) | copy-start | bytes 2308
  28.2 1.8 %copy-start.2 = (bf16[3,3,3,192,192]{4,3,2,1,0:T(8,128)(2,1)S(1)}, bf16[3,3,3,192,192]{4,3,2,1,0:T(8,128)(2,1)}, u32[]{:S(2)}) copy-start(bf16[3,3,3,192,192]{4,3,2,1,0:T(8,128)(2,1)} %param.14) | copy-start | bytes 5971972
  28.2 2.1 %copy-start.6 = (bf16[4,10,64,192]{3,2,1,0:T(8,128)(2,1)S(1)}, bf16[4,10,64,192]{3,2,1,0:T(8,128)(2,1)}, u32[]{:S(2)}) copy-start(bf16[4,10,64,192]{3,2,1,0:T(8,128)(2,1)} %copy-done.5) | copy-start | bytes 2949124
  30.3 16.9 %copy-start.3 = (bf16[3,3,3,192,192]{4,3,2,1,0:T(8,128)(2,1)S(1)}, bf16[3,3,3,192,192]{4,3,2,1,0:T(8,128)(2,1)}, u32[]{:S(2)}) copy-start(bf16[3,3,3,192,192]{4,3,2,1,0:T(8,128)(2,1)} %param.14) | copy-start | bytes 5971972
  34.8 0.8 %copy-start.17 = (bf16[4,4,64,192]{3,2,1,0:T(8,128)(2,1)}, bf16[4,4,64,192]{3,2,1,0:T(8,128)(2,1)S(1)}, u32[]{:S(2)}) copy-start(bf16[4,4,64,192]{3,2,1,0:T(8,128)(2,1)S(1)} %get-tuple-element.25.rest_0_.h_ref) | copy-start | bytes 1179652
  35.6 21.6 %all-to-all-start.1 = ((f32[128,2,128]{2,1,0:T(2,128)}), f32[128,2,128]{2,1,0:T(2,128)S(1)}, u32[]{:S(2)}, u32[]{:S(2)}) async-start(f32[128,2,128]{2,1,0:T(2,128)} %get-tuple-element.28.after_hbm), calls=%async_computation.1 | async-start | bytes 262144 | tf_op jit(solution)/shard_map/all_to_all | solution.py:380
  47.2 1.3 %copy-start.7 = (bf16[4,10,64,192]{3,2,1,0:T(8,128)(2,1)S(1)}, bf16[4,10,64,192]{3,2,1,0:T(8,128)(2,1)}, u32[]{:S(2)}) copy-start(bf16[4,10,64,192]{3,2,1,0:T(8,128)(2,1)} %copy-done.5) | copy-start | bytes 2949124
  48.6 1.0 %copy-start.18 = (bf16[4,4,64,192]{3,2,1,0:T(8,128)(2,1)S(1)}, bf16[4,4,64,192]{3,2,1,0:T(8,128)(2,1)}, u32[]{:S(2)}) copy-start(bf16[4,4,64,192]{3,2,1,0:T(8,128)(2,1)} %copy-done.17) | copy-start | bytes 1179652
  49.6 6.4 %copy-start.9 = (bf16[3,3,192,96]{3,2,1,0:T(8,128)(2,1)S(1)}, bf16[3,3,192,96]{3,2,1,0:T(8,128)(2,1)}, u32[]{:S(2)}) copy-start(bf16[3,3,192,96]{3,2,1,0:T(8,128)(2,1)} %param.20) | copy-start | bytes 995332
  53.7 0.8 %copy-start.20 = (bf16[4,4,64,192]{3,2,1,0:T(8,128)(2,1)}, bf16[4,4,64,192]{3,2,1,0:T(8,128)(2,1)S(1)}, u32[]{:S(2)}) copy-start(bf16[4,4,64,192]{3,2,1,0:T(8,128)(2,1)S(1)} %get-tuple-element.26.hh_ref) | copy-start | bytes 1179652
  54.5 4.0 %collective-permute-start.3 = (bf16[2,8,64,192]{3,2,1,0:T(8,128)(2,1)}, bf16[2,8,64,192]{3,2,1,0:T(8,128)(2,1)S(1)}, u32[]{:S(2)}, u32[]{:S(2)}) collective-permute-start(bf16[2,8,64,192]{3,2,1,0:T(8,128)(2,1)} %get-tuple-element.27), channel_id=1, source_target_pairs={{0,64},{1,65},{2,66},{3,67},{4,68},{5,69},{6,70},{7,71},{8,72},{9,... | collective-permute-start | bytes 1179656 | tf_op jit(solution)/shard_map/ppermute | solution.py:493
  56.0 1.1 %copy-start.15 = (f32[192]{0:T(256)S(1)}, f32[192]{0:T(256)}, u32[]{:S(2)}) copy-start(f32[192]{0:T(256)} %param.16) | copy-start | bytes 2308
  57.2 1.8 %copy-start.4 = (bf16[3,3,3,192,192]{4,3,2,1,0:T(8,128)(2,1)S(1)}, bf16[3,3,3,192,192]{4,3,2,1,0:T(8,128)(2,1)}, u32[]{:S(2)}) copy-start(bf16[3,3,3,192,192]{4,3,2,1,0:T(8,128)(2,1)} %param.18) | copy-start | bytes 5971972
  57.2 2.1 %copy-start.8 = (bf16[4,10,64,192]{3,2,1,0:T(8,128)(2,1)S(1)}, bf16[4,10,64,192]{3,2,1,0:T(8,128)(2,1)}, u32[]{:S(2)}) copy-start(bf16[4,10,64,192]{3,2,1,0:T(8,128)(2,1)} %copy-done.5) | copy-start | bytes 2949124
  57.2 2.2 %copy-start.19 = (bf16[4,4,64,192]{3,2,1,0:T(8,128)(2,1)S(1)}, bf16[4,4,64,192]{3,2,1,0:T(8,128)(2,1)}, u32[]{:S(2)}) copy-start(bf16[4,4,64,192]{3,2,1,0:T(8,128)(2,1)} %copy-done.17) | copy-start | bytes 1179652
  57.2 2.4 %copy-start.21 = (bf16[4,4,64,192]{3,2,1,0:T(8,128)(2,1)S(1)}, bf16[4,4,64,192]{3,2,1,0:T(8,128)(2,1)}, u32[]{:S(2)}) copy-start(bf16[4,4,64,192]{3,2,1,0:T(8,128)(2,1)} %copy-done.20) | copy-start | bytes 1179652

commit v4 on v3

--- a/solution.py
+++ b/solution.py
@@ -204,9 +204,9 @@
     ring, row_list, own_ref, c_ref, w_ref, vec_ref, mean_ref, scale_ref, *rest
 ):
     if ring:
-        out_ref, stat_ref, a_ref, b_ref, d_ref = rest
+        out_hbm, stat_ref, a_ref, b_ref, d_ref, out_ref, out_sems = rest
     else:
-        h_hbm, out_ref, cache_ref, a_ref, b_ref, d_ref, sem = rest
+        h_hbm, out_hbm, cache_ref, a_ref, b_ref, d_ref, out_ref, out_sems, sem = rest
     frames, rows, cols, chan = own_ref.shape
     rows -= 6
     if not ring:
@@ -245,7 +245,7 @@
 
     norm_frame(0)
     norm_frame(1)
-    stats, runs, k = [], [], 0
+    stats, written, runs, k = [], [], [], 0
     for _, n, _ in row_list:
         runs.append((k, n))
         k += n + 2
@@ -261,12 +261,17 @@
                 at = where_to if where_to == 0 else where_to + rows
                 cache_ref[f - frames + 2, at : at + n] = rows_out[k : k + n]
             k += n
+        copy = pltpu.make_async_copy(out_ref.at[f], out_hbm.at[f], out_sems.at[f])
+        copy.start()
+        written.append(copy)
         if ring:
             stats.append(channel_stats(out.astype(F32)))
     if ring:
         local_stats(stats, rows * cols, stat_ref)
     else:
         load_h.wait()
+    for copy in written:
+        copy.wait()
 
 
 def put_both(tail, d_ref, slot, k):
@@ -473,15 +478,18 @@
     table_one = table(all_one, gain_one)
 
     def conv_one(ring, row_list, *more):
-        outs = (shape((frames, rows, cols, chan), BF16),)
+        outs = (pltpu.HBM((frames, rows, cols, chan), BF16),)
+        extra = [
+            pltpu.VMEM((frames, rows, cols, chan), BF16),
+            pltpu.SemaphoreType.DMA((frames,)),
+        ] + [pltpu.SemaphoreType.DMA] * len(more)
         outs += (stat_shape,) if ring else (shape((2, rows + 4, cols, chan), BF16),)
         return pl.pallas_call(
             functools.partial(conv_one_kernel, ring, row_list),
             out_shape=outs,
             in_specs=[VM] * (len(args) + 3) + [HB] * len(more),
-            out_specs=(VM,) * len(outs),
-            scratch_shapes=scratch(sum(n + 2 for _, n, _ in row_list))
-            + [pltpu.SemaphoreType.DMA] * len(more),
+            out_specs=(HB, VM),
+            scratch_shapes=scratch(sum(n + 2 for _, n, _ in row_list)) + extra,
             compiler_params=limit,
             cost_estimate=cost(one_conv if ring else RIM_FLOPS, 4 * 2**20),
             name="conv_one" if ring else "conv_one_rim",

time: 67.6 us -> 67 us (level)
  local copies, waits for them, and re-layouts: 13.3 us -> 11.8 us
  Pallas kernels: 18.4 us -> 19.4 us
    unnamed x44 -> x40, local copies, waits for them, and re-layouts: 13.3 us -> 11.8 us
    pallas_call x2, Pallas kernels: 8.57 us -> 9.53 us  [conv_one(): pl.pallas_call(functools.partial(conv_one_kernel, ring, row_list), out_sh...]
  transfers between devices with their start and end apart: 6 -> 6, of which waited for: 3 -> 3; matrix products, arithmetic and copies ran while one was open for 0% -> 0% of each run, Pallas kernels for 8% -> 9%
where the time goes in v4:
time: 67 us; the launch traced here: 66.6 us
  starting transfers between devices  30.2 us (45%)
  Pallas kernels  19.4 us (29%)
  local copies, waits for them, and re-layouts  11.8 us (18%)
  waiting for transfers between devices  4.79 us (7%)
    all_to_all x2, starting transfers between devices, exchange(): return lax.all_to_all(stat, ('tm', 'tile'), 0, 0)  24.8 us
    unnamed x40, local copies, waits for them, and re-layouts  11.8 us
    pallas_call x2, Pallas kernels, conv_one(): pl.pallas_call(functools.partial(conv_one_kernel, ring, row_list), out_sh...  9.53 us
    pallas_call x1, Pallas kernels, body(): pl.pallas_call(conv_two_kernel, out_shape=out_shape, in_specs=[VM] * (len...  7.36 us
    all_to_all x2, waiting for transfers between devices, exchange(): return lax.all_to_all(stat, ('tm', 'tile'), 0, 0)  3.89 us
    ppermute x1, starting transfers between devices, body(): p1 = lax.ppermute(even, 'tile', even_pairs)  2.04 us
    ppermute x1, starting transfers between devices, body(): hidden_before = lax.ppermute(hidden_two, 'tm', down)  1.47 us
    pallas_call x1, Pallas kernels, body(): pl.pallas_call(pack_kernel, out_shape=(shape((frames, 3, cols, chan), BF1...  1.36 us
  transfers between devices with their start and end apart: 6, of which 3 were waited for; matrix products, arithmetic and copies ran while one was open for 0% of the time, Pallas kernels for 9%

profile of v4, /device:TPU:1, one launch (start us, length us, event | category | flops | bytes accessed | tf_op | source)
XLA Modules:
  0.0 66.6 jit_solution(12300512872695076128)
XLA Ops:
  0.0 1.0 %copy-done = bf16[1,4,4,64,192]{4,3,2,1,0:T(8,128)(2,1)S(1)} copy-done((bf16[1,4,4,64,192]{4,3,2,1,0:T(8,128)(2,1)S(1)}, bf16[1,4,4,64,192]{4,3,2,1,0:T(8,128)(2,1)}, u32[]{:S(2)}) %copy-start) | copy-done | bytes 393240
  1.0 1.4 %pack.1 = (bf16[4,3,64,192]{3,2,1,0:T(8,128)(2,1)S(1)}, bf16[4,3,64,192]{3,2,1,0:T(8,128)(2,1)S(1)}, f32[128,2,128]{2,1,0:T(2,128)}) custom-call(bf16[4,4,64,192]{3,2,1,0:T(8,128)(2,1)S(1)} %bitcast.12), custom_call_target="tpu_custom_call" | custom-call | tf_op jit(solution)/shard_map/pack/pallas_call | solution.py:417
  2.4 2.0 %collective-permute-start = (bf16[4,3,64,192]{3,2,1,0:T(8,128)(2,1)S(1)}, bf16[4,3,64,192]{3,2,1,0:T(8,128)(2,1)S(1)}, u32[]{:S(2)}, u32[]{:S(2)}) collective-permute-start(bf16[4,3,64,192]{3,2,1,0:T(8,128)(2,1)S(1)} %get-tuple-element.18), channel_id=1, source_target_pairs={{0,1},{1,0},{2,3},{3,2},{4,5},{5,4},{6,7},{7,6},{8,9},{9,8},{10,11... | collective-permute-start | bytes 884744 | tf_op jit(solution)/shard_map/ppermute | solution.py:429
  4.4 0.7 %collective-permute-start.1 = (bf16[4,3,64,192]{3,2,1,0:T(8,128)(2,1)S(1)}, bf16[4,3,64,192]{3,2,1,0:T(8,128)(2,1)S(1)}, u32[]{:S(2)}, u32[]{:S(2)}) collective-permute-start(bf16[4,3,64,192]{3,2,1,0:T(8,128)(2,1)S(1)} %get-tuple-element.19), channel_id=1, source_target_pairs={{1,2},{3,4},{5,6},{7,8},{9,10},{11,12},{13,14},{15,16},{17,18},{19... | collective-permute-start | bytes 884744 | tf_op jit(solution)/shard_map/ppermute | solution.py:430
  5.1 13.1 %all-to-all-start = ((f32[128,2,128]{2,1,0:T(2,128)}), f32[128,2,128]{2,1,0:T(2,128)S(1)}, u32[]{:S(2)}, u32[]{:S(2)}) async-start(f32[128,2,128]{2,1,0:T(2,128)} %get-tuple-element.22), calls=%async_computation | async-start | bytes 262144 | tf_op jit(solution)/shard_map/all_to_all | solution.py:385
  18.3 1.0 %copy-done.1 = bf16[1,4,4,64,192]{4,3,2,1,0:T(8,128)(2,1)S(1)} copy-done((bf16[1,4,4,64,192]{4,3,2,1,0:T(8,128)(2,1)S(1)}, bf16[1,4,4,64,192]{4,3,2,1,0:T(8,128)(2,1)}, u32[]{:S(2)}) %copy-start.1) | copy-done | bytes 393240
  19.3 0.2 assemble.1
  19.5 1.1 %copy-done.5 = bf16[4,10,64,192]{3,2,1,0:T(8,128)(2,1)} copy-done((bf16[4,10,64,192]{3,2,1,0:T(8,128)(2,1)}, bf16[4,10,64,192]{3,2,1,0:T(8,128)(2,1)S(1)}, u32[]{:S(2)}) %copy-start.5) | copy-done | bytes 983064
  20.6 1.3 %collective-permute-start.2 = (bf16[2,10,64,192]{3,2,1,0:T(8,128)(2,1)S(1)}, bf16[2,10,64,192]{3,2,1,0:T(8,128)(2,1)S(1)}, u32[]{:S(2)}, u32[]{:S(2)}) collective-permute-start(bf16[2,10,64,192]{3,2,1,0:T(8,128)(2,1)S(1)} %get-tuple-element.21), channel_id=1, source_target_pairs={{0,64},{1,65},{2,66},{3,67},{4,68},{5,69},{6,70},{7,71},{8,72},{9,... | collective-permute-start | bytes 1474568 | tf_op jit(solution)/shard_map/ppermute | solution.py:445
  21.9 0.7 %copy-done.10 = f32[192]{0:T(256)S(1)} copy-done((f32[192]{0:T(256)S(1)}, f32[192]{0:T(256)}, u32[]{:S(2)}) %copy-start.10) | copy-done | bytes 792
  22.6 0.7 %copy-done.11 = f32[192]{0:T(256)S(1)} copy-done((f32[192]{0:T(256)S(1)}, f32[192]{0:T(256)}, u32[]{:S(2)}) %copy-start.11) | copy-done | bytes 792
  23.2 0.7 %copy-done.12 = f32[192]{0:T(256)S(1)} copy-done((f32[192]{0:T(256)S(1)}, f32[192]{0:T(256)}, u32[]{:S(2)}) %copy-start.12) | copy-done | bytes 792
  23.9 0.7 %copy-done.13 = f32[192]{0:T(256)S(1)} copy-done((f32[192]{0:T(256)S(1)}, f32[192]{0:T(256)}, u32[]{:S(2)}) %copy-start.13) | copy-done | bytes 792
  24.6 0.7 copy-done.16
  25.3 2.8 %all-to-all-done.stat_ref = f32[128,2,128]{2,1,0:T(2,128)S(1)} async-done(((f32[128,2,128]{2,1,0:T(2,128)}), f32[128,2,128]{2,1,0:T(2,128)S(1)}, u32[]{:S(2)}, u32[]{:S(2)}) %all-to-all-start) | async-done | bytes 131104 | tf_op jit(solution)/shard_map/all_to_all | solution.py:385
  28.2 0.3 table.2
  28.5 1.4 %copy-done.2 = bf16[3,3,3,192,192]{4,3,2,1,0:T(8,128)(2,1)S(1)} copy-done((bf16[3,3,3,192,192]{4,3,2,1,0:T(8,128)(2,1)S(1)}, bf16[3,3,3,192,192]{4,3,2,1,0:T(8,128)(2,1)}, u32[]{:S(2)}) %copy-start.2) | copy-done | bytes 1990680
  29.9 0.4 copy-done.6
  30.3 4.7 %conv_one.1 = (bf16[4,4,64,192]{3,2,1,0:T(8,128)(2,1)}, f32[128,2,128]{2,1,0:T(2,128)}) custom-call(bf16[4,10,64,192]{3,2,1,0:T(8,128)(2,1)S(1)} %copy-done.6, bf16[2,10,64,192]{3,2,1,0:T(8,128)(2,1)S(1)} %collective-permute-done.2.c_ref, bf16[27,192,192]{2,1,0:T(8,128)(2,1)S(1)} %bitcast.14, f32[5,192]{1,0:T(8,128)S(1)} %vectors.1.vec_ref, ...), custom_call_target="tpu_custom_call" | custom-call | flops 2038431744 | bytes 4194304 | tf_op jit(solution)/shard_map/conv_one/pallas_call | solution.py:487
  35.0 11.7 %all-to-all-start.1 = ((f32[128,2,128]{2,1,0:T(2,128)}), f32[128,2,128]{2,1,0:T(2,128)S(1)}, u32[]{:S(2)}, u32[]{:S(2)}) async-start(f32[128,2,128]{2,1,0:T(2,128)} %get-tuple-element.28.after_hbm), calls=%async_computation.1 | async-start | bytes 262144 | tf_op jit(solution)/shard_map/all_to_all | solution.py:385
  46.7 1.3 %copy-done.7 = bf16[4,10,64,192]{3,2,1,0:T(8,128)(2,1)S(1)} copy-done((bf16[4,10,64,192]{3,2,1,0:T(8,128)(2,1)S(1)}, bf16[4,10,64,192]{3,2,1,0:T(8,128)(2,1)}, u32[]{:S(2)}) %copy-start.7) | copy-done | bytes 983064
  48.0 1.0 %copy-done.17 = bf16[4,4,64,192]{3,2,1,0:T(8,128)(2,1)S(1)} copy-done((bf16[4,4,64,192]{3,2,1,0:T(8,128)(2,1)S(1)}, bf16[4,4,64,192]{3,2,1,0:T(8,128)(2,1)}, u32[]{:S(2)}) %copy-start.17) | copy-done | bytes 393240
  49.1 4.8 %conv_one_rim.1 = (bf16[4,4,64,192]{3,2,1,0:T(8,128)(2,1)}, bf16[2,8,64,192]{3,2,1,0:T(8,128)(2,1)}) custom-call(bf16[4,10,64,192]{3,2,1,0:T(8,128)(2,1)S(1)} %copy-done.7, bf16[2,10,64,192]{3,2,1,0:T(8,128)(2,1)S(1)} %collective-permute-done.2.c_ref, bf16[27,192,192]{2,1,0:T(8,128)(2,1)S(1)} %bitcast.15, f32[5,192]{1,0:T(8,128)S(1)} %vectors.1.vec_ref, ...), custom_call_target="tpu_custom_call" | custom-call | flops 4000000000 | bytes 4194304 | tf_op jit(solution)/shard_map/conv_one_rim/pallas_call | solution.py:487
  53.9 1.5 %collective-permute-start.3 = (bf16[2,8,64,192]{3,2,1,0:T(8,128)(2,1)}, bf16[2,8,64,192]{3,2,1,0:T(8,128)(2,1)S(1)}, u32[]{:S(2)}, u32[]{:S(2)}) collective-permute-start(bf16[2,8,64,192]{3,2,1,0:T(8,128)(2,1)} %get-tuple-element.27), channel_id=1, source_target_pairs={{0,64},{1,65},{2,66},{3,67},{4,68},{5,69},{6,70},{7,71},{8,72},{9,... | collective-permute-start | bytes 1179656 | tf_op jit(solution)/shard_map/ppermute | solution.py:501
  55.4 0.2 fold.1.wu_ref
  55.6 1.0 %all-to-all-done.1.stat_ref = f32[128,2,128]{2,1,0:T(2,128)S(1)} async-done(((f32[128,2,128]{2,1,0:T(2,128)}), f32[128,2,128]{2,1,0:T(2,128)S(1)}, u32[]{:S(2)}, u32[]{:S(2)}) %all-to-all-start.1) | async-done | bytes 131104 | tf_op jit(solution)/shard_map/all_to_all | solution.py:385
  56.7 0.3 table.3
  57.0 0.9 %collective-permute-done.3.hc_ref = bf16[2,8,64,192]{3,2,1,0:T(8,128)(2,1)S(1)} collective-permute-done((bf16[2,8,64,192]{3,2,1,0:T(8,128)(2,1)}, bf16[2,8,64,192]{3,2,1,0:T(8,128)(2,1)S(1)}, u32[]{:S(2)}, u32[]{:S(2)}) %collective-permute-start.3) | collective-permute-done | bytes 393248 | tf_op jit(solution)/shard_map/ppermute | solution.py:501
  57.9 0.5 copy-done.4
  58.4 0.4 copy-done.8
  58.9 0.2 copy-done.19
  59.0 7.4 %conv_two.1 = bf16[4,8,64,192]{3,2,1,0:T(8,128)(2,1)} custom-call(bf16[4,10,64,192]{3,2,1,0:T(8,128)(2,1)S(1)} %copy-done.8, bf16[4,4,64,192]{3,2,1,0:T(8,128)(2,1)S(1)} %copy-done.18, bf16[4,4,64,192]{3,2,1,0:T(8,128)(2,1)S(1)} %copy-done.19, bf16[2,8,64,192]{3,2,1,0:T(8,128)(2,1)S(1)} %collective-permute-done.3.hc_ref, bf16[27,192,192]{2,1,0:T(8,128)(2,1)S(1)} %bitcast.16, ...), custom_call_target="tpu_custom_call" | custom-call | flops 6115295232 | bytes 4194304 | tf_op jit(solution)/shard_map/conv_two/pallas_call | solution.py:513
  (29 shorter events, 0.3 us)
Async XLA Ops:
  0.0 1.0 %copy-start = (bf16[1,4,4,64,192]{4,3,2,1,0:T(8,128)(2,1)S(1)}, bf16[1,4,4,64,192]{4,3,2,1,0:T(8,128)(2,1)}, u32[]{:S(2)}) copy-start(bf16[1,4,4,64,192]{4,3,2,1,0:T(8,128)(2,1)} %param.11) | copy-start | bytes 1179652
  2.4 15.8 %collective-permute-start = (bf16[4,3,64,192]{3,2,1,0:T(8,128)(2,1)S(1)}, bf16[4,3,64,192]{3,2,1,0:T(8,128)(2,1)S(1)}, u32[]{:S(2)}, u32[]{:S(2)}) collective-permute-start(bf16[4,3,64,192]{3,2,1,0:T(8,128)(2,1)S(1)} %get-tuple-element.18), channel_id=1, source_target_pairs={{0,1},{1,0},{2,3},{3,2},{4,5},{5,4},{6,7},{7,6},{8,9},{9,8},{10,11... | collective-permute-start | bytes 884744 | tf_op jit(solution)/shard_map/ppermute | solution.py:429
  4.4 13.8 %collective-permute-start.1 = (bf16[4,3,64,192]{3,2,1,0:T(8,128)(2,1)S(1)}, bf16[4,3,64,192]{3,2,1,0:T(8,128)(2,1)S(1)}, u32[]{:S(2)}, u32[]{:S(2)}) collective-permute-start(bf16[4,3,64,192]{3,2,1,0:T(8,128)(2,1)S(1)} %get-tuple-element.19), channel_id=1, source_target_pairs={{1,2},{3,4},{5,6},{7,8},{9,10},{11,12},{13,14},{15,16},{17,18},{19... | collective-permute-start | bytes 884744 | tf_op jit(solution)/shard_map/ppermute | solution.py:430
  5.1 23.0 %all-to-all-start = ((f32[128,2,128]{2,1,0:T(2,128)}), f32[128,2,128]{2,1,0:T(2,128)S(1)}, u32[]{:S(2)}, u32[]{:S(2)}) async-start(f32[128,2,128]{2,1,0:T(2,128)} %get-tuple-element.22), calls=%async_computation | async-start | bytes 262144 | tf_op jit(solution)/shard_map/all_to_all | solution.py:385
  18.3 1.0 %copy-start.1 = (bf16[1,4,4,64,192]{4,3,2,1,0:T(8,128)(2,1)S(1)}, bf16[1,4,4,64,192]{4,3,2,1,0:T(8,128)(2,1)}, u32[]{:S(2)}) copy-start(bf16[1,4,4,64,192]{4,3,2,1,0:T(8,128)(2,1)} %param.11) | copy-start | bytes 1179652
  19.5 1.1 %copy-start.5 = (bf16[4,10,64,192]{3,2,1,0:T(8,128)(2,1)}, bf16[4,10,64,192]{3,2,1,0:T(8,128)(2,1)S(1)}, u32[]{:S(2)}) copy-start(bf16[4,10,64,192]{3,2,1,0:T(8,128)(2,1)S(1)} %get-tuple-element.20.own_ref) | copy-start | bytes 2949124
  20.6 7.9 %collective-permute-start.2 = (bf16[2,10,64,192]{3,2,1,0:T(8,128)(2,1)S(1)}, bf16[2,10,64,192]{3,2,1,0:T(8,128)(2,1)S(1)}, u32[]{:S(2)}, u32[]{:S(2)}) collective-permute-start(bf16[2,10,64,192]{3,2,1,0:T(8,128)(2,1)S(1)} %get-tuple-element.21), channel_id=1, source_target_pairs={{0,64},{1,65},{2,66},{3,67},{4,68},{5,69},{6,70},{7,71},{8,72},{9,... | collective-permute-start | bytes 1474568 | tf_op jit(solution)/shard_map/ppermute | solution.py:445
  21.9 0.7 %copy-start.10 = (f32[192]{0:T(256)S(1)}, f32[192]{0:T(256)}, u32[]{:S(2)}) copy-start(f32[192]{0:T(256)} %param.13) | copy-start | bytes 2308
  22.6 0.7 %copy-start.11 = (f32[192]{0:T(256)S(1)}, f32[192]{0:T(256)}, u32[]{:S(2)}) copy-start(f32[192]{0:T(256)} %param.15) | copy-start | bytes 2308
  23.2 0.7 %copy-start.12 = (f32[192]{0:T(256)S(1)}, f32[192]{0:T(256)}, u32[]{:S(2)}) copy-start(f32[192]{0:T(256)} %param.17) | copy-start | bytes 2308
  23.9 0.7 %copy-start.13 = (f32[192]{0:T(256)S(1)}, f32[192]{0:T(256)}, u32[]{:S(2)}) copy-start(f32[192]{0:T(256)} %param.19) | copy-start | bytes 2308
  24.6 0.7 copy-start.16
  25.2 2.9 %copy-start.14 = (f32[192]{0:T(256)S(1)}, f32[192]{0:T(256)}, u32[]{:S(2)}) copy-start(f32[192]{0:T(256)} %param.12) | copy-start | bytes 2308
  28.2 1.8 %copy-start.2 = (bf16[3,3,3,192,192]{4,3,2,1,0:T(8,128)(2,1)S(1)}, bf16[3,3,3,192,192]{4,3,2,1,0:T(8,128)(2,1)}, u32[]{:S(2)}) copy-start(bf16[3,3,3,192,192]{4,3,2,1,0:T(8,128)(2,1)} %param.14) | copy-start | bytes 5971972
  28.2 2.1 %copy-start.6 = (bf16[4,10,64,192]{3,2,1,0:T(8,128)(2,1)S(1)}, bf16[4,10,64,192]{3,2,1,0:T(8,128)(2,1)}, u32[]{:S(2)}) copy-start(bf16[4,10,64,192]{3,2,1,0:T(8,128)(2,1)} %copy-done.5) | copy-start | bytes 2949124
  30.3 16.4 %copy-start.3 = (bf16[3,3,3,192,192]{4,3,2,1,0:T(8,128)(2,1)S(1)}, bf16[3,3,3,192,192]{4,3,2,1,0:T(8,128)(2,1)}, u32[]{:S(2)}) copy-start(bf16[3,3,3,192,192]{4,3,2,1,0:T(8,128)(2,1)} %param.14) | copy-start | bytes 5971972
  35.0 21.6 %all-to-all-start.1 = ((f32[128,2,128]{2,1,0:T(2,128)}), f32[128,2,128]{2,1,0:T(2,128)S(1)}, u32[]{:S(2)}, u32[]{:S(2)}) async-start(f32[128,2,128]{2,1,0:T(2,128)} %get-tuple-element.28.after_hbm), calls=%async_computation.1 | async-start | bytes 262144 | tf_op jit(solution)/shard_map/all_to_all | solution.py:385
  46.7 1.3 %copy-start.7 = (bf16[4,10,64,192]{3,2,1,0:T(8,128)(2,1)S(1)}, bf16[4,10,64,192]{3,2,1,0:T(8,128)(2,1)}, u32[]{:S(2)}) copy-start(bf16[4,10,64,192]{3,2,1,0:T(8,128)(2,1)} %copy-done.5) | copy-start | bytes 2949124
  48.0 1.0 %copy-start.17 = (bf16[4,4,64,192]{3,2,1,0:T(8,128)(2,1)S(1)}, bf16[4,4,64,192]{3,2,1,0:T(8,128)(2,1)}, u32[]{:S(2)}) copy-start(bf16[4,4,64,192]{3,2,1,0:T(8,128)(2,1)} %get-tuple-element.25.rest_0_.h_ref) | copy-start | bytes 1179652
  49.1 6.3 %copy-start.9 = (bf16[3,3,192,96]{3,2,1,0:T(8,128)(2,1)S(1)}, bf16[3,3,192,96]{3,2,1,0:T(8,128)(2,1)}, u32[]{:S(2)}) copy-start(bf16[3,3,192,96]{3,2,1,0:T(8,128)(2,1)} %param.20) | copy-start | bytes 995332
  53.9 4.0 %collective-permute-start.3 = (bf16[2,8,64,192]{3,2,1,0:T(8,128)(2,1)}, bf16[2,8,64,192]{3,2,1,0:T(8,128)(2,1)S(1)}, u32[]{:S(2)}, u32[]{:S(2)}) collective-permute-start(bf16[2,8,64,192]{3,2,1,0:T(8,128)(2,1)} %get-tuple-element.27), channel_id=1, source_target_pairs={{0,64},{1,65},{2,66},{3,67},{4,68},{5,69},{6,70},{7,71},{8,72},{9,... | collective-permute-start | bytes 1179656 | tf_op jit(solution)/shard_map/ppermute | solution.py:501
  55.4 1.3 %copy-start.15 = (f32[192]{0:T(256)S(1)}, f32[192]{0:T(256)}, u32[]{:S(2)}) copy-start(f32[192]{0:T(256)} %param.16) | copy-start | bytes 2308
  56.6 1.8 %copy-start.4 = (bf16[3,3,3,192,192]{4,3,2,1,0:T(8,128)(2,1)S(1)}, bf16[3,3,3,192,192]{4,3,2,1,0:T(8,128)(2,1)}, u32[]{:S(2)}) copy-start(bf16[3,3,3,192,192]{4,3,2,1,0:T(8,128)(2,1)} %param.18) | copy-start | bytes 5971972
  56.6 2.1 %copy-start.8 = (bf16[4,10,64,192]{3,2,1,0:T(8,128)(2,1)S(1)}, bf16[4,10,64,192]{3,2,1,0:T(8,128)(2,1)}, u32[]{:S(2)}) copy-start(bf16[4,10,64,192]{3,2,1,0:T(8,128)(2,1)} %copy-done.5) | copy-start | bytes 2949124
  56.6 2.2 %copy-start.18 = (bf16[4,4,64,192]{3,2,1,0:T(8,128)(2,1)S(1)}, bf16[4,4,64,192]{3,2,1,0:T(8,128)(2,1)}, u32[]{:S(2)}) copy-start(bf16[4,4,64,192]{3,2,1,0:T(8,128)(2,1)} %get-tuple-element.25.rest_0_.h_ref) | copy-start | bytes 1179652
  56.7 2.4 %copy-start.19 = (bf16[4,4,64,192]{3,2,1,0:T(8,128)(2,1)S(1)}, bf16[4,4,64,192]{3,2,1,0:T(8,128)(2,1)}, u32[]{:S(2)}) copy-start(bf16[4,4,64,192]{3,2,1,0:T(8,128)(2,1)} %get-tuple-element.26.hh_ref) | copy-start | bytes 1179652

commit v5 on v4

--- a/solution.py
+++ b/solution.py
@@ -201,8 +201,12 @@
 
 
 def conv_one_kernel(
-    ring, row_list, own_ref, c_ref, w_ref, vec_ref, mean_ref, scale_ref, *rest
+    ring, row_list, own_ref, c_hbm, w_ref, vec_ref, mean_ref, scale_ref, *rest
 ):
+    c_ref, c_sem = rest[-2:]
+    rest = rest[:-2]
+    load_c = pltpu.make_async_copy(c_hbm, c_ref, c_sem)
+    load_c.start()
     if ring:
         out_hbm, stat_ref, a_ref, b_ref, d_ref, out_ref, out_sems = rest
     else:
@@ -243,6 +247,8 @@
                 put_both(put_row(v, a_ref, b_ref, slot, k), d_ref, slot, k)
                 k += 1
 
+    norm_frame(2)
+    load_c.wait()
     norm_frame(0)
     norm_frame(1)
     stats, written, runs, k = [], [], [], 0
@@ -250,7 +256,8 @@
         runs.append((k, n))
         k += n + 2
     for f in range(frames):
-        norm_frame(f + 2)
+        if f > 0:
+            norm_frame(f + 2)
         here = [(f, first, n) for first, n in runs]
         out = (conv_rows(a_ref, b_ref, d_ref, w_ref, here, cols) + bias).astype(BF16)
         rows_out = out.reshape(rows, cols, chan)
@@ -483,11 +490,12 @@
             pltpu.VMEM((frames, rows, cols, chan), BF16),
             pltpu.SemaphoreType.DMA((frames,)),
         ] + [pltpu.SemaphoreType.DMA] * len(more)
+        extra += [pltpu.VMEM(before.shape, BF16), pltpu.SemaphoreType.DMA]
         outs += (stat_shape,) if ring else (shape((2, rows + 4, cols, chan), BF16),)
         return pl.pallas_call(
             functools.partial(conv_one_kernel, ring, row_list),
             out_shape=outs,
-            in_specs=[VM] * (len(args) + 3) + [HB] * len(more),
+            in_specs=[VM, HB] + [VM] * 4 + [HB] * len(more),
             out_specs=(HB, VM),
             scratch_shapes=scratch(sum(n + 2 for _, n, _ in row_list)) + extra,
             compiler_params=limit,

time: 67 us -> 67.4 us (level)
  no operation moved by 1% of the time
where the time goes in v5:
time: 67.4 us; the launch traced here: 66.9 us
  starting transfers between devices  30.2 us (45%)
  Pallas kernels  20 us (30%)
  local copies, waits for them, and re-layouts  11.5 us (17%)
  waiting for transfers between devices  4.79 us (7%)
    all_to_all x2, starting transfers between devices, exchange(): return lax.all_to_all(stat, ('tm', 'tile'), 0, 0)  24.8 us
    unnamed x40, local copies, waits for them, and re-layouts  11.5 us
    pallas_call x2, Pallas kernels, conv_one(): pl.pallas_call(functools.partial(conv_one_kernel, ring, row_list), out_sh...  10.1 us
    pallas_call x1, Pallas kernels, body(): pl.pallas_call(conv_two_kernel, out_shape=out_shape, in_specs=[VM] * (len...  7.36 us
    all_to_all x2, waiting for transfers between devices, exchange(): return lax.all_to_all(stat, ('tm', 'tile'), 0, 0)  3.65 us
    ppermute x1, starting transfers between devices, body(): p1 = lax.ppermute(even, 'tile', even_pairs)  2.04 us
    ppermute x1, starting transfers between devices, body(): hidden_before = lax.ppermute(hidden_two, 'tm', down)  1.47 us
    pallas_call x1, Pallas kernels, body(): pl.pallas_call(pack_kernel, out_shape=(shape((frames, 3, cols, chan), BF1...  1.36 us
  transfers between devices with their start and end apart: 6, of which 3 were waited for; matrix products, arithmetic and copies ran while one was open for 0% of the time, Pallas kernels for 9%

profile of v5, /device:TPU:1, one launch (start us, length us, event | category | flops | bytes accessed | tf_op | source)
XLA Modules:
  0.0 66.9 jit_solution(8189608110889610516)
XLA Ops:
  0.0 1.0 %copy-done = bf16[1,4,4,64,192]{4,3,2,1,0:T(8,128)(2,1)S(1)} copy-done((bf16[1,4,4,64,192]{4,3,2,1,0:T(8,128)(2,1)S(1)}, bf16[1,4,4,64,192]{4,3,2,1,0:T(8,128)(2,1)}, u32[]{:S(2)}) %copy-start) | copy-done | bytes 393240
  1.0 1.4 %pack.1 = (bf16[4,3,64,192]{3,2,1,0:T(8,128)(2,1)S(1)}, bf16[4,3,64,192]{3,2,1,0:T(8,128)(2,1)S(1)}, f32[128,2,128]{2,1,0:T(2,128)}) custom-call(bf16[4,4,64,192]{3,2,1,0:T(8,128)(2,1)S(1)} %bitcast.12), custom_call_target="tpu_custom_call" | custom-call | tf_op jit(solution)/shard_map/pack/pallas_call | solution.py:424
  2.4 2.0 %collective-permute-start = (bf16[4,3,64,192]{3,2,1,0:T(8,128)(2,1)S(1)}, bf16[4,3,64,192]{3,2,1,0:T(8,128)(2,1)S(1)}, u32[]{:S(2)}, u32[]{:S(2)}) collective-permute-start(bf16[4,3,64,192]{3,2,1,0:T(8,128)(2,1)S(1)} %get-tuple-element.18), channel_id=1, source_target_pairs={{0,1},{1,0},{2,3},{3,2},{4,5},{5,4},{6,7},{7,6},{8,9},{9,8},{10,11... | collective-permute-start | bytes 884744 | tf_op jit(solution)/shard_map/ppermute | solution.py:436
  4.4 0.7 %collective-permute-start.1 = (bf16[4,3,64,192]{3,2,1,0:T(8,128)(2,1)S(1)}, bf16[4,3,64,192]{3,2,1,0:T(8,128)(2,1)S(1)}, u32[]{:S(2)}, u32[]{:S(2)}) collective-permute-start(bf16[4,3,64,192]{3,2,1,0:T(8,128)(2,1)S(1)} %get-tuple-element.19), channel_id=1, source_target_pairs={{1,2},{3,4},{5,6},{7,8},{9,10},{11,12},{13,14},{15,16},{17,18},{19... | collective-permute-start | bytes 884744 | tf_op jit(solution)/shard_map/ppermute | solution.py:437
  5.1 13.1 %all-to-all-start = ((f32[128,2,128]{2,1,0:T(2,128)}), f32[128,2,128]{2,1,0:T(2,128)S(1)}, u32[]{:S(2)}, u32[]{:S(2)}) async-start(f32[128,2,128]{2,1,0:T(2,128)} %get-tuple-element.22), calls=%async_computation | async-start | bytes 262144 | tf_op jit(solution)/shard_map/all_to_all | solution.py:392
  18.3 1.0 %copy-done.1 = bf16[1,4,4,64,192]{4,3,2,1,0:T(8,128)(2,1)S(1)} copy-done((bf16[1,4,4,64,192]{4,3,2,1,0:T(8,128)(2,1)S(1)}, bf16[1,4,4,64,192]{4,3,2,1,0:T(8,128)(2,1)}, u32[]{:S(2)}) %copy-start.1) | copy-done | bytes 393240
  19.3 0.2 assemble.1
  19.5 1.1 %copy-done.5 = bf16[4,10,64,192]{3,2,1,0:T(8,128)(2,1)} copy-done((bf16[4,10,64,192]{3,2,1,0:T(8,128)(2,1)}, bf16[4,10,64,192]{3,2,1,0:T(8,128)(2,1)S(1)}, u32[]{:S(2)}) %copy-start.5) | copy-done | bytes 983064
  20.6 1.3 %collective-permute-start.2 = (bf16[2,10,64,192]{3,2,1,0:T(8,128)(2,1)S(1)}, bf16[2,10,64,192]{3,2,1,0:T(8,128)(2,1)S(1)}, u32[]{:S(2)}, u32[]{:S(2)}) collective-permute-start(bf16[2,10,64,192]{3,2,1,0:T(8,128)(2,1)S(1)} %get-tuple-element.21), channel_id=1, source_target_pairs={{0,64},{1,65},{2,66},{3,67},{4,68},{5,69},{6,70},{7,71},{8,72},{9,... | collective-permute-start | bytes 1474568 | tf_op jit(solution)/shard_map/ppermute | solution.py:452
  21.9 0.7 %copy-done.10 = f32[192]{0:T(256)S(1)} copy-done((f32[192]{0:T(256)S(1)}, f32[192]{0:T(256)}, u32[]{:S(2)}) %copy-start.10) | copy-done | bytes 792
  22.6 0.7 %copy-done.11 = f32[192]{0:T(256)S(1)} copy-done((f32[192]{0:T(256)S(1)}, f32[192]{0:T(256)}, u32[]{:S(2)}) %copy-start.11) | copy-done | bytes 792
  23.2 0.7 %copy-done.12 = f32[192]{0:T(256)S(1)} copy-done((f32[192]{0:T(256)S(1)}, f32[192]{0:T(256)}, u32[]{:S(2)}) %copy-start.12) | copy-done | bytes 792
  23.9 0.7 %copy-done.13 = f32[192]{0:T(256)S(1)} copy-done((f32[192]{0:T(256)S(1)}, f32[192]{0:T(256)}, u32[]{:S(2)}) %copy-start.13) | copy-done | bytes 792
  24.6 0.7 copy-done.16
  25.3 2.8 %all-to-all-done.stat_ref = f32[128,2,128]{2,1,0:T(2,128)S(1)} async-done(((f32[128,2,128]{2,1,0:T(2,128)}), f32[128,2,128]{2,1,0:T(2,128)S(1)}, u32[]{:S(2)}, u32[]{:S(2)}) %all-to-all-start) | async-done | bytes 131104 | tf_op jit(solution)/shard_map/all_to_all | solution.py:392
  28.2 0.3 table.2
  28.5 1.4 %copy-done.2 = bf16[3,3,3,192,192]{4,3,2,1,0:T(8,128)(2,1)S(1)} copy-done((bf16[3,3,3,192,192]{4,3,2,1,0:T(8,128)(2,1)S(1)}, bf16[3,3,3,192,192]{4,3,2,1,0:T(8,128)(2,1)}, u32[]{:S(2)}) %copy-start.2) | copy-done | bytes 1990680
  29.9 0.4 copy-done.6
  30.3 5.1 %conv_one.1 = (bf16[4,4,64,192]{3,2,1,0:T(8,128)(2,1)}, f32[128,2,128]{2,1,0:T(2,128)}) custom-call(bf16[4,10,64,192]{3,2,1,0:T(8,128)(2,1)S(1)} %copy-done.6, bf16[2,10,64,192]{3,2,1,0:T(8,128)(2,1)S(1)} %collective-permute-done.2.c_hbm, bf16[27,192,192]{2,1,0:T(8,128)(2,1)S(1)} %bitcast.14, f32[5,192]{1,0:T(8,128)S(1)} %vectors.1.vec_ref, ...), custom_call_target="tpu_custom_call" | custom-call | flops 2038431744 | bytes 4194304 | tf_op jit(solution)/shard_map/conv_one/pallas_call | solution.py:495
  35.4 11.7 %all-to-all-start.1 = ((f32[128,2,128]{2,1,0:T(2,128)}), f32[128,2,128]{2,1,0:T(2,128)S(1)}, u32[]{:S(2)}, u32[]{:S(2)}) async-start(f32[128,2,128]{2,1,0:T(2,128)} %get-tuple-element.28.after_hbm), calls=%async_computation.1 | async-start | bytes 262144 | tf_op jit(solution)/shard_map/all_to_all | solution.py:392
  47.1 1.3 %copy-done.7 = bf16[4,10,64,192]{3,2,1,0:T(8,128)(2,1)S(1)} copy-done((bf16[4,10,64,192]{3,2,1,0:T(8,128)(2,1)S(1)}, bf16[4,10,64,192]{3,2,1,0:T(8,128)(2,1)}, u32[]{:S(2)}) %copy-start.7) | copy-done | bytes 983064
  48.4 1.0 %copy-done.17 = bf16[4,4,64,192]{3,2,1,0:T(8,128)(2,1)S(1)} copy-done((bf16[4,4,64,192]{3,2,1,0:T(8,128)(2,1)S(1)}, bf16[4,4,64,192]{3,2,1,0:T(8,128)(2,1)}, u32[]{:S(2)}) %copy-start.17) | copy-done | bytes 393240
  49.4 5.0 %conv_one_rim.1 = (bf16[4,4,64,192]{3,2,1,0:T(8,128)(2,1)}, bf16[2,8,64,192]{3,2,1,0:T(8,128)(2,1)}) custom-call(bf16[4,10,64,192]{3,2,1,0:T(8,128)(2,1)S(1)} %copy-done.7, bf16[2,10,64,192]{3,2,1,0:T(8,128)(2,1)S(1)} %collective-permute-done.2.c_hbm, bf16[27,192,192]{2,1,0:T(8,128)(2,1)S(1)} %bitcast.15, f32[5,192]{1,0:T(8,128)S(1)} %vectors.1.vec_ref, ...), custom_call_target="tpu_custom_call" | custom-call | flops 4000000000 | bytes 4194304 | tf_op jit(solution)/shard_map/conv_one_rim/pallas_call | solution.py:495
  54.4 1.5 %collective-permute-start.3 = (bf16[2,8,64,192]{3,2,1,0:T(8,128)(2,1)}, bf16[2,8,64,192]{3,2,1,0:T(8,128)(2,1)S(1)}, u32[]{:S(2)}, u32[]{:S(2)}) collective-permute-start(bf16[2,8,64,192]{3,2,1,0:T(8,128)(2,1)} %get-tuple-element.27), channel_id=1, source_target_pairs={{0,64},{1,65},{2,66},{3,67},{4,68},{5,69},{6,70},{7,71},{8,72},{9,... | collective-permute-start | bytes 1179656 | tf_op jit(solution)/shard_map/ppermute | solution.py:509
  56.0 0.2 fold.1.wu_ref
  56.2 0.8 %all-to-all-done.1.stat_ref = f32[128,2,128]{2,1,0:T(2,128)S(1)} async-done(((f32[128,2,128]{2,1,0:T(2,128)}), f32[128,2,128]{2,1,0:T(2,128)S(1)}, u32[]{:S(2)}, u32[]{:S(2)}) %all-to-all-start.1) | async-done | bytes 131104 | tf_op jit(solution)/shard_map/all_to_all | solution.py:392
  57.0 0.3 table.3
  57.3 1.1 %collective-permute-done.3.hc_ref = bf16[2,8,64,192]{3,2,1,0:T(8,128)(2,1)S(1)} collective-permute-done((bf16[2,8,64,192]{3,2,1,0:T(8,128)(2,1)}, bf16[2,8,64,192]{3,2,1,0:T(8,128)(2,1)S(1)}, u32[]{:S(2)}, u32[]{:S(2)}) %collective-permute-start.3) | collective-permute-done | bytes 393248 | tf_op jit(solution)/shard_map/ppermute | solution.py:509
  58.5 0.3 copy-done.4
  58.7 0.4 copy-done.8
  59.2 0.2 copy-done.19
  59.4 7.4 %conv_two.1 = bf16[4,8,64,192]{3,2,1,0:T(8,128)(2,1)} custom-call(bf16[4,10,64,192]{3,2,1,0:T(8,128)(2,1)S(1)} %copy-done.8, bf16[4,4,64,192]{3,2,1,0:T(8,128)(2,1)S(1)} %copy-done.18, bf16[4,4,64,192]{3,2,1,0:T(8,128)(2,1)S(1)} %copy-done.19, bf16[2,8,64,192]{3,2,1,0:T(8,128)(2,1)S(1)} %collective-permute-done.3.hc_ref, bf16[27,192,192]{2,1,0:T(8,128)(2,1)S(1)} %bitcast.16, ...), custom_call_target="tpu_custom_call" | custom-call | flops 6115295232 | bytes 4194304 | tf_op jit(solution)/shard_map/conv_two/pallas_call | solution.py:521
  (29 shorter events, 0.3 us)
Async XLA Ops:
  0.0 1.0 %copy-start = (bf16[1,4,4,64,192]{4,3,2,1,0:T(8,128)(2,1)S(1)}, bf16[1,4,4,64,192]{4,3,2,1,0:T(8,128)(2,1)}, u32[]{:S(2)}) copy-start(bf16[1,4,4,64,192]{4,3,2,1,0:T(8,128)(2,1)} %param.11) | copy-start | bytes 1179652
  2.4 15.8 %collective-permute-start = (bf16[4,3,64,192]{3,2,1,0:T(8,128)(2,1)S(1)}, bf16[4,3,64,192]{3,2,1,0:T(8,128)(2,1)S(1)}, u32[]{:S(2)}, u32[]{:S(2)}) collective-permute-start(bf16[4,3,64,192]{3,2,1,0:T(8,128)(2,1)S(1)} %get-tuple-element.18), channel_id=1, source_target_pairs={{0,1},{1,0},{2,3},{3,2},{4,5},{5,4},{6,7},{7,6},{8,9},{9,8},{10,11... | collective-permute-start | bytes 884744 | tf_op jit(solution)/shard_map/ppermute | solution.py:436
  4.4 13.8 %collective-permute-start.1 = (bf16[4,3,64,192]{3,2,1,0:T(8,128)(2,1)S(1)}, bf16[4,3,64,192]{3,2,1,0:T(8,128)(2,1)S(1)}, u32[]{:S(2)}, u32[]{:S(2)}) collective-permute-start(bf16[4,3,64,192]{3,2,1,0:T(8,128)(2,1)S(1)} %get-tuple-element.19), channel_id=1, source_target_pairs={{1,2},{3,4},{5,6},{7,8},{9,10},{11,12},{13,14},{15,16},{17,18},{19... | collective-permute-start | bytes 884744 | tf_op jit(solution)/shard_map/ppermute | solution.py:437
  5.1 23.0 %all-to-all-start = ((f32[128,2,128]{2,1,0:T(2,128)}), f32[128,2,128]{2,1,0:T(2,128)S(1)}, u32[]{:S(2)}, u32[]{:S(2)}) async-start(f32[128,2,128]{2,1,0:T(2,128)} %get-tuple-element.22), calls=%async_computation | async-start | bytes 262144 | tf_op jit(solution)/shard_map/all_to_all | solution.py:392
  18.3 1.0 %copy-start.1 = (bf16[1,4,4,64,192]{4,3,2,1,0:T(8,128)(2,1)S(1)}, bf16[1,4,4,64,192]{4,3,2,1,0:T(8,128)(2,1)}, u32[]{:S(2)}) copy-start(bf16[1,4,4,64,192]{4,3,2,1,0:T(8,128)(2,1)} %param.11) | copy-start | bytes 1179652
  19.5 1.1 %copy-start.5 = (bf16[4,10,64,192]{3,2,1,0:T(8,128)(2,1)}, bf16[4,10,64,192]{3,2,1,0:T(8,128)(2,1)S(1)}, u32[]{:S(2)}) copy-start(bf16[4,10,64,192]{3,2,1,0:T(8,128)(2,1)S(1)} %get-tuple-element.20.own_ref) | copy-start | bytes 2949124
  20.6 7.9 %collective-permute-start.2 = (bf16[2,10,64,192]{3,2,1,0:T(8,128)(2,1)S(1)}, bf16[2,10,64,192]{3,2,1,0:T(8,128)(2,1)S(1)}, u32[]{:S(2)}, u32[]{:S(2)}) collective-permute-start(bf16[2,10,64,192]{3,2,1,0:T(8,128)(2,1)S(1)} %get-tuple-element.21), channel_id=1, source_target_pairs={{0,64},{1,65},{2,66},{3,67},{4,68},{5,69},{6,70},{7,71},{8,72},{9,... | collective-permute-start | bytes 1474568 | tf_op jit(solution)/shard_map/ppermute | solution.py:452
  21.9 0.7 %copy-start.10 = (f32[192]{0:T(256)S(1)}, f32[192]{0:T(256)}, u32[]{:S(2)}) copy-start(f32[192]{0:T(256)} %param.13) | copy-start | bytes 2308
  22.6 0.7 %copy-start.11 = (f32[192]{0:T(256)S(1)}, f32[192]{0:T(256)}, u32[]{:S(2)}) copy-start(f32[192]{0:T(256)} %param.15) | copy-start | bytes 2308
  23.2 0.7 %copy-start.12 = (f32[192]{0:T(256)S(1)}, f32[192]{0:T(256)}, u32[]{:S(2)}) copy-start(f32[192]{0:T(256)} %param.17) | copy-start | bytes 2308
  23.9 0.7 %copy-start.13 = (f32[192]{0:T(256)S(1)}, f32[192]{0:T(256)}, u32[]{:S(2)}) copy-start(f32[192]{0:T(256)} %param.19) | copy-start | bytes 2308
  24.6 0.7 copy-start.16
  25.2 2.9 %copy-start.14 = (f32[192]{0:T(256)S(1)}, f32[192]{0:T(256)}, u32[]{:S(2)}) copy-start(f32[192]{0:T(256)} %param.12) | copy-start | bytes 2308
  28.2 1.8 %copy-start.2 = (bf16[3,3,3,192,192]{4,3,2,1,0:T(8,128)(2,1)S(1)}, bf16[3,3,3,192,192]{4,3,2,1,0:T(8,128)(2,1)}, u32[]{:S(2)}) copy-start(bf16[3,3,3,192,192]{4,3,2,1,0:T(8,128)(2,1)} %param.14) | copy-start | bytes 5971972
  28.2 2.1 %copy-start.6 = (bf16[4,10,64,192]{3,2,1,0:T(8,128)(2,1)S(1)}, bf16[4,10,64,192]{3,2,1,0:T(8,128)(2,1)}, u32[]{:S(2)}) copy-start(bf16[4,10,64,192]{3,2,1,0:T(8,128)(2,1)} %copy-done.5) | copy-start | bytes 2949124
  30.3 16.7 %copy-start.3 = (bf16[3,3,3,192,192]{4,3,2,1,0:T(8,128)(2,1)S(1)}, bf16[3,3,3,192,192]{4,3,2,1,0:T(8,128)(2,1)}, u32[]{:S(2)}) copy-start(bf16[3,3,3,192,192]{4,3,2,1,0:T(8,128)(2,1)} %param.14) | copy-start | bytes 5971972
  35.4 21.6 %all-to-all-start.1 = ((f32[128,2,128]{2,1,0:T(2,128)}), f32[128,2,128]{2,1,0:T(2,128)S(1)}, u32[]{:S(2)}, u32[]{:S(2)}) async-start(f32[128,2,128]{2,1,0:T(2,128)} %get-tuple-element.28.after_hbm), calls=%async_computation.1 | async-start | bytes 262144 | tf_op jit(solution)/shard_map/all_to_all | solution.py:392
  47.0 1.3 %copy-start.7 = (bf16[4,10,64,192]{3,2,1,0:T(8,128)(2,1)S(1)}, bf16[4,10,64,192]{3,2,1,0:T(8,128)(2,1)}, u32[]{:S(2)}) copy-start(bf16[4,10,64,192]{3,2,1,0:T(8,128)(2,1)} %copy-done.5) | copy-start | bytes 2949124
  48.4 1.0 %copy-start.17 = (bf16[4,4,64,192]{3,2,1,0:T(8,128)(2,1)S(1)}, bf16[4,4,64,192]{3,2,1,0:T(8,128)(2,1)}, u32[]{:S(2)}) copy-start(bf16[4,4,64,192]{3,2,1,0:T(8,128)(2,1)} %get-tuple-element.25.rest_0_.h_ref) | copy-start | bytes 1179652
  49.4 6.5 %copy-start.9 = (bf16[3,3,192,96]{3,2,1,0:T(8,128)(2,1)S(1)}, bf16[3,3,192,96]{3,2,1,0:T(8,128)(2,1)}, u32[]{:S(2)}) copy-start(bf16[3,3,192,96]{3,2,1,0:T(8,128)(2,1)} %param.20) | copy-start | bytes 995332
  54.4 4.0 %collective-permute-start.3 = (bf16[2,8,64,192]{3,2,1,0:T(8,128)(2,1)}, bf16[2,8,64,192]{3,2,1,0:T(8,128)(2,1)S(1)}, u32[]{:S(2)}, u32[]{:S(2)}) collective-permute-start(bf16[2,8,64,192]{3,2,1,0:T(8,128)(2,1)} %get-tuple-element.27), channel_id=1, source_target_pairs={{0,64},{1,65},{2,66},{3,67},{4,68},{5,69},{6,70},{7,71},{8,72},{9,... | collective-permute-start | bytes 1179656 | tf_op jit(solution)/shard_map/ppermute | solution.py:509
  55.9 1.0 %copy-start.15 = (f32[192]{0:T(256)S(1)}, f32[192]{0:T(256)}, u32[]{:S(2)}) copy-start(f32[192]{0:T(256)} %param.16) | copy-start | bytes 2308
  57.0 1.8 %copy-start.4 = (bf16[3,3,3,192,192]{4,3,2,1,0:T(8,128)(2,1)S(1)}, bf16[3,3,3,192,192]{4,3,2,1,0:T(8,128)(2,1)}, u32[]{:S(2)}) copy-start(bf16[3,3,3,192,192]{4,3,2,1,0:T(8,128)(2,1)} %param.18) | copy-start | bytes 5971972
  57.0 2.1 %copy-start.8 = (bf16[4,10,64,192]{3,2,1,0:T(8,128)(2,1)S(1)}, bf16[4,10,64,192]{3,2,1,0:T(8,128)(2,1)}, u32[]{:S(2)}) copy-start(bf16[4,10,64,192]{3,2,1,0:T(8,128)(2,1)} %copy-done.5) | copy-start | bytes 2949124
  57.0 2.2 %copy-start.18 = (bf16[4,4,64,192]{3,2,1,0:T(8,128)(2,1)S(1)}, bf16[4,4,64,192]{3,2,1,0:T(8,128)(2,1)}, u32[]{:S(2)}) copy-start(bf16[4,4,64,192]{3,2,1,0:T(8,128)(2,1)} %get-tuple-element.25.rest_0_.h_ref) | copy-start | bytes 1179652
  57.0 2.4 %copy-start.19 = (bf16[4,4,64,192]{3,2,1,0:T(8,128)(2,1)S(1)}, bf16[4,4,64,192]{3,2,1,0:T(8,128)(2,1)}, u32[]{:S(2)}) copy-start(bf16[4,4,64,192]{3,2,1,0:T(8,128)(2,1)} %get-tuple-element.26.hh_ref) | copy-start | bytes 1179652
